TPU v7x, 128 devices: a whole 4x4x4 slice. The times are simulated.
128 devices in a mesh: row: 16 (over x, y), col: 8 (over z, core).
Axes of the slice: x: 4, y: 4, z: 4, core: 2. Of those that a mesh axis runs over, the one named last changes fastest.
Arguments:
- object_field: float32 [2, 8192, 4096], P(None, 'row', 'col'), may hold values from -6 to 6
- probe: bfloat16 [2, 4, 256, 256], replicated, may hold values from -3 to 3
- patterns: float32 [1024, 256, 256], P(('row', 'col')), may hold values from 0.3 to 4
- offsets: int32 [2, 1024], P(None, ('row', 'col')), may hold values from 0 to 7936, as said below
- counts: int32 [16, 8], P('row', 'col'), may hold values from 1 to 8, as said below
Outputs:
- object_grad: float32 [2, 8192, 4096], P(None, 'row', 'col')
- probe_grad: float32 [2, 4, 256, 256], replicated
Inputs may be any that keep to these rules, and one draw needn't show every extreme that they name: `offsets`: the patch of a slot held by the device at (r, c) lies inside object rows r * 512 - 128 to (r + 1) * 512 + 128 and columns c * 512 - 128 to (c + 1) * 512 + 128, and inside the object. `counts`: some device has all 8 slots live.
All inputs are finite; a program needn't handle non-finite values.
Results may differ from a plain program's by a relative error of at most 0.005.
Values sent between devices are 32-bit elements; how exact they have to be, the bound alone decides.
No kernel may reach another device: no remote copies, remote signals or barrier semaphores. Data moves between devices by JAX's collectives and lax.ppermute only.
A program may use at most 128 MiB of HBM per device.

v0:
```python
import math

import jax
import jax.numpy as jnp
from jax import lax
from jax.sharding import PartitionSpec as P


def shifted(block, axis, distance):
    devices = range(lax.axis_size(axis))
    route = [(i - distance, i) for i in devices if i - distance in devices]
    return lax.ppermute(block, axis, route)


def extended_2(block, sides, width):
    for axis, dim in sides:
        count = lax.axis_size(axis)
        forward = [(i, i + 1) for i in range(count - 1)]
        backward = [(target, source) for source, target in forward]
        low = lax.ppermute(
            lax.slice_in_dim(block, block.shape[dim] - width, None, axis=dim), axis, forward
        )
        high = lax.ppermute(lax.slice_in_dim(block, 0, width, axis=dim), axis, backward)
        block = jnp.concatenate([low, block, high], axis=dim)
    return block


def tables(length):
    index = jnp.arange(length, dtype=jnp.int32)
    product = index[:, None] * index[None, :] % length
    angle = product.astype(jnp.float32) * (2.0 * math.pi / length)
    factor = 1.0 / math.sqrt(length)
    return (
        (jnp.cos(angle) * factor).astype(jnp.bfloat16),
        (-jnp.sin(angle) * factor).astype(jnp.bfloat16),
    )


def right_dot(matrix, table):
    return jnp.einsum("kab,bc->kac", matrix, table, preferred_element_type=jnp.float32)


def left_dot(table, matrix):
    return jnp.einsum("ab,kbc->kac", table, matrix, preferred_element_type=jnp.float32)


def right_mult(real_part, imag_part, table_re, table_im):
    return (
        right_dot(real_part, table_re) - right_dot(imag_part, table_im),
        right_dot(real_part, table_im) + right_dot(imag_part, table_re),
    )


def left_mult(table_re, table_im, real_part, imag_part):
    return (
        left_dot(table_re, real_part) - left_dot(table_im, imag_part),
        left_dot(table_re, imag_part) + left_dot(table_im, real_part),
    )


def position(patch_re, patch_im, measured, probe_re, probe_im, table_re, table_im):
    probe_fr = probe_re.astype(jnp.float32)
    probe_fi = probe_im.astype(jnp.float32)
    exit_re = (probe_fr * patch_re - probe_fi * patch_im).astype(jnp.bfloat16)
    exit_im = (probe_fr * patch_im + probe_fi * patch_re).astype(jnp.bfloat16)
    half_re, half_im = right_mult(exit_re, exit_im, table_re, table_im)
    field_re, field_im = left_mult(
        table_re, table_im, half_re.astype(jnp.bfloat16), half_im.astype(jnp.bfloat16)
    )
    intensity = jnp.sum(field_re * field_re + field_im * field_im, axis=0)
    amplitude = jnp.sqrt(jnp.maximum(intensity, 1.0))
    ratio = 1.0 - measured / amplitude
    resid_re = (field_re * ratio).astype(jnp.bfloat16)
    resid_im = (field_im * ratio).astype(jnp.bfloat16)
    conj_im = -table_im
    back_re, back_im = right_mult(resid_re, resid_im, table_re, conj_im)
    wave_re, wave_im = left_mult(
        table_re, conj_im, back_re.astype(jnp.bfloat16), back_im.astype(jnp.bfloat16)
    )
    object_re = jnp.sum(probe_fr * wave_re + probe_fi * wave_im, axis=0)
    object_im = jnp.sum(probe_fr * wave_im - probe_fi * wave_re, axis=0)
    update_re = patch_re * wave_re + patch_im * wave_im
    update_im = patch_re * wave_im - patch_im * wave_re
    return (jnp.stack([object_re, object_im]), jnp.stack([update_re, update_im]))


def send_cols(strip, amount):
    return shifted(strip, "col", amount)


def send_rows(strip, amount):
    return shifted(strip, "row", amount)


def on_device(object_field, probe, patterns, offsets, counts):
    tile_rows = object_field.shape[1]
    tile_cols = object_field.shape[2]
    slots = patterns.shape[0]
    width = patterns.shape[1]
    margin = width // 2
    modes = probe.shape[1]
    zero_index = jnp.int32(0)
    extended = extended_2(object_field, (("row", 1), ("col", 2)), margin)
    base_row = lax.axis_index("row") * tile_rows - margin
    base_col = lax.axis_index("col") * tile_cols - margin
    local_rows = offsets[0] - base_row
    local_cols = offsets[1] - base_col
    alive = jnp.arange(slots, dtype=jnp.int32) < counts[0, 0]
    table_re, table_im = tables(width)
    probe_re = probe[0]
    probe_im = probe[1]

    def cut_patch(start_row, start_col):
        return lax.dynamic_slice(extended, (zero_index, start_row, start_col), (2, width, width))

    def add_patch(totals, term, start_row, start_col):
        previous = lax.dynamic_slice(totals, (zero_index, start_row, start_col), (2, width, width))
        return lax.dynamic_update_slice(totals, previous + term, (zero_index, start_row, start_col))

    empty_ext = jnp.zeros(extended.shape, jnp.float32)
    empty_probe = jnp.zeros((2, modes, width, width), jnp.float32)

    def visit(number, carried):

        def work(inner):
            totals, probe_total = inner
            patch = cut_patch(local_rows[number], local_cols[number])
            object_term, probe_term = position(
                patch[0], patch[1], patterns[number], probe_re, probe_im, table_re, table_im
            )
            totals = add_patch(totals, object_term, local_rows[number], local_cols[number])
            return (totals, probe_total + probe_term)

        return lax.cond(alive[number], work, lambda inner: inner, carried)

    totals, probe_total = lax.fori_loop(0, slots, visit, (empty_ext, empty_probe))
    from_left = send_cols(totals[:, :, tile_cols + margin :], 1)
    from_right = send_cols(totals[:, :, :margin], -1)
    totals = totals.at[:, :, margin : 2 * margin].add(from_left)
    totals = totals.at[:, :, tile_cols : tile_cols + margin].add(from_right)
    from_above = send_rows(totals[:, tile_rows + margin :, margin : margin + tile_cols], 1)
    from_below = send_rows(totals[:, :margin, margin : margin + tile_cols], -1)
    totals = totals.at[:, margin : 2 * margin, margin : margin + tile_cols].add(from_above)
    totals = totals.at[:, tile_rows : tile_rows + margin, margin : margin + tile_cols].add(
        from_below
    )
    object_grad = totals[:, margin : margin + tile_rows, margin : margin + tile_cols]
    probe_grad = lax.psum(probe_total, ("row", "col"))
    return (object_grad, probe_grad)


def solution(mesh):
    in_specs = (
        P(None, "row", "col"),
        P(),
        P(("row", "col"), None, None),
        P(None, ("row", "col")),
        P("row", "col"),
    )
    out_specs = (P(None, "row", "col"), P())
    return jax.shard_map(
        on_device, mesh=mesh, in_specs=in_specs, out_specs=out_specs, check_vma=False
    )
```

profile of v0, /device:TPU:1, one launch (start us, length us, event | category | flops | bytes accessed | tf_op | source)
XLA Modules:
  0.0 449.2 jit_solution(17679808130954502893)
XLA Ops:
  7.2 1.9 copy.47
  9.2 4.1 collective-permute-start
  14.6 9.2 %collective-permute-done = f32[2,128,512]{1,2,0:T(8,128)S(1)} collective-permute-done((f32[2,128,512]{1,2,0:T(8,128)S(1)}, f32[2,128,512]{1,2,0:T(8,128)S(1)}, u32[]{:S(2)}, u32[]{:S(2)}) %collective-permute-start) | collective-permute-done | bytes 524320 | tf_op jit(solution)/shard_map/ppermute | solution.py:20
  23.8 3.8 collective-permute-done.1
  29.0 5.4 %collective-permute-start.2 = (f32[2,768,128]{1,2,0:T(8,128)}, f32[2,768,128]{1,2,0:T(8,128)}, u32[]{:S(2)}, u32[]{:S(2)}) collective-permute-start(f32[2,768,128]{1,2,0:T(8,128)} %get-tuple-element.491), channel_id=1, source_target_pairs={{0,1},{1,2},{2,3},{3,4},{4,5},{5,6},{6,7},{8,9},{9,10},{10,11},{11... | collective-permute-start | bytes 2359304 | tf_op jit(solution)/shard_map/ppermute | solution.py:20
  34.4 1.9 collective-permute-start.3
  36.4 2.3 fusion.67
  41.1 2.9 copy.51
  44.7 3.3 collective-permute-done.3
  48.0 3.6 pad_maximum_fusion
  51.6 2.5 broadcast_in_dim.4
  54.3 133.0 %while.21 = (s32[]{:T(128)}, f32[2,768,768]{1,2,0:T(8,128)}, f32[2,4,256,256]{2,3,1,0:T(8,128)S(1)}, pred[8]{0:T(512)(128)(4,1)S(1)}, s32[8]{0:T(128)S(1)}, /*in...) while((s32[]{:T(128)}, f32[2,768,768]{1,2,0:T(8,128)}, ...), condition=%wide.region_6.7_spmd.clone.clone, body=%wide.region_0.6_spmd.clone.clone.sunk | while | flops 2167078912 | bytes 57410060 | solution.py:136
  56.7 23.3 %conditional.4 = ((f32[2,768,768]{1,2,0:T(8,128)}, f32[2,4,256,256]{2,3,1,0:T(8,128)S(1)})) conditional(s32[]{:T(128)} %bitcast.99, (f32[2,768,768]{1,2,0:T(8,128)}, f32[2,4,256,256]{2,3,1,0:T(8,128)S(1)}) %tuple.84, (s32[]{:T(128)}, s32[8]{0:T(128)S(1)}, s32[8]{0:T(128)S(1)}, f32[2,768,768]{1,2,0:T(8,128)}, bf16[4,256,256]{1,2,0:T(8,128)(2,1)S(1)}, ...), branch_computations={%region_1.1_spmd, %region_2.5_spmd} | conditional | flops 2165833728 | bytes 57147580 | solution.py:134
  61.8 1.3 dynamic-slice_bitcast_fusion.1
  71.4 2.2 maximum_add_fusion.1
  73.6 6.4 %dynamic_update_slice.2 = f32[2,768,768]{1,2,0:T(8,128)} dynamic-update-slice(f32[2,768,768]{1,2,0:T(8,128)} %get-tuple-element.305, f32[2,256,256]{1,2,0:T(8,128)} %maximum_add_fusion.1, s32[]{:T(128)} %constant.165.clone, s32[]{:T(128)S(6)} %select_n.41, s32[]{:T(128)S(6)} %select_n.42) | dynamic-update-slice | bytes 1048580 | tf_op jit(solution)/shard_map/while/body/eval_jaxpr/cond/branch_1_fun/dynamic_update_slice | solution.py:118
  82.3 22.8 %conditional.4 = ((f32[2,768,768]{1,2,0:T(8,128)}, f32[2,4,256,256]{2,3,1,0:T(8,128)S(1)})) conditional(s32[]{:T(128)} %bitcast.99, (f32[2,768,768]{1,2,0:T(8,128)}, f32[2,4,256,256]{2,3,1,0:T(8,128)S(1)}) %tuple.84, (s32[]{:T(128)}, s32[8]{0:T(128)S(1)}, s32[8]{0:T(128)S(1)}, f32[2,768,768]{1,2,0:T(8,128)}, bf16[4,256,256]{1,2,0:T(8,128)(2,1)S(1)}, ...), branch_computations={%region_1.1_spmd, %region_2.5_spmd} | conditional | flops 2165833728 | bytes 57147580 | solution.py:134
  87.4 1.3 dynamic-slice_bitcast_fusion.1
  97.0 2.2 maximum_add_fusion.1
  99.2 5.9 %dynamic_update_slice.2 = f32[2,768,768]{1,2,0:T(8,128)} dynamic-update-slice(f32[2,768,768]{1,2,0:T(8,128)} %get-tuple-element.305, f32[2,256,256]{1,2,0:T(8,128)} %maximum_add_fusion.1, s32[]{:T(128)} %constant.165.clone, s32[]{:T(128)S(6)} %select_n.41, s32[]{:T(128)S(6)} %select_n.42) | dynamic-update-slice | bytes 1048580 | tf_op jit(solution)/shard_map/while/body/eval_jaxpr/cond/branch_1_fun/dynamic_update_slice | solution.py:118
  107.4 22.1 %conditional.4 = ((f32[2,768,768]{1,2,0:T(8,128)}, f32[2,4,256,256]{2,3,1,0:T(8,128)S(1)})) conditional(s32[]{:T(128)} %bitcast.99, (f32[2,768,768]{1,2,0:T(8,128)}, f32[2,4,256,256]{2,3,1,0:T(8,128)S(1)}) %tuple.84, (s32[]{:T(128)}, s32[8]{0:T(128)S(1)}, s32[8]{0:T(128)S(1)}, f32[2,768,768]{1,2,0:T(8,128)}, bf16[4,256,256]{1,2,0:T(8,128)(2,1)S(1)}, ...), branch_computations={%region_1.1_spmd, %region_2.5_spmd} | conditional | flops 2165833728 | bytes 57147580 | solution.py:134
  122.1 2.1 maximum_add_fusion.1
  124.1 5.4 %dynamic_update_slice.2 = f32[2,768,768]{1,2,0:T(8,128)} dynamic-update-slice(f32[2,768,768]{1,2,0:T(8,128)} %get-tuple-element.305, f32[2,256,256]{1,2,0:T(8,128)} %maximum_add_fusion.1, s32[]{:T(128)} %constant.165.clone, s32[]{:T(128)S(6)} %select_n.41, s32[]{:T(128)S(6)} %select_n.42) | dynamic-update-slice | bytes 1048580 | tf_op jit(solution)/shard_map/while/body/eval_jaxpr/cond/branch_1_fun/dynamic_update_slice | solution.py:118
  131.9 23.6 %conditional.4 = ((f32[2,768,768]{1,2,0:T(8,128)}, f32[2,4,256,256]{2,3,1,0:T(8,128)S(1)})) conditional(s32[]{:T(128)} %bitcast.99, (f32[2,768,768]{1,2,0:T(8,128)}, f32[2,4,256,256]{2,3,1,0:T(8,128)S(1)}) %tuple.84, (s32[]{:T(128)}, s32[8]{0:T(128)S(1)}, s32[8]{0:T(128)S(1)}, f32[2,768,768]{1,2,0:T(8,128)}, bf16[4,256,256]{1,2,0:T(8,128)(2,1)S(1)}, ...), branch_computations={%region_1.1_spmd, %region_2.5_spmd} | conditional | flops 2165833728 | bytes 57147580 | solution.py:134
  137.0 1.3 dynamic-slice_bitcast_fusion.1
  146.6 2.2 maximum_add_fusion.1
  148.8 6.7 %dynamic_update_slice.2 = f32[2,768,768]{1,2,0:T(8,128)} dynamic-update-slice(f32[2,768,768]{1,2,0:T(8,128)} %get-tuple-element.305, f32[2,256,256]{1,2,0:T(8,128)} %maximum_add_fusion.1, s32[]{:T(128)} %constant.165.clone, s32[]{:T(128)S(6)} %select_n.41, s32[]{:T(128)S(6)} %select_n.42) | dynamic-update-slice | bytes 1048580 | tf_op jit(solution)/shard_map/while/body/eval_jaxpr/cond/branch_1_fun/dynamic_update_slice | solution.py:118
  157.8 22.3 %conditional.4 = ((f32[2,768,768]{1,2,0:T(8,128)}, f32[2,4,256,256]{2,3,1,0:T(8,128)S(1)})) conditional(s32[]{:T(128)} %bitcast.99, (f32[2,768,768]{1,2,0:T(8,128)}, f32[2,4,256,256]{2,3,1,0:T(8,128)S(1)}) %tuple.84, (s32[]{:T(128)}, s32[8]{0:T(128)S(1)}, s32[8]{0:T(128)S(1)}, f32[2,768,768]{1,2,0:T(8,128)}, bf16[4,256,256]{1,2,0:T(8,128)(2,1)S(1)}, ...), branch_computations={%region_1.1_spmd, %region_2.5_spmd} | conditional | flops 2165833728 | bytes 57147580 | solution.py:134
  162.9 1.3 dynamic-slice_bitcast_fusion.1
  172.6 2.2 maximum_add_fusion.1
  174.7 5.4 %dynamic_update_slice.2 = f32[2,768,768]{1,2,0:T(8,128)} dynamic-update-slice(f32[2,768,768]{1,2,0:T(8,128)} %get-tuple-element.305, f32[2,256,256]{1,2,0:T(8,128)} %maximum_add_fusion.1, s32[]{:T(128)} %constant.165.clone, s32[]{:T(128)S(6)} %select_n.41, s32[]{:T(128)S(6)} %select_n.42) | dynamic-update-slice | bytes 1048580 | tf_op jit(solution)/shard_map/while/body/eval_jaxpr/cond/branch_1_fun/dynamic_update_slice | solution.py:118
  187.3 6.1 %copy.54 = f32[2,768,768]{2,1,0:T(8,128)} copy(f32[2,768,768]{1,2,0:T(8,128)} %get-tuple-element.363) | data formatting | bytes 9437184 | tf_op jit(solution)/shard_map/while | solution.py:136
  193.4 1.5 fusion.65
  194.9 1.9 collective-permute-start.4
  196.8 2.5 collective-permute-start.5
  199.3 6.5 %collective-permute-done.4 = f32[2,768,128]{2,1,0:T(8,128)S(1)} collective-permute-done((f32[2,768,128]{2,1,0:T(8,128)S(1)}, f32[2,768,128]{2,1,0:T(8,128)S(1)}, u32[]{:S(2)}, u32[]{:S(2)}) %collective-permute-start.4) | collective-permute-done | bytes 786464 | tf_op jit(solution)/shard_map/ppermute | solution.py:12
  205.7 2.2 fusion.61
  207.9 2.2 collective-permute-done.5
  210.1 2.2 fusion.60
  213.4 13.0 %collective-permute-start.6 = (f32[2,128,512]{2,1,0:T(8,128)S(1)}, f32[2,128,512]{2,1,0:T(8,128)S(1)}, u32[]{:S(2)}, u32[]{:S(2)}) collective-permute-start(f32[2,128,512]{2,1,0:T(8,128)S(1)} %slice.175), channel_id=1, source_target_pairs={{0,8},{8,16},{16,24},{24,32},{32,40},{40,48},{48,56},{56,64},{64,7... | collective-permute-start | bytes 1572872 | tf_op jit(solution)/shard_map/ppermute | solution.py:12
  226.4 1.8 copy.56
  228.2 9.4 %collective-permute-done.6 = f32[2,128,512]{2,1,0:T(8,128)S(1)} collective-permute-done((f32[2,128,512]{2,1,0:T(8,128)S(1)}, f32[2,128,512]{2,1,0:T(8,128)S(1)}, u32[]{:S(2)}, u32[]{:S(2)}) %collective-permute-start.6) | collective-permute-done | bytes 524320 | tf_op jit(solution)/shard_map/ppermute | solution.py:12
  237.6 2.2 fusion.64
  241.1 14.3 %collective-permute-done.7 = f32[2,128,512]{2,1,0:T(8,128)S(1)} collective-permute-done((f32[2,128,512]{2,1,0:T(8,128)S(1)}, f32[2,128,512]{2,1,0:T(8,128)S(1)}, u32[]{:S(2)}, u32[]{:S(2)}) %collective-permute-start.7) | collective-permute-done | bytes 524320 | tf_op jit(solution)/shard_map/ppermute | solution.py:12
  255.3 1.9 fusion.62
  257.3 3.1 slice.178
  260.4 178.9 %all-reduce.2.cloned.1.call-done = f32[2,4,256,256]{3,2,1,0:T(8,128)} async-done(((f32[2,4,256,256]{3,2,1,0:T(8,128)}), f32[2,4,256,256]{3,2,1,0:T(8,128)}) %all-reduce.2.cloned.1.call-update) | async-done | bytes 2097168 | tf_op jit(solution)/shard_map/psum | solution.py:148
  439.3 3.0 copy.97
  (139 shorter events, 69.5 us)
Async XLA Ops:
  7.2 432.1 %all-reduce.2.cloned.1.call-start = ((), (), s32[]{:S(2)}) async-start(), calls=%async_computation | async-start | bytes 4194304 | tf_op jit(solution)/shard_map/psum | solution.py:148
  9.2 14.6 %collective-permute-start = (f32[2,128,512]{1,2,0:T(8,128)S(1)}, f32[2,128,512]{1,2,0:T(8,128)S(1)}, u32[]{:S(2)}, u32[]{:S(2)}) collective-permute-start(f32[2,128,512]{1,2,0:T(8,128)S(1)} %get-tuple-element.493), channel_id=1, source_target_pairs={{0,8},{8,16},{16,24},{24,32},{32,40},{40,48},{48,56},{56,64},{64,7... | collective-permute-start | bytes 1572872 | tf_op jit(solution)/shard_map/ppermute | solution.py:20
  13.3 14.4 %collective-permute-start.1 = (f32[2,128,512]{1,2,0:T(8,128)S(1)}, f32[2,128,512]{1,2,0:T(8,128)S(1)}, u32[]{:S(2)}, u32[]{:S(2)}) collective-permute-start(f32[2,128,512]{1,2,0:T(8,128)S(1)} %get-tuple-element.494), channel_id=1, source_target_pairs={{8,0},{16,8},{24,16},{32,24},{40,32},{48,40},{56,48},{64,56},{72,6... | collective-permute-start | bytes 1572872 | tf_op jit(solution)/shard_map/ppermute | solution.py:23
  23.8 14.8 %copy-start = (f32[2,128,512]{1,2,0:T(8,128)}, f32[2,128,512]{1,2,0:T(8,128)S(1)}, u32[]{:S(2)}) copy-start(f32[2,128,512]{1,2,0:T(8,128)S(1)} %collective-permute-done) | copy-start | bytes 1572868
  27.7 12.2 %copy-start.1 = (f32[2,128,512]{1,2,0:T(8,128)}, f32[2,128,512]{1,2,0:T(8,128)S(1)}, u32[]{:S(2)}) copy-start(f32[2,128,512]{1,2,0:T(8,128)S(1)} %collective-permute-done.1) | copy-start | bytes 1572868
  29.0 15.7 %copy-start.2 = (s32[2,8]{1,0:T(2,128)S(1)}, s32[2,8]{1,0:T(2,128)}, u32[]{:S(2)}) copy-start(s32[2,8]{1,0:T(2,128)} %param.20) | copy-start | bytes 196
  29.0 15.7 %collective-permute-start.2 = (f32[2,768,128]{1,2,0:T(8,128)}, f32[2,768,128]{1,2,0:T(8,128)}, u32[]{:S(2)}, u32[]{:S(2)}) collective-permute-start(f32[2,768,128]{1,2,0:T(8,128)} %get-tuple-element.491), channel_id=1, source_target_pairs={{0,1},{1,2},{2,3},{3,4},{4,5},{5,6},{6,7},{8,9},{9,10},{10,11},{11... | collective-permute-start | bytes 2359304 | tf_op jit(solution)/shard_map/ppermute | solution.py:20
  34.4 13.6 %collective-permute-start.3 = (f32[2,768,128]{1,2,0:T(8,128)}, f32[2,768,128]{1,2,0:T(8,128)}, u32[]{:S(2)}, u32[]{:S(2)}) collective-permute-start(f32[2,768,128]{1,2,0:T(8,128)} %get-tuple-element.492), channel_id=1, source_target_pairs={{1,0},{2,1},{3,2},{4,3},{5,4},{6,5},{7,6},{9,8},{10,9},{11,10},{12... | collective-permute-start | bytes 2359304 | tf_op jit(solution)/shard_map/ppermute | solution.py:23
  194.9 10.8 %collective-permute-start.4 = (f32[2,768,128]{2,1,0:T(8,128)S(1)}, f32[2,768,128]{2,1,0:T(8,128)S(1)}, u32[]{:S(2)}, u32[]{:S(2)}) collective-permute-start(f32[2,768,128]{2,1,0:T(8,128)S(1)} %get-tuple-element.490), channel_id=1, source_target_pairs={{0,1},{1,2},{2,3},{3,4},{4,5},{5,6},{6,7},{8,9},{9,10},{10,11},{11... | collective-permute-start | bytes 2359304 | tf_op jit(solution)/shard_map/ppermute | solution.py:12
  196.8 13.3 %collective-permute-start.5 = (f32[2,768,128]{2,1,0:T(8,128)S(1)}, f32[2,768,128]{2,1,0:T(8,128)S(1)}, u32[]{:S(2)}, u32[]{:S(2)}) collective-permute-start(f32[2,768,128]{2,1,0:T(8,128)S(1)} %get-tuple-element.489), channel_id=1, source_target_pairs={{1,0},{2,1},{3,2},{4,3},{5,4},{6,5},{7,6},{9,8},{10,9},{11,10},{12... | collective-permute-start | bytes 2359304 | tf_op jit(solution)/shard_map/ppermute | solution.py:12
  213.4 24.2 %collective-permute-start.6 = (f32[2,128,512]{2,1,0:T(8,128)S(1)}, f32[2,128,512]{2,1,0:T(8,128)S(1)}, u32[]{:S(2)}, u32[]{:S(2)}) collective-permute-start(f32[2,128,512]{2,1,0:T(8,128)S(1)} %slice.175), channel_id=1, source_target_pairs={{0,8},{8,16},{16,24},{24,32},{32,40},{40,48},{48,56},{56,64},{64,7... | collective-permute-start | bytes 1572872 | tf_op jit(solution)/shard_map/ppermute | solution.py:12
  239.8 15.5 %collective-permute-start.7 = (f32[2,128,512]{2,1,0:T(8,128)S(1)}, f32[2,128,512]{2,1,0:T(8,128)S(1)}, u32[]{:S(2)}, u32[]{:S(2)}) collective-permute-start(f32[2,128,512]{2,1,0:T(8,128)S(1)} %get-tuple-element.487), channel_id=1, source_target_pairs={{8,0},{16,8},{24,16},{32,24},{40,32},{48,40},{56,48},{64,56},{72,6... | collective-permute-start | bytes 1572872 | tf_op jit(solution)/shard_map/ppermute | solution.py:12
Sparse Core Ops, SparseCore 0:
  228.3 210.9 all-reduce.1
where the time goes:
time: 453 us; the launch traced here: 449 us
  waiting for transfers between devices  228 us (50%)
  local copies, waits for them, and re-layouts  75.7 us (17%)
  other arithmetic  40.8 us (9%)
  matrix products  33.2 us (7%)
  starting transfers between devices  31.4 us (7%)
  loops' own time  25.6 us (6%)
  between operations  14.8 us (3%)
    psum x1, waiting for transfers between devices, on_device(): probe_grad = lax.psum(probe_total, ('row', 'col'))  179 us
    ppermute x4, waiting for transfers between devices, shifted(): return lax.ppermute(block, axis, route)  32.3 us
    dynamic_update_slice x5, local copies, waits for them, and re-layouts, add_patch(): lax.dynamic_update_slice(totals, previous + term, (zero_index, start_row,...  29.7 us
    another operation x8, loops' own time, visit(): return lax.cond(alive[number], work, lambda inner: inner, carried)  20.2 us
    ppermute x4, starting transfers between devices, shifted(): return lax.ppermute(block, axis, route)  18.6 us
    dot_general x40, matrix products, left_dot(): jnp.einsum('ab,kbc->kac', table, matrix, preferred_element_type=jnp.float32)  16.6 us
    dot_general x40, matrix products, right_dot(): jnp.einsum('kab,bc->kac', matrix, table, preferred_element_type=jnp.float32)  16.5 us
    add x5, other arithmetic, add_patch(): previous + term  10.8 us
  transfers between devices with their start and end apart: 9, of which 8 were waited for; matrix products, arithmetic and copies ran while one was open for 4% of the time, Pallas kernels for 0%

commit v1 on v0

v1 whole, which is shorter than its diff:
```python
import math

import jax
import jax.numpy as jnp
import numpy as np
from jax import lax
from jax.experimental import pallas as pl
from jax.experimental.pallas import tpu as pltpu
from jax.sharding import Mesh, PartitionSpec as P

LANES = 128
CHUNK = 32


def tables(length):
    index = np.arange(length)
    angle = (index[:, None] * index[None, :] % length) * (2.0 * math.pi / length)
    factor = 1.0 / math.sqrt(length)
    table_re = (np.cos(angle) * factor).astype(jnp.bfloat16)
    table_im = (-np.sin(angle) * factor).astype(jnp.bfloat16)
    forward = np.block([[table_re, table_im], [-table_im, table_re]])
    backward = np.block([[table_re, -table_im], [table_im, table_re]])
    return (forward.astype(jnp.bfloat16), backward.astype(jnp.bfloat16))


def slots_kernel(
    meta, tile, above, below, left, right, corner_left, corner_right, patterns, probe_hbm,
    forward_hbm, backward_hbm,
    center_out, top_out, bottom_out, left_out, right_out, keep_out, send_out,
    ext, totals, pat, probe, forward, backward, probe_total, obj, psi, half, field, wave, sems,
):
    slots, width = pat.shape[0], pat.shape[1]
    modes = probe.shape[1]
    tile_rows = tile.shape[1]
    blocks = tile.shape[2] // LANES
    last = blocks + 1
    margin = above.shape[1]
    low_end = margin + tile_rows
    moves = []

    def begin(source, target):
        move = pltpu.make_async_copy(source, target, sems.at[len(moves)])
        move.start()
        moves.append(move)

    for j in range(blocks):
        span = pl.ds(j * LANES, LANES)
        begin(tile.at[:, :, span], ext.at[:, 1 + j, pl.ds(margin, tile_rows), :])
        begin(above.at[:, :, span], ext.at[:, 1 + j, pl.ds(0, margin), :])
        begin(below.at[:, :, span], ext.at[:, 1 + j, pl.ds(low_end, margin), :])
    for side, corner, j in ((left, corner_left, 0), (right, corner_right, last)):
        begin(side, ext.at[:, j, pl.ds(margin, tile_rows), :])
        begin(corner.at[:, pl.ds(0, margin), :], ext.at[:, j, pl.ds(0, margin), :])
        begin(corner.at[:, pl.ds(margin, margin), :], ext.at[:, j, pl.ds(low_end, margin), :])
    begin(probe_hbm, probe)
    begin(forward_hbm, forward)
    begin(backward_hbm, backward)
    begin(patterns, pat)
    totals[...] = jnp.zeros_like(totals)
    probe_total[...] = jnp.zeros_like(probe_total)
    for move in moves:
        move.wait()

    lane = lax.broadcasted_iota(jnp.int32, (CHUNK, LANES), 1)

    def visit(number, carry):
        row = meta[number]
        col = meta[slots + number]
        block = jnp.minimum(col // LANES, blocks - 1)
        rest = col - block * LANES
        back_shift = lax.rem(LANES - rest, LANES)
        shift = lax.rem(rest, LANES)
        from_first = lane < LANES - rest
        at_or_after = lane >= rest

        for c in range(width // CHUNK):
            rows = pl.ds(c * CHUNK, CHUNK)
            source = pl.ds(row + c * CHUNK, CHUNK)
            patch = []
            for p in range(2):
                parts = [
                    pltpu.roll(ext[p, block + j, source, :], back_shift, 1) for j in range(3)
                ]
                whole = jnp.concatenate(
                    [
                        jnp.where(from_first, parts[0], parts[1]),
                        jnp.where(from_first, parts[1], parts[2]),
                    ],
                    axis=1,
                )
                obj[p, rows, :] = whole
                patch.append(whole)
            for k in range(modes):
                probe_re = probe[0, k, rows, :].astype(jnp.float32)
                probe_im = probe[1, k, rows, :].astype(jnp.float32)
                exit_re = probe_re * patch[0] - probe_im * patch[1]
                exit_im = probe_re * patch[1] + probe_im * patch[0]
                psi[k, rows, pl.ds(0, width)] = exit_re.astype(jnp.bfloat16)
                psi[k, rows, pl.ds(width, width)] = exit_im.astype(jnp.bfloat16)

        for k in range(modes):
            product = jnp.dot(psi[k], forward[...], preferred_element_type=jnp.float32)
            half[k, pl.ds(0, width), :] = product[:, :width].astype(jnp.bfloat16)
            half[k, pl.ds(width, width), :] = product[:, width:].astype(jnp.bfloat16)
        for k in range(modes):
            field[k] = jnp.dot(backward[...], half[k], preferred_element_type=jnp.float32)

        for c in range(width // CHUNK):
            rows = pl.ds(c * CHUNK, CHUNK)
            rows_im = pl.ds(width + c * CHUNK, CHUNK)
            values = [(field[k, rows, :], field[k, rows_im, :]) for k in range(modes)]
            intensity = sum(re * re + im * im for re, im in values)
            ratio = 1.0 - pat[number, rows, :] * lax.rsqrt(jnp.maximum(intensity, 1.0))
            for k, (re, im) in enumerate(values):
                psi[k, rows, pl.ds(0, width)] = (re * ratio).astype(jnp.bfloat16)
                psi[k, rows, pl.ds(width, width)] = (im * ratio).astype(jnp.bfloat16)

        for k in range(modes):
            product = jnp.dot(psi[k], backward[...], preferred_element_type=jnp.float32)
            half[k, pl.ds(0, width), :] = product[:, :width].astype(jnp.bfloat16)
            half[k, pl.ds(width, width), :] = product[:, width:].astype(jnp.bfloat16)
        for k in range(modes):
            wave[k] = jnp.dot(forward[...], half[k], preferred_element_type=jnp.float32)

        for c in range(width // CHUNK):
            rows = pl.ds(c * CHUNK, CHUNK)
            rows_im = pl.ds(width + c * CHUNK, CHUNK)
            target = pl.ds(row + c * CHUNK, CHUNK)
            patch_re = obj[0, rows, :]
            patch_im = obj[1, rows, :]
            term = [jnp.zeros((CHUNK, width), jnp.float32)] * 2
            for k in range(modes):
                probe_re = probe[0, k, rows, :].astype(jnp.float32)
                probe_im = probe[1, k, rows, :].astype(jnp.float32)
                wave_re = wave[k, rows, :]
                wave_im = wave[k, rows_im, :]
                term[0] = term[0] + (probe_re * wave_re + probe_im * wave_im)
                term[1] = term[1] + (probe_re * wave_im - probe_im * wave_re)
                probe_total[0, k, rows, :] += patch_re * wave_re + patch_im * wave_im
                probe_total[1, k, rows, :] += patch_re * wave_im - patch_im * wave_re
            for p in range(2):
                first = pltpu.roll(term[p][:, :LANES], shift, 1)
                second = pltpu.roll(term[p][:, LANES:], shift, 1)
                totals[p, block, target, :] += jnp.where(at_or_after, first, 0.0)
                totals[p, block + 1, target, :] += jnp.where(at_or_after, second, first)
                totals[p, block + 2, target, :] += jnp.where(at_or_after, 0.0, second)
        return carry

    lax.fori_loop(0, meta[2 * slots], visit, 0)

    core = meta[2 * slots + 1]
    moves.clear()
    begin(probe_total.at[1 - core], send_out)
    begin(totals.at[:, 0], left_out)
    begin(totals.at[:, last], right_out)
    begin(probe_total.at[core], keep_out)
    for j in range(blocks):
        span = pl.ds(j * LANES, LANES)
        begin(totals.at[:, 1 + j, pl.ds(0, margin), :], top_out.at[:, :, span])
        begin(totals.at[:, 1 + j, pl.ds(low_end, margin), :], bottom_out.at[:, :, span])
        begin(totals.at[:, 1 + j, pl.ds(margin, tile_rows), :], center_out.at[:, :, span])
    for move in moves:
        move.wait()


def run_slots(meta, tile, sides, patterns, probe, forward, backward):
    slots, width = patterns.shape[0], patterns.shape[1]
    modes = probe.shape[1]
    rows, cols = tile.shape[1], tile.shape[2]
    margin = width // 2
    blocks = cols // LANES
    f32 = jnp.float32
    bf16 = jnp.bfloat16
    out_shapes = [
        (2, rows, cols),
        (2, margin, cols),
        (2, margin, cols),
        (2, rows + 2 * margin, margin),
        (2, rows + 2 * margin, margin),
        (modes, width, width),
        (modes, width, width),
    ]
    hbm = pl.BlockSpec(memory_space=pl.ANY)
    work = slots * modes * width * width * width * 4 * 4 * 2
    return pl.pallas_call(
        slots_kernel,
        out_shape=[jax.ShapeDtypeStruct(shape, f32) for shape in out_shapes],
        in_specs=[pl.BlockSpec(memory_space=pltpu.SMEM)] + [hbm] * 11,
        out_specs=[hbm] * 7,
        scratch_shapes=[
            pltpu.VMEM((2, blocks + 2, rows + 2 * margin, LANES), f32),
            pltpu.VMEM((2, blocks + 2, rows + 2 * margin, LANES), f32),
            pltpu.VMEM(patterns.shape, f32),
            pltpu.VMEM(probe.shape, bf16),
            pltpu.VMEM(forward.shape, bf16),
            pltpu.VMEM(backward.shape, bf16),
            pltpu.VMEM((2, modes, width, width), f32),
            pltpu.VMEM((2, width, width), f32),
            pltpu.VMEM((modes, width, 2 * width), bf16),
            pltpu.VMEM((modes, 2 * width, width), bf16),
            pltpu.VMEM((modes, 2 * width, width), f32),
            pltpu.VMEM((modes, 2 * width, width), f32),
            pltpu.SemaphoreType.DMA((32,)),
        ],
        compiler_params=pltpu.CompilerParams(vmem_limit_bytes=48 * 1024 * 1024),
        cost_estimate=pl.CostEstimate(
            flops=work, bytes_accessed=20_000_000, transcendentals=slots * width * width
        ),
        name="slots",
    )(meta, tile, *sides, patterns, probe, forward, backward)


def up(block, axes):
    count = lax.axis_size(axes)
    return lax.ppermute(block, axes, [(i, i + 1) for i in range(count - 1)])


def down(block, axes):
    count = lax.axis_size(axes)
    return lax.ppermute(block, axes, [(i + 1, i) for i in range(count - 1)])


def on_device(row_axes, col_axes, core_axis, object_field, probe, patterns, offsets, counts):
    tile_rows, tile_cols = object_field.shape[1:]
    width = patterns.shape[1]
    modes = probe.shape[1]
    margin = width // 2
    chip_axes = row_axes + tuple(name for name in col_axes if name != core_axis)

    from_above = up(object_field[:, tile_rows - margin :, :], row_axes)
    from_below = down(object_field[:, :margin, :], row_axes)
    from_left = up(object_field[:, :, tile_cols - margin :], col_axes)
    from_right = down(object_field[:, :, :margin], col_axes)
    ends = jnp.concatenate([from_above, from_below], axis=1)
    corner_left = up(ends[:, :, tile_cols - margin :], col_axes)
    corner_right = down(ends[:, :, :margin], col_axes)

    base_row = lax.axis_index(row_axes) * tile_rows - margin
    base_col = lax.axis_index(col_axes) * tile_cols - margin
    core = lax.axis_index(core_axis)
    meta = jnp.concatenate(
        [offsets[0] - base_row, offsets[1] - base_col, counts[0], core.reshape(1)]
    ).astype(jnp.int32)
    forward, backward = tables(width)
    sides = (from_above, from_below, from_left, from_right, corner_left, corner_right)
    center, top, bottom, left, right, keep, send = run_slots(
        meta, object_field, sides, patterns, probe, jnp.asarray(forward), jnp.asarray(backward)
    )

    mates = [(0, 1), (1, 0)]
    received = lax.ppermute(send, core_axis, mates)
    to_left = up(right, col_axes)
    to_right = down(left, col_axes)
    pair = keep + received
    chips = lax.axis_size(chip_axes)
    pieces = pair.reshape(chips, modes * width // chips, width)
    pieces = lax.all_to_all(pieces, chip_axes, 0, 0, tiled=True)

    def spread(band, start):
        band = band.at[:, :, :margin].add(to_left[:, start : start + margin])
        return band.at[:, :, tile_cols - margin :].add(to_right[:, start : start + margin])

    top = spread(top, 0)
    bottom = spread(bottom, margin + tile_rows)
    add_top = up(bottom, row_axes)
    add_bottom = down(top, row_axes)

    mine = jnp.sum(pieces, axis=0)
    gathered = lax.all_to_all(
        jnp.broadcast_to(mine, pieces.shape), chip_axes, 0, 0, tiled=True
    ).reshape(modes, width, width)
    other = lax.ppermute(gathered, core_axis, mates)
    probe_grad = jnp.where(
        core == 0, jnp.stack([gathered, other]), jnp.stack([other, gathered])
    )

    center = center.at[:, :, :margin].add(to_left[:, margin : margin + tile_rows])
    center = center.at[:, :, tile_cols - margin :].add(to_right[:, margin : margin + tile_rows])
    center = center.at[:, :margin, :].add(add_top)
    center = center.at[:, tile_rows - margin :, :].add(add_bottom)
    return (center, probe_grad)


def solution(mesh):
    rows, cols = mesh.devices.shape
    side = math.isqrt(rows)
    fine = Mesh(mesh.devices.reshape(side, side, cols // 2, 2), ("x", "y", "z", "core"))
    row_axes, col_axes = ("x", "y"), ("z", "core")
    every = row_axes + col_axes
    in_specs = (
        P(None, row_axes, col_axes),
        P(),
        P(every, None, None),
        P(None, every),
        P(row_axes, col_axes),
    )
    out_specs = (P(None, row_axes, col_axes), P())

    def body(*args):
        return on_device(row_axes, col_axes, "core", *args)

    return jax.shard_map(
        body, mesh=fine, in_specs=in_specs, out_specs=out_specs, check_vma=False
    )
```

time: 453 us -> 156 us (0.34)
  the two profiles are of different devices: /device:TPU:1 before, /device:TPU:67 now
where the time goes in v1:
time: 156 us; the launch traced here: 154 us
  starting transfers between devices  65.3 us (42%)
  waiting for transfers between devices  49.6 us (32%)
  Pallas kernels  16 us (10%)
  other arithmetic  14 us (9%)
  local copies, waits for them, and re-layouts  7.59 us (5%)
    all_to_all x1, starting transfers between devices, on_device(): pieces = lax.all_to_all(pieces, chip_axes, 0, 0, tiled=True)  23.1 us
    ppermute x5, waiting for transfers between devices, down(): return lax.ppermute(block, axes, [(i + 1, i) for i in range(count - 1)])  19.9 us
    ppermute x5, starting transfers between devices, down(): return lax.ppermute(block, axes, [(i + 1, i) for i in range(count - 1)])  19.2 us
    pallas_call x1, Pallas kernels, run_slots(): pl.pallas_call(slots_kernel, out_shape=[jax.ShapeDtypeStruct(shape, f32)...  16 us
    ppermute x5, waiting for transfers between devices, up(): return lax.ppermute(block, axes, [(i, i + 1) for i in range(count - 1)])  15 us
    ppermute x5, starting transfers between devices, up(): return lax.ppermute(block, axes, [(i, i + 1) for i in range(count - 1)])  14.8 us
    all_to_all x1, waiting for transfers between devices, on_device(): pieces = lax.all_to_all(pieces, chip_axes, 0, 0, tiled=True)  12.2 us
    all_to_all x1, starting transfers between devices, on_device(): lax.all_to_all(jnp.broadcast_to(mine, pieces.shape), chip_axes, 0, 0, til...  6.72 us
  transfers between devices with their start and end apart: 14, of which 8 were waited for; matrix products, arithmetic and copies ran while one was open for 7% of the time, Pallas kernels for 0%

profile of v1, /device:TPU:67, one launch (start us, length us, event | category | flops | bytes accessed | tf_op | source)
XLA Modules:
  0.0 154.0 jit_solution(12185446644515598019)
XLA Ops:
  0.6 0.0 copy-start.4
  0.6 2.4 %fusion.9 = (f32[2,128,512]{2,1,0:T(8,128)}, f32[2,128,512]{2,1,0:T(8,128)}) fusion(f32[2,512,512]{2,1,0:T(8,128)} %tile.1), kind=kLoop, calls=%fused_computation.23 | loop fusion | bytes 2097152 | tf_op jit(solution)/shard_map/slice | solution.py:231
  3.0 3.2 %collective-permute-start = (f32[2,128,512]{2,1,0:T(8,128)}, f32[2,128,512]{2,1,0:T(8,128)S(1)}, u32[]{:S(2)}, u32[]{:S(2)}) collective-permute-start(f32[2,128,512]{2,1,0:T(8,128)} %get-tuple-element.115), channel_id=1, source_target_pairs={{0,8},{8,16},{16,24},{24,32},{32,40},{40,48},{48,56},{56,64},{64,7... | collective-permute-start | bytes 1572872 | tf_op jit(solution)/shard_map/ppermute | solution.py:215
  6.2 4.2 %collective-permute-start.1 = (f32[2,128,512]{2,1,0:T(8,128)}, f32[2,128,512]{2,1,0:T(8,128)S(1)}, u32[]{:S(2)}, u32[]{:S(2)}) collective-permute-start(f32[2,128,512]{2,1,0:T(8,128)} %get-tuple-element.114), channel_id=1, source_target_pairs={{8,0},{16,8},{24,16},{32,24},{40,32},{48,40},{56,48},{64,56},{72,6... | collective-permute-start | bytes 1572872 | tf_op jit(solution)/shard_map/ppermute | solution.py:220
  10.4 0.1 fusion.8
  10.5 0.0 copy-start.5
  10.5 3.1 %collective-permute-start.3 = (f32[2,512,128]{2,1,0:T(8,128)S(1)}, f32[2,512,128]{2,1,0:T(8,128)S(1)}, u32[]{:S(2)}, u32[]{:S(2)}) collective-permute-start(f32[2,512,128]{2,1,0:T(8,128)S(1)} %get-tuple-element.112), channel_id=1, source_target_pairs={{1,0},{2,1},{3,2},{4,3},{5,4},{6,5},{7,6},{9,8},{10,9},{11,10},{12... | collective-permute-start | bytes 1572872 | tf_op jit(solution)/shard_map/ppermute | solution.py:220
  13.7 3.1 %collective-permute-start.2 = (f32[2,512,128]{2,1,0:T(8,128)S(1)}, f32[2,512,128]{2,1,0:T(8,128)S(1)}, u32[]{:S(2)}, u32[]{:S(2)}) collective-permute-start(f32[2,512,128]{2,1,0:T(8,128)S(1)} %get-tuple-element.113), channel_id=1, source_target_pairs={{0,1},{1,2},{2,3},{3,4},{4,5},{5,6},{6,7},{8,9},{9,10},{10,11},{11... | collective-permute-start | bytes 1572872 | tf_op jit(solution)/shard_map/ppermute | solution.py:215
  17.5 2.5 %collective-permute-done.above = f32[2,128,512]{2,1,0:T(8,128)S(1)} collective-permute-done((f32[2,128,512]{2,1,0:T(8,128)}, f32[2,128,512]{2,1,0:T(8,128)S(1)}, u32[]{:S(2)}, u32[]{:S(2)}) %collective-permute-start) | collective-permute-done | bytes 524320 | tf_op jit(solution)/shard_map/ppermute | solution.py:215
  20.1 0.9 collective-permute-done.1.below
  21.1 3.8 %collective-permute-start.5 = (f32[2,256,128]{2,1,0:T(8,128)S(1)}, f32[2,256,128]{2,1,0:T(8,128)S(1)}, u32[]{:S(2)}, u32[]{:S(2)}) collective-permute-start(f32[2,256,128]{2,1,0:T(8,128)S(1)} %get-tuple-element.116), channel_id=1, source_target_pairs={{1,0},{2,1},{3,2},{4,3},{5,4},{6,5},{7,6},{9,8},{10,9},{11,10},{12... | collective-permute-start | bytes 786440 | tf_op jit(solution)/shard_map/ppermute | solution.py:220
  24.9 3.1 %collective-permute-start.4 = (f32[2,256,128]{2,1,0:T(8,128)S(1)}, f32[2,256,128]{2,1,0:T(8,128)S(1)}, u32[]{:S(2)}, u32[]{:S(2)}) collective-permute-start(f32[2,256,128]{2,1,0:T(8,128)S(1)} %get-tuple-element.117), channel_id=1, source_target_pairs={{0,1},{1,2},{2,3},{3,4},{4,5},{5,6},{6,7},{8,9},{9,10},{10,11},{11... | collective-permute-start | bytes 786440 | tf_op jit(solution)/shard_map/ppermute | solution.py:215
  28.0 0.1 pad_add_fusion.meta
  28.1 0.0 collective-permute-done.3.right
  28.1 0.0 collective-permute-done.2.left
  28.1 0.8 copy-done
  28.9 1.5 collective-permute-done.5.corner_right
  30.4 0.9 collective-permute-done.4.corner_left
  31.3 1.0 copy-done.1
  32.4 1.0 copy-done.2
  33.4 1.0 copy-done.3
  34.4 16.0 %slots.1 = (f32[2,512,512]{2,1,0:T(8,128)}, f32[2,128,512]{2,1,0:T(8,128)S(1)}, f32[2,128,512]{2,1,0:T(8,128)S(1)}, f32[2,768,128]{2,1,0:T(8,128)S(1)}, f32[2,76...) custom-call(s32[18]{0:T(128)S(1)} %pad_add_fusion.meta, f32[2,512,512]{2,1,0:T(8,128)} %tile.1, ...), custom_call_target="tpu_custom_call" | custom-call | flops 17179869184 | bytes 20000000 | tf_op jit(solution)/shard_map/slots/pallas_call | solution.py:185
  50.4 1.3 collective-permute-start.10
  51.8 2.5 %collective-permute-done.10 = f32[4,256,256]{2,1,0:T(8,128)S(1)} collective-permute-done((f32[4,256,256]{2,1,0:T(8,128)}, f32[4,256,256]{2,1,0:T(8,128)S(1)}, u32[]{:S(2)}, u32[]{:S(2)}) %collective-permute-start.10) | collective-permute-done | bytes 1048608 | tf_op jit(solution)/shard_map/ppermute | solution.py:251
  54.3 2.3 %add.77 = f32[4,256,256]{2,1,0:T(8,128)} add(f32[4,256,256]{2,1,0:T(8,128)} %get-tuple-element.110, f32[4,256,256]{2,1,0:T(8,128)S(1)} %collective-permute-done.10) | non-fusion elementwise | flops 262144 | bytes 3145728 | tf_op jit(solution)/shard_map/add | solution.py:254
  56.6 23.1 %all-to-all-start = ((f32[64,16,256]{2,1,0:T(8,128)}), f32[64,16,256]{2,1,0:T(8,128)S(1)}, u32[]{:S(2)}, u32[]{:S(2)}) async-start(f32[64,16,256]{2,1,0:T(8,128)} %bitcast.4), calls=%async_computation | async-start | bytes 2097152 | tf_op jit(solution)/shard_map/all_to_all | solution.py:257
  79.7 3.4 %collective-permute-start.6 = (f32[2,768,128]{2,1,0:T(8,128)}, f32[2,768,128]{2,1,0:T(8,128)}, u32[]{:S(2)}, u32[]{:S(2)}) collective-permute-start(f32[2,768,128]{2,1,0:T(8,128)} %get-tuple-element.106), channel_id=1, source_target_pairs={{0,1},{1,2},{2,3},{3,4},{4,5},{5,6},{6,7},{8,9},{9,10},{10,11},{11... | collective-permute-start | bytes 2359304 | tf_op jit(solution)/shard_map/ppermute | solution.py:215
  83.1 12.2 %all-to-all-done = f32[64,16,256]{2,1,0:T(8,128)S(1)} async-done(((f32[64,16,256]{2,1,0:T(8,128)}), f32[64,16,256]{2,1,0:T(8,128)S(1)}, u32[]{:S(2)}, u32[]{:S(2)}) %all-to-all-start) | async-done | bytes 1048608 | tf_op jit(solution)/shard_map/all_to_all | solution.py:257
  95.3 0.1 reduce_sum.9
  95.4 1.1 broadcast_in_dim.3
  96.5 6.7 %all-to-all-start.1 = ((f32[64,16,256]{2,1,0:T(8,128)}), f32[64,16,256]{2,1,0:T(8,128)S(1)}, u32[]{:S(2)}, u32[]{:S(2)}) async-start(f32[64,16,256]{2,1,0:T(8,128)} %broadcast_in_dim.3), calls=%async_computation.1 | async-start | bytes 2097152 | tf_op jit(solution)/shard_map/all_to_all | solution.py:269
  103.2 4.1 %collective-permute-start.7 = (f32[2,768,128]{2,1,0:T(8,128)S(1)}, f32[2,768,128]{2,1,0:T(8,128)}, u32[]{:S(2)}, u32[]{:S(2)}) collective-permute-start(f32[2,768,128]{2,1,0:T(8,128)S(1)} %get-tuple-element.107), channel_id=1, source_target_pairs={{1,0},{2,1},{3,2},{4,3},{5,4},{6,5},{7,6},{9,8},{10,9},{11,10},{12... | collective-permute-start | bytes 2359304 | tf_op jit(solution)/shard_map/ppermute | solution.py:220
  107.4 0.0 collective-permute-done.6
  107.4 1.0 fusion.5
  108.4 17.5 %collective-permute-done.7 = f32[2,768,128]{2,1,0:T(8,128)} collective-permute-done((f32[2,768,128]{2,1,0:T(8,128)S(1)}, f32[2,768,128]{2,1,0:T(8,128)}, u32[]{:S(2)}, u32[]{:S(2)}) %collective-permute-start.7) | collective-permute-done | bytes 786464 | tf_op jit(solution)/shard_map/ppermute | solution.py:220
  125.9 1.0 fusion.4
  126.9 4.0 %collective-permute-start.9 = (f32[2,128,512]{2,1,0:T(8,128)S(1)}, f32[2,128,512]{2,1,0:T(8,128)S(1)}, u32[]{:S(2)}, u32[]{:S(2)}) collective-permute-start(f32[2,128,512]{2,1,0:T(8,128)S(1)} %get-tuple-element.118), channel_id=1, source_target_pairs={{8,0},{16,8},{24,16},{32,24},{40,32},{48,40},{56,48},{64,56},{72,6... | collective-permute-start | bytes 1572872 | tf_op jit(solution)/shard_map/ppermute | solution.py:220
  130.9 1.9 %collective-permute-start.8 = (f32[2,128,512]{2,1,0:T(8,128)S(1)}, f32[2,128,512]{2,1,0:T(8,128)S(1)}, u32[]{:S(2)}, u32[]{:S(2)}) collective-permute-start(f32[2,128,512]{2,1,0:T(8,128)S(1)} %get-tuple-element.119), channel_id=1, source_target_pairs={{0,8},{8,16},{16,24},{24,32},{32,40},{40,48},{48,56},{56,64},{64,7... | collective-permute-start | bytes 1572872 | tf_op jit(solution)/shard_map/ppermute | solution.py:215
  132.8 0.0 all-to-all-done.1
  132.8 0.1 collective-permute-start.11
  132.9 2.1 %fusion.3 = f32[2,512,512]{2,1,0:T(8,128)} fusion(f32[2,512,512]{2,1,0:T(8,128)} %get-tuple-element.105, f32[2,768,128]{2,1,0:T(8,128)} %collective-permute-done.6), kind=kLoop, calls=%fused_computation.8 | loop fusion | flops 131072 | bytes 1572864 | tf_op jit(solution)/shard_map/scatter-add | solution.py:277
  135.0 2.1 %fusion.2 = f32[2,512,512]{2,1,0:T(8,128)} fusion(f32[2,512,512]{2,1,0:T(8,128)} %fusion.3, f32[2,768,128]{2,1,0:T(8,128)} %collective-permute-done.7), kind=kLoop, calls=%fused_computation.6 | loop fusion | flops 131072 | bytes 1572864 | tf_op jit(solution)/shard_map/scatter-add | solution.py:278
  137.1 11.6 %collective-permute-done.8 = f32[2,128,512]{2,1,0:T(8,128)S(1)} collective-permute-done((f32[2,128,512]{2,1,0:T(8,128)S(1)}, f32[2,128,512]{2,1,0:T(8,128)S(1)}, u32[]{:S(2)}, u32[]{:S(2)}) %collective-permute-start.8) | collective-permute-done | bytes 524320 | tf_op jit(solution)/shard_map/ppermute | solution.py:215
  148.7 1.9 %fusion.1 = f32[2,512,512]{2,1,0:T(8,128)} fusion(f32[2,512,512]{2,1,0:T(8,128)} %fusion.2, f32[2,128,512]{2,1,0:T(8,128)S(1)} %collective-permute-done.8), kind=kLoop, calls=%fused_computation.4 | loop fusion | flops 131072 | bytes 1572864 | tf_op jit(solution)/shard_map/scatter-add | solution.py:279
  150.6 0.0 collective-permute-done.9
  150.6 1.9 %fusion = f32[2,512,512]{2,1,0:T(8,128)} fusion(f32[2,512,512]{2,1,0:T(8,128)} %fusion.1, f32[2,128,512]{2,1,0:T(8,128)S(1)} %collective-permute-done.9), kind=kLoop, calls=%fused_computation.2 | loop fusion | flops 131072 | bytes 1572864 | tf_op jit(solution)/shard_map/scatter-add | solution.py:280
  152.5 0.0 collective-permute-done.11
  152.5 1.5 maximum_select_fusion
  (10 shorter events, 0.1 us)
Async XLA Ops:
  0.6 9.8 %copy-start.4 = (f32[2,512,512]{2,1,0:T(8,128)S(1)}, f32[2,512,512]{2,1,0:T(8,128)}, u32[]{:S(2)}) copy-start(f32[2,512,512]{2,1,0:T(8,128)} %tile.1) | copy-start | bytes 6291460
  3.0 17.0 %collective-permute-start = (f32[2,128,512]{2,1,0:T(8,128)}, f32[2,128,512]{2,1,0:T(8,128)S(1)}, u32[]{:S(2)}, u32[]{:S(2)}) collective-permute-start(f32[2,128,512]{2,1,0:T(8,128)} %get-tuple-element.115), channel_id=1, source_target_pairs={{0,8},{8,16},{16,24},{24,32},{32,40},{40,48},{48,56},{56,64},{64,7... | collective-permute-start | bytes 1572872 | tf_op jit(solution)/shard_map/ppermute | solution.py:215
  6.2 14.8 %collective-permute-start.1 = (f32[2,128,512]{2,1,0:T(8,128)}, f32[2,128,512]{2,1,0:T(8,128)S(1)}, u32[]{:S(2)}, u32[]{:S(2)}) collective-permute-start(f32[2,128,512]{2,1,0:T(8,128)} %get-tuple-element.114), channel_id=1, source_target_pairs={{8,0},{16,8},{24,16},{32,24},{40,32},{48,40},{56,48},{64,56},{72,6... | collective-permute-start | bytes 1572872 | tf_op jit(solution)/shard_map/ppermute | solution.py:220
  10.5 17.5 %copy-start.5 = (s32[2,8]{1,0:T(2,128)S(1)}, s32[2,8]{1,0:T(2,128)}, u32[]{:S(2)}) copy-start(s32[2,8]{1,0:T(2,128)} %param.26) | copy-start | bytes 196
  10.5 17.6 %collective-permute-start.3 = (f32[2,512,128]{2,1,0:T(8,128)S(1)}, f32[2,512,128]{2,1,0:T(8,128)S(1)}, u32[]{:S(2)}, u32[]{:S(2)}) collective-permute-start(f32[2,512,128]{2,1,0:T(8,128)S(1)} %get-tuple-element.112), channel_id=1, source_target_pairs={{1,0},{2,1},{3,2},{4,3},{5,4},{6,5},{7,6},{9,8},{10,9},{11,10},{12... | collective-permute-start | bytes 1572872 | tf_op jit(solution)/shard_map/ppermute | solution.py:220
  13.7 14.4 %collective-permute-start.2 = (f32[2,512,128]{2,1,0:T(8,128)S(1)}, f32[2,512,128]{2,1,0:T(8,128)S(1)}, u32[]{:S(2)}, u32[]{:S(2)}) collective-permute-start(f32[2,512,128]{2,1,0:T(8,128)S(1)} %get-tuple-element.113), channel_id=1, source_target_pairs={{0,1},{1,2},{2,3},{3,4},{4,5},{5,6},{6,7},{8,9},{9,10},{10,11},{11... | collective-permute-start | bytes 1572872 | tf_op jit(solution)/shard_map/ppermute | solution.py:215
  21.1 9.3 %collective-permute-start.5 = (f32[2,256,128]{2,1,0:T(8,128)S(1)}, f32[2,256,128]{2,1,0:T(8,128)S(1)}, u32[]{:S(2)}, u32[]{:S(2)}) collective-permute-start(f32[2,256,128]{2,1,0:T(8,128)S(1)} %get-tuple-element.116), channel_id=1, source_target_pairs={{1,0},{2,1},{3,2},{4,3},{5,4},{6,5},{7,6},{9,8},{10,9},{11,10},{12... | collective-permute-start | bytes 786440 | tf_op jit(solution)/shard_map/ppermute | solution.py:220
  24.9 6.5 %collective-permute-start.4 = (f32[2,256,128]{2,1,0:T(8,128)S(1)}, f32[2,256,128]{2,1,0:T(8,128)S(1)}, u32[]{:S(2)}, u32[]{:S(2)}) collective-permute-start(f32[2,256,128]{2,1,0:T(8,128)S(1)} %get-tuple-element.117), channel_id=1, source_target_pairs={{0,1},{1,2},{2,3},{3,4},{4,5},{5,6},{6,7},{8,9},{9,10},{10,11},{11... | collective-permute-start | bytes 786440 | tf_op jit(solution)/shard_map/ppermute | solution.py:215
  28.1 0.8 copy-start
  31.3 1.0 copy-start.1
  32.3 1.0 copy-start.2
  33.4 1.0 copy-start.3
  50.4 3.8 %collective-permute-start.10 = (f32[4,256,256]{2,1,0:T(8,128)}, f32[4,256,256]{2,1,0:T(8,128)S(1)}, u32[]{:S(2)}, u32[]{:S(2)}) collective-permute-start(f32[4,256,256]{2,1,0:T(8,128)} %get-tuple-element.111), channel_id=1, source_target_pairs={{0,1},{1,0},{2,3},{3,2},{4,5},{5,4},{6,7},{7,6},{8,9},{9,8},{10,11... | collective-permute-start | bytes 3145736 | tf_op jit(solution)/shard_map/ppermute | solution.py:251
  56.6 38.7 %all-to-all-start = ((f32[64,16,256]{2,1,0:T(8,128)}), f32[64,16,256]{2,1,0:T(8,128)S(1)}, u32[]{:S(2)}, u32[]{:S(2)}) async-start(f32[64,16,256]{2,1,0:T(8,128)} %bitcast.4), calls=%async_computation | async-start | bytes 2097152 | tf_op jit(solution)/shard_map/all_to_all | solution.py:257
  79.7 27.7 %collective-permute-start.6 = (f32[2,768,128]{2,1,0:T(8,128)}, f32[2,768,128]{2,1,0:T(8,128)}, u32[]{:S(2)}, u32[]{:S(2)}) collective-permute-start(f32[2,768,128]{2,1,0:T(8,128)} %get-tuple-element.106), channel_id=1, source_target_pairs={{0,1},{1,2},{2,3},{3,4},{4,5},{5,6},{6,7},{8,9},{9,10},{10,11},{11... | collective-permute-start | bytes 2359304 | tf_op jit(solution)/shard_map/ppermute | solution.py:215
  96.5 36.3 %all-to-all-start.1 = ((f32[64,16,256]{2,1,0:T(8,128)}), f32[64,16,256]{2,1,0:T(8,128)S(1)}, u32[]{:S(2)}, u32[]{:S(2)}) async-start(f32[64,16,256]{2,1,0:T(8,128)} %broadcast_in_dim.3), calls=%async_computation.1 | async-start | bytes 2097152 | tf_op jit(solution)/shard_map/all_to_all | solution.py:269
  103.2 22.7 %collective-permute-start.7 = (f32[2,768,128]{2,1,0:T(8,128)S(1)}, f32[2,768,128]{2,1,0:T(8,128)}, u32[]{:S(2)}, u32[]{:S(2)}) collective-permute-start(f32[2,768,128]{2,1,0:T(8,128)S(1)} %get-tuple-element.107), channel_id=1, source_target_pairs={{1,0},{2,1},{3,2},{4,3},{5,4},{6,5},{7,6},{9,8},{10,9},{11,10},{12... | collective-permute-start | bytes 2359304 | tf_op jit(solution)/shard_map/ppermute | solution.py:220
  126.9 23.7 %collective-permute-start.9 = (f32[2,128,512]{2,1,0:T(8,128)S(1)}, f32[2,128,512]{2,1,0:T(8,128)S(1)}, u32[]{:S(2)}, u32[]{:S(2)}) collective-permute-start(f32[2,128,512]{2,1,0:T(8,128)S(1)} %get-tuple-element.118), channel_id=1, source_target_pairs={{8,0},{16,8},{24,16},{32,24},{40,32},{48,40},{56,48},{64,56},{72,6... | collective-permute-start | bytes 1572872 | tf_op jit(solution)/shard_map/ppermute | solution.py:220
  130.9 17.8 %collective-permute-start.8 = (f32[2,128,512]{2,1,0:T(8,128)S(1)}, f32[2,128,512]{2,1,0:T(8,128)S(1)}, u32[]{:S(2)}, u32[]{:S(2)}) collective-permute-start(f32[2,128,512]{2,1,0:T(8,128)S(1)} %get-tuple-element.119), channel_id=1, source_target_pairs={{0,8},{8,16},{16,24},{24,32},{32,40},{40,48},{48,56},{56,64},{64,7... | collective-permute-start | bytes 1572872 | tf_op jit(solution)/shard_map/ppermute | solution.py:215
  132.8 19.7 %collective-permute-start.11 = (f32[4,256,256]{2,1,0:T(8,128)S(1)}, f32[4,256,256]{2,1,0:T(8,128)S(1)}, u32[]{:S(2)}, u32[]{:S(2)}) collective-permute-start(f32[4,256,256]{2,1,0:T(8,128)S(1)} %bitcast.11), channel_id=1, source_target_pairs={{0,1},{1,0},{2,3},{3,2},{4,5},{5,4},{6,7},{7,6},{8,9},{9,8},{10,11... | collective-permute-start | bytes 3145736 | tf_op jit(solution)/shard_map/ppermute | solution.py:272

commit v2 on v0

v2 whole, which is shorter than its diff:
```python
import math

import jax
import jax.numpy as jnp
import numpy as np
from jax import lax
from jax.experimental import pallas as pl
from jax.experimental.pallas import tpu as pltpu
from jax.sharding import Mesh, PartitionSpec as P

LANES = 128
CHUNK = 32
F32 = jnp.float32
BF16 = jnp.bfloat16
RIGHT = (0, 2)
LEFT = (1, 3)
MIB = 1024 * 1024
FREE = pl.BlockSpec(memory_space=pl.ANY)
VMEM = pl.BlockSpec(memory_space=pltpu.VMEM)
ROW, COL, CORE = ("x", "y"), ("z", "core"), "core"
CHIP = ("x", "y", "z")
SMEM = pl.BlockSpec(memory_space=pltpu.SMEM)


def tables(length):
    index = np.arange(length // 2)
    parts = []
    for parity in range(2):
        product = index[:, None] * (2 * index[None, :] + parity) % length
        angle = product * (2.0 * math.pi / length)
        factor = 1.0 / math.sqrt(length)
        re = (np.cos(angle) * factor).astype(BF16)
        im = (-np.sin(angle) * factor).astype(BF16)
        right = np.block([[re, im], [-im, re]])
        parts += [right, right.T]
    return np.stack(parts).astype(BF16)


def dot(a, b):
    return jnp.dot(a, b, preferred_element_type=F32)


def one_slot(number, row, col, ext, pat, probe, table, totals, keep, send, work):
    obj, term, psi, half, field, ratio = work
    width = pat.shape[1]
    modes = probe.shape[1]
    mid = width // 2
    blocks = ext.shape[1] - 2
    core = lax.axis_index(CORE)
    block = jnp.minimum(col // LANES, blocks - 1)
    rest = col - block * LANES
    back_shift = lax.rem(LANES - rest, LANES)
    shift = lax.rem(rest, LANES)
    lane = lax.broadcasted_iota(jnp.int32, (CHUNK, LANES), 1)
    from_first = lane < LANES - rest
    at_or_after = lane >= rest
    turn = (core + jnp.zeros((CHUNK, LANES), jnp.int32)) == 0
    low, high = pl.ds(0, mid), pl.ds(mid, mid)

    def span(c, base=0):
        return pl.ds(base + c * CHUNK, CHUNK)

    def gather_patch():
        for c in range(width // CHUNK):
            source = pl.ds(row + c * CHUNK, CHUNK)
            patch = []
            for p in range(2):
                parts = [
                    pltpu.roll(ext[p, block + j, source, :], back_shift, 1) for j in range(3)
                ]
                patch.append(
                    [
                        jnp.where(from_first, parts[0], parts[1]),
                        jnp.where(from_first, parts[1], parts[2]),
                    ]
                )
            for side, lanes in enumerate((low, high)):
                re, im = patch[0][side], patch[1][side]
                obj[0, span(c), lanes] = re
                obj[1, span(c), lanes] = im

    def make_psi(k):
        for c in range(width // CHUNK):
            waves = []
            for lanes in (low, high):
                o_re, o_im = obj[0, span(c), lanes], obj[1, span(c), lanes]
                p_re = probe[0, k, span(c), lanes]
                p_im = probe[1, k, span(c), lanes]
                waves.append((p_re * o_re - p_im * o_im, p_re * o_im + p_im * o_re))
            for part, lanes in enumerate((low, high)):
                a, b = waves[0][part], waves[1][part]
                psi[k, 0, span(c), lanes] = (a + b).astype(BF16)
                psi[k, 1, span(c), lanes] = (a - b).astype(BF16)

    def right_forward(k):
        for parity, lanes in enumerate((low, high)):
            y = dot(psi[k, parity], table[RIGHT[parity]])
            top, bottom = y[:mid], y[mid:]
            total, difference = (top + bottom).astype(BF16), (top - bottom).astype(BF16)
            half[k, 0, low, lanes] = total[:, :mid]
            half[k, 0, high, lanes] = total[:, mid:]
            half[k, 1, low, lanes] = difference[:, :mid]
            half[k, 1, high, lanes] = difference[:, mid:]

    def left_forward(k):
        for parity in range(2):
            field[k, parity] = dot(table[LEFT[parity]], half[k, parity])

    def make_ratio():
        for parity in range(2):
            for c in range(mid // CHUNK):
                total = None
                for k in range(modes):
                    re, im = field[k, parity, span(c), :], field[k, parity, span(c, mid), :]
                    square = re * re + im * im
                    total = square if total is None else total + square
                measured = pat[number, span(c, parity * mid), :]
                ratio[parity, span(c), :] = 1.0 - measured * lax.rsqrt(jnp.maximum(total, 1.0))

    def make_chi(k):
        for parity in range(2):
            for c in range(mid // CHUNK):
                scale = ratio[parity, span(c), :]
                re = (field[k, parity, span(c), :] * scale).astype(BF16)
                im = (field[k, parity, span(c, mid), :] * scale).astype(BF16)
                rows = span(c, parity * mid)
                psi[k, 0, rows, low] = re[:, :mid]
                psi[k, 0, rows, high] = im[:, :mid]
                psi[k, 1, rows, low] = re[:, mid:]
                psi[k, 1, rows, high] = im[:, mid:]

    def right_backward(k):
        even = dot(psi[k, 0], table[LEFT[0]])
        odd = dot(psi[k, 1], table[LEFT[1]])
        for value, lanes in (((even + odd).astype(BF16), low), ((even - odd).astype(BF16), high)):
            for parity in range(2):
                rows = value[parity * mid : parity * mid + mid]
                half[k, parity, low, lanes] = rows[:, :mid]
                half[k, parity, high, lanes] = rows[:, mid:]

    def left_backward(k):
        for parity in range(2):
            field[k, parity] = dot(table[RIGHT[parity]], half[k, parity])

    def collect(k):
        for c in range(mid // CHUNK):
            even_re, odd_re = field[k, 0, span(c), :], field[k, 1, span(c), :]
            even_im, odd_im = field[k, 0, span(c, mid), :], field[k, 1, span(c, mid), :]
            for rows, re, im in (
                (span(c), even_re + odd_re, even_im + odd_im),
                (span(c, mid), even_re - odd_re, even_im - odd_im),
            ):
                p_re, p_im = probe[0, k, rows, :], probe[1, k, rows, :]
                add_re = p_re * re + p_im * im
                add_im = p_re * im - p_im * re
                if k == 0:
                    term[0, rows, :] = add_re
                    term[1, rows, :] = add_im
                else:
                    term[0, rows, :] += add_re
                    term[1, rows, :] += add_im
                o_re, o_im = obj[0, rows, :], obj[1, rows, :]
                keep[k, rows, :] += o_re * re + o_im * im
                send[k, rows, :] += o_re * im - o_im * re

    def turn_patch():
        for c in range(width // CHUNK):
            for lanes in (low, high):
                re, im = obj[0, span(c), lanes], obj[1, span(c), lanes]
                obj[0, span(c), lanes] = jnp.where(turn, re, -im)
                obj[1, span(c), lanes] = jnp.where(turn, im, re)

    def add_term():
        for c in range(width // CHUNK):
            target = pl.ds(row + c * CHUNK, CHUNK)
            for p in range(2):
                first = pltpu.roll(term[p, span(c), low], shift, 1)
                second = pltpu.roll(term[p, span(c), high], shift, 1)
                totals[p, block, target, :] += jnp.where(at_or_after, first, 0.0)
                totals[p, block + 1, target, :] += jnp.where(at_or_after, second, first)
                totals[p, block + 2, target, :] += jnp.where(at_or_after, 0.0, second)

    gather_patch()
    make_psi(0)
    make_psi(1)
    for k in range(modes):
        right_forward(k)
        if k + 2 < modes:
            make_psi(k + 2)
        if k == modes - 2:
            turn_patch()
        if k >= 1:
            left_forward(k - 1)
    left_forward(modes - 1)
    make_ratio()
    make_chi(0)
    make_chi(1)
    for k in range(modes):
        right_backward(k)
        if k + 2 < modes:
            make_chi(k + 2)
        if k >= 1:
            left_backward(k - 1)
        if k >= 2:
            collect(k - 2)
    left_backward(modes - 1)
    collect(modes - 2)
    collect(modes - 1)
    add_term()


class Moves:
    def __init__(self, sems):
        self.sems = sems
        self.started = []

    def begin(self, source, target):
        move = pltpu.make_async_copy(source, target, self.sems.at[len(self.started)])
        move.start()
        self.started.append(move)

    def wait(self):
        for move in self.started:
            move.wait()


def visit_all(later, offsets, counts, tile_rows, tile_cols, ext, pat, *rest):
    width = pat.shape[1]
    margin = width // 2
    base_row = lax.axis_index(ROW) * tile_rows - margin
    base_col = lax.axis_index(COL) * tile_cols - margin

    def visit(number, carry):
        row = offsets[0, number] - base_row
        col = offsets[1, number] - base_col
        beyond = jnp.logical_or(row < margin, row + width > margin + tile_rows)

        @pl.when(beyond if later else jnp.logical_not(beyond))
        def _():
            one_slot(number, row, col, ext, pat, *rest)

        return carry

    lax.fori_loop(0, counts[0, 0], visit, 0)


def first_kernel(
    offsets, counts, tile, inner, outer, pat, probe, table,
    ext, totals, keep, send, obj, term, psi, half, field, ratio, sems,
):
    rows, cols = tile.shape[1:]
    margin = inner.shape[2]
    last = cols // LANES + 1
    core = lax.axis_index(CORE)
    middle = pl.ds(margin, rows)
    moves = Moves(sems)
    for j in range(1, last):
        moves.begin(tile.at[:, :, pl.ds((j - 1) * LANES, LANES)], ext.at[:, j, middle, :])
    moves.begin(inner, ext.at[:, (1 - core) * last, middle, :])
    moves.begin(outer, ext.at[:, core * last, middle, :])
    totals[...] = jnp.zeros_like(totals)
    keep[...] = jnp.zeros_like(keep)
    send[...] = jnp.zeros_like(send)
    moves.wait()
    work = (obj, term, psi, half, field, ratio)
    visit_all(False, offsets, counts, rows, cols, ext, pat, probe, table, totals, keep, send, work)


def second_kernel(
    offsets, counts, above, below, corner_above, corner_below, ext_in, totals_in, keep_in,
    send_in, pat, probe, table,
    totals, keep, send, inner_out, outer_out, inner_ends, outer_ends,
    ext, obj, term, psi, half, field, ratio, sems,
):
    margin, cols = above.shape[1:]
    last = ext.shape[1] - 1
    rows = ext.shape[2] - 2 * margin
    core = lax.axis_index(CORE)
    inner_block, outer_block = (1 - core) * last, core * last
    top, middle, bottom = pl.ds(0, margin), pl.ds(margin, rows), pl.ds(margin + rows, margin)
    moves = Moves(sems)
    moves.begin(ext_in.at[:, :, middle, :], ext.at[:, :, middle, :])
    for j in range(1, last):
        lanes = pl.ds((j - 1) * LANES, LANES)
        moves.begin(above.at[:, :, lanes], ext.at[:, j, top, :])
        moves.begin(below.at[:, :, lanes], ext.at[:, j, bottom, :])
    for n, j in enumerate((inner_block, outer_block)):
        lanes = pl.ds(n * margin, margin)
        moves.begin(corner_above.at[:, :, lanes], ext.at[:, j, top, :])
        moves.begin(corner_below.at[:, :, lanes], ext.at[:, j, bottom, :])
    totals[...] = totals_in[...]
    keep[...] = keep_in[...]
    send[...] = send_in[...]
    moves.wait()
    work = (obj, term, psi, half, field, ratio)
    visit_all(True, offsets, counts, rows, cols, ext, pat, probe, table, totals, keep, send, work)
    moves = Moves(sems)
    for edge, ends, j in (
        (outer_out, outer_ends, outer_block), (inner_out, inner_ends, inner_block)
    ):
        moves.begin(totals.at[:, j, top, :], ends.at[:, pl.ds(0, margin), :])
        moves.begin(totals.at[:, j, bottom, :], ends.at[:, pl.ds(margin, margin), :])
        moves.begin(totals.at[:, j, middle, :], edge)
    moves.wait()


def slot_scratch(modes, width):
    return [
        pltpu.VMEM((2, width, width), F32),
        pltpu.VMEM((2, width, width), F32),
        pltpu.VMEM((modes, 2, width, width), BF16),
        pltpu.VMEM((modes, 2, width, width), BF16),
        pltpu.VMEM((modes, 2, width, width), F32),
        pltpu.VMEM((2, width // 2, width), F32),
        pltpu.SemaphoreType.DMA((16,)),
    ]


def shapes(*dims):
    return [jax.ShapeDtypeStruct(shape, F32) for shape in dims]


def cost(slots, modes, width):
    return pl.CostEstimate(
        flops=slots * modes * width * width * width * 16,
        bytes_accessed=30 * MIB,
        transcendentals=slots * width * width,
    )


def first_slots(offsets, counts, tile, inner, outer, patterns, probe, table):
    modes, width = probe.shape[1:3]
    rows, cols = tile.shape[1:]
    grown = (2, cols // LANES + 2, rows + 2 * inner.shape[2], LANES)
    plane = (modes, width, width)
    return pl.pallas_call(
        first_kernel,
        out_shape=shapes(grown, grown, plane, plane),
        in_specs=[SMEM] * 2 + [FREE] * 3 + [VMEM] * 3,
        out_specs=[VMEM] * 4,
        scratch_shapes=slot_scratch(modes, width),
        compiler_params=pltpu.CompilerParams(vmem_limit_bytes=24 * MIB),
        cost_estimate=cost(4, modes, width),
        name="slots_first",
    )(offsets, counts, tile, inner, outer, patterns, probe, table)


def second_slots(offsets, counts, sides, ext, totals, keep, send, patterns, probe, table):
    modes, width = probe.shape[1:3]
    margin = sides[0].shape[1]
    rows = ext.shape[2] - 2 * margin
    edge, ends = (2, rows, margin), (2, 2 * margin, margin)
    return pl.pallas_call(
        second_kernel,
        out_shape=shapes(totals.shape, keep.shape, send.shape, edge, edge, ends, ends),
        in_specs=[SMEM] * 2 + [FREE] * 5 + [VMEM] * 6,
        out_specs=[VMEM] * 3 + [FREE] * 4,
        scratch_shapes=[pltpu.VMEM(ext.shape, F32)] + slot_scratch(modes, width),
        input_output_aliases={7: 0, 8: 1, 9: 2},
        compiler_params=pltpu.CompilerParams(vmem_limit_bytes=24 * MIB),
        cost_estimate=cost(4, modes, width),
        name="slots_second",
    )(offsets, counts, *sides, ext, totals, keep, send, patterns, probe, table)


def prepare_kernel(patterns, probe, out, wide, moving):
    wide[...] = probe[...].astype(F32)
    slots, width = patterns.shape[:2]
    mid = width // 2
    source = lax.broadcasted_iota(jnp.int32, (width, width), 0)
    target = lax.broadcasted_iota(jnp.int32, (width, width), 1)
    wanted = jnp.where(target < mid, 2 * target, 2 * target - (width - 1))
    pick = (source == wanted).astype(BF16)

    def one(number, carry):
        value = patterns[number]
        total = None
        for _ in range(3):
            part = value.astype(BF16)
            value = value - part.astype(F32)
            moved = dot(part, pick)
            total = moved if total is None else total + moved
        for side in range(2):
            lanes = pl.ds(side * mid, mid)
            moving[side] = total[:, side * mid : side * mid + mid]
            for parity in range(2):
                out[number, pl.ds(parity * mid, mid), lanes] = moving[side, pl.ds(parity, mid, 2), :]
        return carry

    lax.fori_loop(0, slots, one, 0)


def prepare(patterns, probe):
    return pl.pallas_call(
        prepare_kernel,
        out_shape=shapes(patterns.shape, probe.shape),
        in_specs=[VMEM] * 2,
        out_specs=[VMEM] * 2,
        scratch_shapes=[pltpu.VMEM((2, patterns.shape[1], patterns.shape[2] // 2), F32)],
        compiler_params=pltpu.CompilerParams(vmem_limit_bytes=12 * MIB),
        cost_estimate=pl.CostEstimate(
            flops=patterns.size * 256 * 6, bytes_accessed=9 * MIB, transcendentals=0
        ),
        name="prepare",
    )(patterns, probe)


def cut_kernel(tile, top, bottom, inner, outer, sems):
    margin = top.shape[1]
    rows, cols = tile.shape[1:]
    core = lax.axis_index(CORE)

    def strip(start):
        return tile.at[:, :, pl.ds(pl.multiple_of(start, LANES), margin)]

    moves = Moves(sems)
    moves.begin(tile.at[:, pl.ds(rows - margin, margin), :], bottom)
    moves.begin(tile.at[:, pl.ds(0, margin), :], top)
    moves.begin(strip(core * (cols - margin)), outer)
    moves.begin(strip((1 - core) * (cols - margin)), inner)
    moves.wait()


def cut(tile, margin):
    rows, cols = tile.shape[1:]
    return pl.pallas_call(
        cut_kernel,
        out_shape=shapes((2, margin, cols), (2, margin, cols), (2, rows, margin), (2, rows, margin)),
        in_specs=[FREE],
        out_specs=[FREE] * 4,
        scratch_shapes=[pltpu.SemaphoreType.DMA((4,))],
        compiler_params=pltpu.CompilerParams(vmem_limit_bytes=MIB),
        cost_estimate=pl.CostEstimate(flops=0, bytes_accessed=4 * MIB, transcendentals=0),
        name="cut",
    )(tile)


def add_sides(add, inner, outer, last):
    core = lax.axis_index(CORE)

    @pl.when(core == 0)
    def _():
        add(outer, 0)
        add(inner, last)

    @pl.when(core != 0)
    def _():
        add(inner, 0)
        add(outer, last)


def mix_kernel(totals, inner, outer, keep, received, top, bottom, pair):
    margin = top.shape[1]
    blocks = totals.shape[1] - 2
    low_end = totals.shape[2] - margin
    sign = jnp.where(lax.axis_index(CORE) == 0, -1.0, 1.0).astype(F32)
    for k in range(keep.shape[0]):
        pair[k] = keep[k] + received[k] * sign
    for j in range(blocks):
        lanes = pl.ds(j * LANES, LANES)
        top[:, :, lanes] = totals[:, 1 + j, :margin, :]
        bottom[:, :, lanes] = totals[:, 1 + j, low_end:, :]

    def add(side, j):
        lanes = pl.ds(j * LANES, LANES)
        top[:, :, lanes] += side[:, :margin, :]
        bottom[:, :, lanes] += side[:, margin:, :]

    add_sides(add, inner, outer, blocks - 1)


def mix(totals, inner, outer, keep, received):
    margin = inner.shape[1] // 2
    strip = (2, margin, (totals.shape[1] - 2) * LANES)
    return pl.pallas_call(
        mix_kernel,
        out_shape=shapes(strip, strip, keep.shape),
        in_specs=[VMEM] * 5,
        out_specs=[VMEM] * 3,
        compiler_params=pltpu.CompilerParams(vmem_limit_bytes=12 * MIB),
        cost_estimate=pl.CostEstimate(flops=600_000, bytes_accessed=6 * MIB, transcendentals=0),
        name="mix",
    )(totals, inner, outer, keep, received)


def fold_kernel(pieces, out):
    total = pieces[0]
    for n in range(1, pieces.shape[0]):
        total = total + pieces[n]
    for n in range(pieces.shape[0]):
        out[n] = total


def fold(pieces):
    return pl.pallas_call(
        fold_kernel,
        out_shape=jax.ShapeDtypeStruct(pieces.shape, F32),
        in_specs=[VMEM],
        out_specs=VMEM,
        compiler_params=pltpu.CompilerParams(vmem_limit_bytes=4 * MIB),
        cost_estimate=pl.CostEstimate(flops=300_000, bytes_accessed=2 * MIB, transcendentals=0),
        name="fold",
    )(pieces)


def finish_kernel(totals, inner, outer, above, below, out, result, sems):
    margin = above.shape[1]
    rows = inner.shape[1]
    blocks = totals.shape[1] - 2
    moves = Moves(sems)
    for p in range(2):
        for j in range(blocks):
            lanes = pl.ds(j * LANES, LANES)
            result[p, :, lanes] = totals[p, 1 + j, margin : margin + rows, :]
        result[p, :margin, :] += above[p]
        result[p, rows - margin :, :] += below[p]

        def add(side, j):
            result[p, :, pl.ds(j * LANES, LANES)] += side[p]

        add_sides(add, inner, outer, blocks - 1)
        moves.begin(result.at[p], out.at[p])
    moves.wait()


def finish(totals, inner, outer, above, below):
    shape = (2, inner.shape[1], above.shape[2])
    return pl.pallas_call(
        finish_kernel,
        out_shape=jax.ShapeDtypeStruct(shape, F32),
        in_specs=[VMEM] * 5,
        out_specs=FREE,
        scratch_shapes=[pltpu.VMEM(shape, F32), pltpu.SemaphoreType.DMA((2,))],
        compiler_params=pltpu.CompilerParams(vmem_limit_bytes=14 * MIB),
        cost_estimate=pl.CostEstimate(flops=600_000, bytes_accessed=7 * MIB, transcendentals=0),
        name="finish",
    )(totals, inner, outer, above, below)


def join_kernel(own, other, out, sems):
    core = lax.axis_index(CORE)
    moves = Moves(sems)
    moves.begin(own, out.at[core])
    moves.begin(other, out.at[1 - core])
    moves.wait()


def join(own, other):
    return pl.pallas_call(
        join_kernel,
        out_shape=jax.ShapeDtypeStruct((2,) + own.shape, F32),
        in_specs=[FREE, FREE],
        out_specs=FREE,
        scratch_shapes=[pltpu.SemaphoreType.DMA((2,))],
        compiler_params=pltpu.CompilerParams(vmem_limit_bytes=MIB),
        cost_estimate=pl.CostEstimate(flops=0, bytes_accessed=4 * MIB, transcendentals=0),
        name="join",
    )(own, other)


def up(block, axes):
    count = lax.axis_size(axes)
    return lax.ppermute(block, axes, [(i, i + 1) for i in range(count - 1)])


def down(block, axes):
    count = lax.axis_size(axes)
    return lax.ppermute(block, axes, [(i + 1, i) for i in range(count - 1)])


def swap_inner(block, axes):
    count = lax.axis_size(axes)
    return lax.ppermute(block, axes, [(i, i ^ 1) for i in range(count)])


def swap_outer(block, axes):
    count = lax.axis_size(axes)
    pairs = [(i, i + 1) for i in range(1, count - 1, 2)]
    return lax.ppermute(block, axes, pairs + [(j, i) for i, j in pairs])


def on_device(object_field, probe, patterns, offsets, counts):
    rows = object_field.shape[1]
    width = patterns.shape[1]
    modes = probe.shape[1]
    margin = width // 2

    top, bottom, inner, outer = cut(object_field, margin)
    from_above = up(bottom, ROW)
    from_below = down(top, ROW)
    outer = swap_outer(outer, COL)
    inner = swap_inner(inner, COL)

    def corners(start):
        span = slice(start, start + margin)
        return jnp.concatenate([inner[:, span], outer[:, span]], axis=2)

    corner_above = up(corners(rows - margin), ROW)
    corner_below = down(corners(0), ROW)

    table = jnp.asarray(tables(width))
    measured, wide = prepare(patterns, probe)
    ext, totals, keep, send = first_slots(
        offsets, counts, object_field, inner, outer, measured, wide, table
    )
    sides = (from_above, from_below, corner_above, corner_below)
    totals, keep, send, inner, outer, inner_ends, outer_ends = second_slots(
        offsets, counts, sides, ext, totals, keep, send, measured, wide, table
    )

    outer_ends = swap_outer(outer_ends, COL)
    inner_ends = swap_inner(inner_ends, COL)
    received = swap_inner(send, COL)
    top, bottom, pair = mix(totals, inner_ends, outer_ends, keep, received)
    chips = lax.axis_size(CHIP)
    pieces = pair.reshape(chips, modes * width // chips, width)
    pieces = lax.all_to_all(pieces, CHIP, 0, 0, tiled=True)
    from_above = up(bottom, ROW)
    from_below = down(top, ROW)
    outer = swap_outer(outer, COL)
    inner = swap_inner(inner, COL)
    pieces, from_above, from_below = lax.optimization_barrier((pieces, from_above, from_below))
    gathered = lax.all_to_all(fold(pieces), CHIP, 0, 0, tiled=True).reshape(modes, width, width)
    object_grad = finish(totals, inner, outer, from_above, from_below)
    gathered, object_grad = lax.optimization_barrier((gathered, object_grad))
    other = swap_inner(gathered, COL)
    return (object_grad, join(gathered, other))


def solution(mesh):
    rows, cols = mesh.devices.shape
    side = math.isqrt(rows)
    fine = Mesh(mesh.devices.reshape(side, side, cols // 2, 2), CHIP + (CORE,))
    in_specs = (P(None, ROW, COL), P(), P(ROW + COL, None, None), P(None, ROW + COL), P(ROW, COL))
    out_specs = (P(None, ROW, COL), P())
    return jax.shard_map(
        on_device, mesh=fine, in_specs=in_specs, out_specs=out_specs, check_vma=False
    )
```

time: 453 us -> 137 us (0.30)
  waiting for transfers between devices: 228 us -> 42.5 us
  local copies, waits for them, and re-layouts: 75.7 us -> 6.16 us
  other arithmetic: 40.8 us -> 0.04 us
  matrix products: 33.2 us -> 0 us
  Pallas kernels: 0 us -> 28.6 us
  starting transfers between devices: 31.4 us -> 58.4 us
  loops' own time: 25.6 us -> 0 us
  between operations: 14.8 us -> 1.6 us
    psum x1 -> x0, waiting for transfers between devices: 179 us -> none  [on_device(): probe_grad = lax.psum(probe_total, ('row', 'col'))]
    dot_general x80 -> x0, matrix products: 33.2 us -> none  [the longest x40 16.6 us: left_dot(): jnp.einsum('ab,kbc->kac', table, matrix, preferred_element_type=jnp.float32)]
    all_to_all x0 -> x2, starting transfers between devices: none -> 30.8 us  [the longest x1 21.2 us: on_device(): pieces = lax.all_to_all(pieces, CHIP, 0, 0, tiled=True)]
    dynamic_update_slice x5 -> x0, local copies, waits for them, and re-layouts: 29.7 us -> none  [add_patch(): lax.dynamic_update_slice(totals, previous + term, (zero_index, start_row,...]
    pallas_call x0 -> x8, Pallas kernels: none -> 28.6 us  [the longest x1 14.5 us: first_slots(): pl.pallas_call(first_kernel, out_shape=shapes(grown, grown, plane, plane)...]
    another operation x9 -> x0, loops' own time: 25.6 us -> none  [the longest x8 20.2 us: visit(): return lax.cond(alive[number], work, lambda inner: inner, carried)]
    add x10 -> x0, other arithmetic: 13.6 us -> none  [the longest x5 10.8 us: add_patch(): previous + term]
    dynamic_slice x18 -> x0, local copies, waits for them, and re-layouts: 10.6 us -> none  [the longest x8 4.73 us: visit(): return lax.cond(alive[number], work, lambda inner: inner, carried)]
  transfers between devices with their start and end apart: 9 -> 16, of which waited for: 8 -> 5; matrix products, arithmetic and copies ran while one was open for 4% -> 0% of each run, Pallas kernels for 0% -> 14%
where the time goes in v2:
time: 137 us
  starting transfers between devices  58.4 us (43%)
  waiting for transfers between devices  42.5 us (31%)
  Pallas kernels  28.6 us (21%)
  local copies, waits for them, and re-layouts  6.16 us (4%)
  between operations  1.6 us (1%)
    all_to_all x1, starting transfers between devices, on_device(): pieces = lax.all_to_all(pieces, CHIP, 0, 0, tiled=True)  21.2 us
    ppermute x3, waiting for transfers between devices, swap_outer(): return lax.ppermute(block, axes, pairs + [(j, i) for i, j in pairs])  19.9 us
    ppermute x3, waiting for transfers between devices, up(): return lax.ppermute(block, axes, [(i, i + 1) for i in range(count - 1)])  18.1 us
    pallas_call x1, Pallas kernels, first_slots(): pl.pallas_call(first_kernel, out_shape=shapes(grown, grown, plane, plane)...  14.5 us
    ppermute x3, starting transfers between devices, up(): return lax.ppermute(block, axes, [(i, i + 1) for i in range(count - 1)])  10.2 us
    ppermute x3, starting transfers between devices, swap_outer(): return lax.ppermute(block, axes, pairs + [(j, i) for i, j in pairs])  10.1 us
    all_to_all x1, starting transfers between devices, on_device(): lax.all_to_all(fold(pieces), CHIP, 0, 0, tiled=True)  9.55 us
    unnamed x18, local copies, waits for them, and re-layouts  6.12 us
  transfers between devices with their start and end apart: 16, of which 5 were waited for; matrix products, arithmetic and copies ran while one was open for 0% of the time, Pallas kernels for 14%

profile of v2, /device:TPU:1, one launch (start us, length us, event | category | flops | bytes accessed | tf_op | source)
XLA Modules:
  0.0 137.2 jit_solution(2285697395956954061)
XLA Ops:
  0.6 0.0 copy-start.2
  0.6 0.0 copy-start.3
  0.7 1.7 %copy-done.3 = f32[2,512,512]{2,1,0:T(8,128)S(1)} copy-done((f32[2,512,512]{2,1,0:T(8,128)S(1)}, f32[2,512,512]{2,1,0:T(8,128)}, u32[]{:S(2)}) %copy-start.3) | copy-done | bytes 2097176
  2.4 0.3 cut.1
  2.6 1.5 %collective-permute-start.2 = (f32[2,512,128]{2,1,0:T(8,128)S(1)}, f32[2,512,128]{2,1,0:T(8,128)S(1)}, u32[]{:S(2)}, u32[]{:S(2)}) collective-permute-start(f32[2,512,128]{2,1,0:T(8,128)S(1)} %get-tuple-element.29), channel_id=1, source_target_pairs={{0,1},{1,0},{2,3},{3,2},{4,5},{5,4},{6,7},{7,6},{8,9},{9,8},{10,11... | collective-permute-start | bytes 1572872 | tf_op jit(solution)/shard_map/ppermute | solution.py:573
  4.1 3.5 %collective-permute-start.3 = (f32[2,512,128]{2,1,0:T(8,128)S(1)}, f32[2,512,128]{2,1,0:T(8,128)S(1)}, u32[]{:S(2)}, u32[]{:S(2)}) collective-permute-start(f32[2,512,128]{2,1,0:T(8,128)S(1)} %get-tuple-element.30), channel_id=1, source_target_pairs={{1,2},{3,4},{5,6},{2,1},{4,3},{6,5},{9,10},{11,12},{13,14},{10,9},... | collective-permute-start | bytes 1572872 | tf_op jit(solution)/shard_map/ppermute | solution.py:579
  7.7 3.2 %collective-permute-start = (f32[2,128,512]{2,1,0:T(8,128)S(1)}, f32[2,128,512]{2,1,0:T(8,128)S(1)}, u32[]{:S(2)}, u32[]{:S(2)}) collective-permute-start(f32[2,128,512]{2,1,0:T(8,128)S(1)} %get-tuple-element.27), channel_id=1, source_target_pairs={{0,8},{8,16},{16,24},{24,32},{32,40},{40,48},{48,56},{56,64},{64,7... | collective-permute-start | bytes 1572872 | tf_op jit(solution)/shard_map/ppermute | solution.py:563
  10.9 1.3 collective-permute-start.1
  12.9 0.0 copy-start.5
  12.9 1.2 copy-done.5
  14.1 2.5 %prepare.1 = (f32[8,256,256]{2,1,0:T(8,128)S(1)}, f32[2,4,256,256]{3,2,1,0:T(8,128)S(1)}) custom-call(f32[8,256,256]{2,1,0:T(8,128)S(1)} %copy-done.2, bf16[2,4,256,256]{3,2,1,0:T(8,128)(2,1)S(1)} %copy-done.5), custom_call_target="tpu_custom_call" | custom-call | flops 805306368 | bytes 9437184 | tf_op jit(solution)/shard_map/prepare/pallas_call | solution.py:394
  16.7 0.0 collective-permute-done.2.inner
  16.7 0.0 collective-permute-done.3.outer
  16.8 4.0 %collective-permute-start.4 = (f32[2,128,256]{2,1,0:T(8,128)S(1)}, f32[2,128,256]{2,1,0:T(8,128)S(1)}, u32[]{:S(2)}, u32[]{:S(2)}) collective-permute-start(f32[2,128,256]{2,1,0:T(8,128)S(1)} %pad_maximum_fusion), channel_id=1, source_target_pairs={{0,8},{8,16},{16,24},{24,32},{32,40},{40,48},{48,56},{56,64},{64,7... | collective-permute-start | bytes 786440 | tf_op jit(solution)/shard_map/ppermute | solution.py:563
  20.8 1.3 collective-permute-start.5
  22.1 14.5 %slots_first.1 = (f32[2,6,768,128]{3,2,1,0:T(8,128)S(1)}, f32[2,6,768,128]{3,2,1,0:T(8,128)S(1)}, f32[4,256,256]{2,1,0:T(8,128)S(1)}, f32[4,256,256]{2,1,0:T(8,128)S(1)}) custom-call(s32[2,8]{1,0:T(2,128)S(1)} %copy-done.7, s32[1,1]{1,0:T(1,128)S(6)} %copy.14.counts, f32[2,512,512]{2,1,0:T(8,128)S(1)} %copy-done.4, ...), custom_call_target="tpu_custom_call" | custom-call | flops 4294967296 | bytes 31457280 | tf_op jit(solution)/shard_map/slots_first/pallas_call | solution.py:336
  36.7 0.0 collective-permute-done.above
  36.7 0.0 collective-permute-done.1.below
  36.7 0.0 collective-permute-done.4.corner_above
  36.7 0.0 collective-permute-done.5.corner_below
  36.7 5.7 %slots_second.1 = (f32[2,6,768,128]{3,2,1,0:T(8,128)S(1)}, f32[4,256,256]{2,1,0:T(8,128)S(1)}, f32[4,256,256]{2,1,0:T(8,128)S(1)}, f32[2,512,128]{2,1,0:T(8,128)...) custom-call(s32[2,8]{1,0:T(2,128)S(1)} %copy-done.7, ...), custom_call_target="tpu_custom_call", output_to_operand_aliasing={{0}: (7, {}), {1}: (8, {}), {2}: (9, {})} | custom-call | flops 4294967296 | bytes 31457280 | tf_op jit(solution)/shard_map/slots_second/pallas_call | solution.py:353
  42.4 0.0 copy-start
  42.4 0.1 collective-permute-start.8
  42.5 0.5 collective-permute-start.6
  43.0 3.5 %collective-permute-start.7 = (f32[2,256,128]{2,1,0:T(8,128)S(1)}, f32[2,256,128]{2,1,0:T(8,128)S(1)}, u32[]{:S(2)}, u32[]{:S(2)}) collective-permute-start(f32[2,256,128]{2,1,0:T(8,128)S(1)} %get-tuple-element.39), channel_id=1, source_target_pairs={{1,2},{3,4},{5,6},{2,1},{4,3},{6,5},{9,10},{11,12},{13,14},{10,9},... | collective-permute-start | bytes 786440 | tf_op jit(solution)/shard_map/ppermute | solution.py:579
  46.5 0.0 collective-permute-done.6.inner
  46.6 4.1 %collective-permute-done.7.outer = f32[2,256,128]{2,1,0:T(8,128)S(1)} collective-permute-done((f32[2,256,128]{2,1,0:T(8,128)S(1)}, f32[2,256,128]{2,1,0:T(8,128)S(1)}, u32[]{:S(2)}, u32[]{:S(2)}) %collective-permute-start.7) | collective-permute-done | bytes 262176 | tf_op jit(solution)/shard_map/ppermute | solution.py:579
  50.7 0.0 collective-permute-done.8.received
  50.7 1.5 %mix.1 = (f32[2,128,512]{2,1,0:T(8,128)S(1)}, f32[2,128,512]{2,1,0:T(8,128)}, f32[4,256,256]{2,1,0:T(8,128)}) custom-call(f32[2,6,768,128]{3,2,1,0:T(8,128)S(1)} %get-tuple-element.37.totals, f32[2,256,128]{2,1,0:T(8,128)S(1)} %collective-permute-done.6.inner, f32[2,256,128]{2,1,0:T(8,128)S(1)} %collective-permute-done.7.outer, ...), custom_call_target="tpu_custom_call" | custom-call | flops 600000 | bytes 6291456 | tf_op jit(solution)/shard_map/mix/pallas_call | solution.py:475
  52.2 0.8 copy-done.8
  53.0 21.2 %all-to-all-start = ((f32[64,16,256]{2,1,0:T(8,128)}), f32[64,16,256]{2,1,0:T(8,128)S(1)}, u32[]{:S(2)}, u32[]{:S(2)}) async-start(f32[64,16,256]{2,1,0:T(8,128)} %bitcast), calls=%async_computation | async-start | bytes 2097152 | tf_op jit(solution)/shard_map/all_to_all | solution.py:617
  74.3 2.9 %collective-permute-start.9 = (f32[2,128,512]{2,1,0:T(8,128)}, f32[2,128,512]{2,1,0:T(8,128)S(1)}, u32[]{:S(2)}, u32[]{:S(2)}) collective-permute-start(f32[2,128,512]{2,1,0:T(8,128)} %get-tuple-element.43), channel_id=1, source_target_pairs={{0,8},{8,16},{16,24},{24,32},{32,40},{40,48},{48,56},{56,64},{64,7... | collective-permute-start | bytes 1572872 | tf_op jit(solution)/shard_map/ppermute | solution.py:563
  77.2 1.3 collective-permute-start.10
  78.5 18.1 %collective-permute-done.9.above = f32[2,128,512]{2,1,0:T(8,128)S(1)} collective-permute-done((f32[2,128,512]{2,1,0:T(8,128)}, f32[2,128,512]{2,1,0:T(8,128)S(1)}, u32[]{:S(2)}, u32[]{:S(2)}) %collective-permute-start.9) | collective-permute-done | bytes 524320 | tf_op jit(solution)/shard_map/ppermute | solution.py:563
  96.7 1.8 %collective-permute-done.10.below = f32[2,128,512]{2,1,0:T(8,128)S(1)} collective-permute-done((f32[2,128,512]{2,1,0:T(8,128)}, f32[2,128,512]{2,1,0:T(8,128)S(1)}, u32[]{:S(2)}, u32[]{:S(2)}) %collective-permute-start.10) | collective-permute-done | bytes 524320 | tf_op jit(solution)/shard_map/ppermute | solution.py:568
  98.4 0.0 all-to-all-done.pieces
  98.4 1.2 fold.1
  99.6 9.6 %all-to-all-start.1 = ((f32[64,16,256]{2,1,0:T(8,128)}), f32[64,16,256]{2,1,0:T(8,128)S(1)}, u32[]{:S(2)}, u32[]{:S(2)}) async-start(f32[64,16,256]{2,1,0:T(8,128)} %fold.1), calls=%async_computation.1 | async-start | bytes 2097152 | tf_op jit(solution)/shard_map/all_to_all | solution.py:623
  109.1 1.2 collective-permute-start.11
  110.3 3.1 %collective-permute-start.12 = (f32[2,512,128]{2,1,0:T(8,128)S(1)}, f32[2,512,128]{2,1,0:T(8,128)S(1)}, u32[]{:S(2)}, u32[]{:S(2)}) collective-permute-start(f32[2,512,128]{2,1,0:T(8,128)S(1)} %get-tuple-element.47), channel_id=1, source_target_pairs={{1,2},{3,4},{5,6},{2,1},{4,3},{6,5},{9,10},{11,12},{13,14},{10,9},... | collective-permute-start | bytes 1572872 | tf_op jit(solution)/shard_map/ppermute | solution.py:579
  113.4 0.0 collective-permute-done.11.inner
  113.5 15.8 %collective-permute-done.12.outer = f32[2,512,128]{2,1,0:T(8,128)S(1)} collective-permute-done((f32[2,512,128]{2,1,0:T(8,128)S(1)}, f32[2,512,128]{2,1,0:T(8,128)S(1)}, u32[]{:S(2)}, u32[]{:S(2)}) %collective-permute-start.12) | collective-permute-done | bytes 524320 | tf_op jit(solution)/shard_map/ppermute | solution.py:579
  129.3 2.3 %copy-done.1 = f32[2,6,768,128]{3,2,1,0:T(8,128)S(1)} copy-done((f32[2,6,768,128]{3,2,1,0:T(8,128)S(1)}, f32[2,6,768,128]{3,2,1,0:T(8,128)}, u32[]{:S(2)}) %copy-start.1) | copy-done | bytes 4718616
  131.6 1.5 %finish.1 = f32[2,512,512]{2,1,0:T(8,128)} custom-call(f32[2,6,768,128]{3,2,1,0:T(8,128)S(1)} %copy-done.1, f32[2,512,128]{2,1,0:T(8,128)S(1)} %collective-permute-done.11.inner, f32[2,512,128]{2,1,0:T(8,128)S(1)} %collective-permute-done.12.outer, f32[2,128,512]{2,1,0:T(8,128)S(1)} %collective-permute-done.9.above, ...), custom_call_target="tpu_custom_call" | custom-call | flops 600000 | bytes 7340032 | tf_op jit(solution)/shard_map/finish/pallas_call | solution.py:528
  133.1 0.0 all-to-all-done.1
  133.2 0.1 collective-permute-start.13
  133.2 2.6 %collective-permute-done.13.other = f32[4,256,256]{2,1,0:T(8,128)S(1)} collective-permute-done((f32[4,256,256]{2,1,0:T(8,128)S(1)}, f32[4,256,256]{2,1,0:T(8,128)S(1)}, u32[]{:S(2)}, u32[]{:S(2)}) %collective-permute-start.13) | collective-permute-done | bytes 1048608 | tf_op jit(solution)/shard_map/ppermute | solution.py:573
  135.9 1.3 join.1
  (14 shorter events, 0.1 us)
Async XLA Ops:
  0.6 12.2 %copy-start.2 = (f32[8,256,256]{2,1,0:T(8,128)S(1)}, f32[8,256,256]{2,1,0:T(8,128)}, u32[]{:S(2)}) copy-start(f32[8,256,256]{2,1,0:T(8,128)} %patterns.1) | copy-start | bytes 6291460
  0.6 1.7 %copy-start.3 = (f32[2,512,512]{2,1,0:T(8,128)S(1)}, f32[2,512,512]{2,1,0:T(8,128)}, u32[]{:S(2)}) copy-start(f32[2,512,512]{2,1,0:T(8,128)} %tile.3) | copy-start | bytes 6291460
  2.6 14.0 %collective-permute-start.2 = (f32[2,512,128]{2,1,0:T(8,128)S(1)}, f32[2,512,128]{2,1,0:T(8,128)S(1)}, u32[]{:S(2)}, u32[]{:S(2)}) collective-permute-start(f32[2,512,128]{2,1,0:T(8,128)S(1)} %get-tuple-element.29), channel_id=1, source_target_pairs={{0,1},{1,0},{2,3},{3,2},{4,5},{5,4},{6,7},{7,6},{8,9},{9,8},{10,11... | collective-permute-start | bytes 1572872 | tf_op jit(solution)/shard_map/ppermute | solution.py:573
  4.1 12.6 %collective-permute-start.3 = (f32[2,512,128]{2,1,0:T(8,128)S(1)}, f32[2,512,128]{2,1,0:T(8,128)S(1)}, u32[]{:S(2)}, u32[]{:S(2)}) collective-permute-start(f32[2,512,128]{2,1,0:T(8,128)S(1)} %get-tuple-element.30), channel_id=1, source_target_pairs={{1,2},{3,4},{5,6},{2,1},{4,3},{6,5},{9,10},{11,12},{13,14},{10,9},... | collective-permute-start | bytes 1572872 | tf_op jit(solution)/shard_map/ppermute | solution.py:579
  7.7 29.0 %collective-permute-start = (f32[2,128,512]{2,1,0:T(8,128)S(1)}, f32[2,128,512]{2,1,0:T(8,128)S(1)}, u32[]{:S(2)}, u32[]{:S(2)}) collective-permute-start(f32[2,128,512]{2,1,0:T(8,128)S(1)} %get-tuple-element.27), channel_id=1, source_target_pairs={{0,8},{8,16},{16,24},{24,32},{32,40},{40,48},{48,56},{56,64},{64,7... | collective-permute-start | bytes 1572872 | tf_op jit(solution)/shard_map/ppermute | solution.py:563
  10.9 25.8 %collective-permute-start.1 = (f32[2,128,512]{2,1,0:T(8,128)S(1)}, f32[2,128,512]{2,1,0:T(8,128)S(1)}, u32[]{:S(2)}, u32[]{:S(2)}) collective-permute-start(f32[2,128,512]{2,1,0:T(8,128)S(1)} %get-tuple-element.28), channel_id=1, source_target_pairs={{8,0},{16,8},{24,16},{32,24},{40,32},{48,40},{56,48},{64,56},{72,6... | collective-permute-start | bytes 1572872 | tf_op jit(solution)/shard_map/ppermute | solution.py:568
  12.9 1.2 copy-start.5
  14.1 8.0 %copy-start.4 = (f32[2,512,512]{2,1,0:T(8,128)S(1)}, f32[2,512,512]{2,1,0:T(8,128)}, u32[]{:S(2)}) copy-start(f32[2,512,512]{2,1,0:T(8,128)} %tile.3) | copy-start | bytes 6291460
  14.1 8.0 %copy-start.6 = (bf16[4,256,256]{2,1,0:T(8,128)(2,1)S(1)}, bf16[4,256,256]{2,1,0:T(8,128)(2,1)}, u32[]{:S(2)}) copy-start(bf16[4,256,256]{2,1,0:T(8,128)(2,1)} %constant.2.clone.table) | copy-start | bytes 1572868
  14.1 8.0 %copy-start.7 = (s32[2,8]{1,0:T(2,128)S(1)}, s32[2,8]{1,0:T(2,128)}, u32[]{:S(2)}) copy-start(s32[2,8]{1,0:T(2,128)} %offsets.3) | copy-start | bytes 196
  16.8 19.9 %collective-permute-start.4 = (f32[2,128,256]{2,1,0:T(8,128)S(1)}, f32[2,128,256]{2,1,0:T(8,128)S(1)}, u32[]{:S(2)}, u32[]{:S(2)}) collective-permute-start(f32[2,128,256]{2,1,0:T(8,128)S(1)} %pad_maximum_fusion), channel_id=1, source_target_pairs={{0,8},{8,16},{16,24},{24,32},{32,40},{40,48},{48,56},{56,64},{64,7... | collective-permute-start | bytes 786440 | tf_op jit(solution)/shard_map/ppermute | solution.py:563
  20.8 15.9 %collective-permute-start.5 = (f32[2,128,256]{2,1,0:T(8,128)S(1)}, f32[2,128,256]{2,1,0:T(8,128)S(1)}, u32[]{:S(2)}, u32[]{:S(2)}) collective-permute-start(f32[2,128,256]{2,1,0:T(8,128)S(1)} %pad_maximum_fusion.1), channel_id=1, source_target_pairs={{8,0},{16,8},{24,16},{32,24},{40,32},{48,40},{56,48},{64,56},{72,6... | collective-permute-start | bytes 786440 | tf_op jit(solution)/shard_map/ppermute | solution.py:568
  42.4 9.8 %copy-start = (f32[2,6,768,128]{3,2,1,0:T(8,128)}, f32[2,6,768,128]{3,2,1,0:T(8,128)S(1)}, u32[]{:S(2)}) copy-start(f32[2,6,768,128]{3,2,1,0:T(8,128)S(1)} %get-tuple-element.37.totals) | copy-start | bytes 14155780
  42.4 8.3 %collective-permute-start.8 = (f32[4,256,256]{2,1,0:T(8,128)S(1)}, f32[4,256,256]{2,1,0:T(8,128)S(1)}, u32[]{:S(2)}, u32[]{:S(2)}) collective-permute-start(f32[4,256,256]{2,1,0:T(8,128)S(1)} %get-tuple-element.41), channel_id=1, source_target_pairs={{0,1},{1,0},{2,3},{3,2},{4,5},{5,4},{6,7},{7,6},{8,9},{9,8},{10,11... | collective-permute-start | bytes 3145736 | tf_op jit(solution)/shard_map/ppermute | solution.py:573
  42.5 4.0 %collective-permute-start.6 = (f32[2,256,128]{2,1,0:T(8,128)S(1)}, f32[2,256,128]{2,1,0:T(8,128)S(1)}, u32[]{:S(2)}, u32[]{:S(2)}) collective-permute-start(f32[2,256,128]{2,1,0:T(8,128)S(1)} %get-tuple-element.38), channel_id=1, source_target_pairs={{0,1},{1,0},{2,3},{3,2},{4,5},{5,4},{6,7},{7,6},{8,9},{9,8},{10,11... | collective-permute-start | bytes 786440 | tf_op jit(solution)/shard_map/ppermute | solution.py:573
  43.0 7.7 %collective-permute-start.7 = (f32[2,256,128]{2,1,0:T(8,128)S(1)}, f32[2,256,128]{2,1,0:T(8,128)S(1)}, u32[]{:S(2)}, u32[]{:S(2)}) collective-permute-start(f32[2,256,128]{2,1,0:T(8,128)S(1)} %get-tuple-element.39), channel_id=1, source_target_pairs={{1,2},{3,4},{5,6},{2,1},{4,3},{6,5},{9,10},{11,12},{13,14},{10,9},... | collective-permute-start | bytes 786440 | tf_op jit(solution)/shard_map/ppermute | solution.py:579
  52.2 0.8 copy-start.8
  53.0 45.4 %all-to-all-start = ((f32[64,16,256]{2,1,0:T(8,128)}), f32[64,16,256]{2,1,0:T(8,128)S(1)}, u32[]{:S(2)}, u32[]{:S(2)}) async-start(f32[64,16,256]{2,1,0:T(8,128)} %bitcast), calls=%async_computation | async-start | bytes 2097152 | tf_op jit(solution)/shard_map/all_to_all | solution.py:617
  74.3 22.4 %collective-permute-start.9 = (f32[2,128,512]{2,1,0:T(8,128)}, f32[2,128,512]{2,1,0:T(8,128)S(1)}, u32[]{:S(2)}, u32[]{:S(2)}) collective-permute-start(f32[2,128,512]{2,1,0:T(8,128)} %get-tuple-element.43), channel_id=1, source_target_pairs={{0,8},{8,16},{16,24},{24,32},{32,40},{40,48},{48,56},{56,64},{64,7... | collective-permute-start | bytes 1572872 | tf_op jit(solution)/shard_map/ppermute | solution.py:563
  77.2 21.2 %collective-permute-start.10 = (f32[2,128,512]{2,1,0:T(8,128)}, f32[2,128,512]{2,1,0:T(8,128)S(1)}, u32[]{:S(2)}, u32[]{:S(2)}) collective-permute-start(f32[2,128,512]{2,1,0:T(8,128)} %copy-done.8), channel_id=1, source_target_pairs={{8,0},{16,8},{24,16},{32,24},{40,32},{48,40},{56,48},{64,56},{72,6... | collective-permute-start | bytes 1572872 | tf_op jit(solution)/shard_map/ppermute | solution.py:568
  99.6 33.6 %all-to-all-start.1 = ((f32[64,16,256]{2,1,0:T(8,128)}), f32[64,16,256]{2,1,0:T(8,128)S(1)}, u32[]{:S(2)}, u32[]{:S(2)}) async-start(f32[64,16,256]{2,1,0:T(8,128)} %fold.1), calls=%async_computation.1 | async-start | bytes 2097152 | tf_op jit(solution)/shard_map/all_to_all | solution.py:623
  109.1 4.3 %collective-permute-start.11 = (f32[2,512,128]{2,1,0:T(8,128)S(1)}, f32[2,512,128]{2,1,0:T(8,128)S(1)}, u32[]{:S(2)}, u32[]{:S(2)}) collective-permute-start(f32[2,512,128]{2,1,0:T(8,128)S(1)} %get-tuple-element.46), channel_id=1, source_target_pairs={{0,1},{1,0},{2,3},{3,2},{4,5},{5,4},{6,7},{7,6},{8,9},{9,8},{10,11... | collective-permute-start | bytes 1572872 | tf_op jit(solution)/shard_map/ppermute | solution.py:573
  110.3 18.9 %collective-permute-start.12 = (f32[2,512,128]{2,1,0:T(8,128)S(1)}, f32[2,512,128]{2,1,0:T(8,128)S(1)}, u32[]{:S(2)}, u32[]{:S(2)}) collective-permute-start(f32[2,512,128]{2,1,0:T(8,128)S(1)} %get-tuple-element.47), channel_id=1, source_target_pairs={{1,2},{3,4},{5,6},{2,1},{4,3},{6,5},{9,10},{11,12},{13,14},{10,9},... | collective-permute-start | bytes 1572872 | tf_op jit(solution)/shard_map/ppermute | solution.py:579
  129.3 2.3 %copy-start.1 = (f32[2,6,768,128]{3,2,1,0:T(8,128)S(1)}, f32[2,6,768,128]{3,2,1,0:T(8,128)}, u32[]{:S(2)}) copy-start(f32[2,6,768,128]{3,2,1,0:T(8,128)} %copy-done) | copy-start | bytes 14155780
  133.2 2.7 %collective-permute-start.13 = (f32[4,256,256]{2,1,0:T(8,128)S(1)}, f32[4,256,256]{2,1,0:T(8,128)S(1)}, u32[]{:S(2)}, u32[]{:S(2)}) collective-permute-start(f32[4,256,256]{2,1,0:T(8,128)S(1)} %bitcast.2), channel_id=1, source_target_pairs={{0,1},{1,0},{2,3},{3,2},{4,5},{5,4},{6,7},{7,6},{8,9},{9,8},{10,11... | collective-permute-start | bytes 3145736 | tf_op jit(solution)/shard_map/ppermute | solution.py:573

commit v3 on v2

--- a/solution.py
+++ b/solution.py
@@ -15,6 +15,7 @@
 RIGHT = (0, 2)
 LEFT = (1, 3)
 MIB = 1024 * 1024
+SPARE = 15
 FREE = pl.BlockSpec(memory_space=pl.ANY)
 VMEM = pl.BlockSpec(memory_space=pltpu.VMEM)
 ROW, COL, CORE = ("x", "y"), ("z", "core"), "core"
@@ -269,7 +270,7 @@
 def second_kernel(
     offsets, counts, above, below, corner_above, corner_below, ext_in, totals_in, keep_in,
     send_in, pat, probe, table,
-    totals, keep, send, inner_out, outer_out, inner_ends, outer_ends,
+    totals, keep, send, inner_ends, outer_ends,
     ext, obj, term, psi, half, field, ratio, sems,
 ):
     margin, cols = above.shape[1:]
@@ -295,12 +296,9 @@
     work = (obj, term, psi, half, field, ratio)
     visit_all(True, offsets, counts, rows, cols, ext, pat, probe, table, totals, keep, send, work)
     moves = Moves(sems)
-    for edge, ends, j in (
-        (outer_out, outer_ends, outer_block), (inner_out, inner_ends, inner_block)
-    ):
+    for ends, j in ((outer_ends, outer_block), (inner_ends, inner_block)):
         moves.begin(totals.at[:, j, top, :], ends.at[:, pl.ds(0, margin), :])
         moves.begin(totals.at[:, j, bottom, :], ends.at[:, pl.ds(margin, margin), :])
-        moves.begin(totals.at[:, j, middle, :], edge)
     moves.wait()
 
 
@@ -348,13 +346,12 @@
 def second_slots(offsets, counts, sides, ext, totals, keep, send, patterns, probe, table):
     modes, width = probe.shape[1:3]
     margin = sides[0].shape[1]
-    rows = ext.shape[2] - 2 * margin
-    edge, ends = (2, rows, margin), (2, 2 * margin, margin)
+    ends = (2, 2 * margin, LANES)
     return pl.pallas_call(
         second_kernel,
-        out_shape=shapes(totals.shape, keep.shape, send.shape, edge, edge, ends, ends),
+        out_shape=shapes(totals.shape, keep.shape, send.shape, ends, ends),
         in_specs=[SMEM] * 2 + [FREE] * 5 + [VMEM] * 6,
-        out_specs=[VMEM] * 3 + [FREE] * 4,
+        out_specs=[VMEM] * 3 + [FREE] * 2,
         scratch_shapes=[pltpu.VMEM(ext.shape, F32)] + slot_scratch(modes, width),
         input_output_aliases={7: 0, 8: 1, 9: 2},
         compiler_params=pltpu.CompilerParams(vmem_limit_bytes=24 * MIB),
@@ -435,6 +432,49 @@
     )(tile)
 
 
+def pair_kernel(keep, received, out, total, sems):
+    sign = jnp.where(lax.axis_index(CORE) == 0, -1.0, 1.0).astype(F32)
+    moves = Moves(sems)
+    for k in range(keep.shape[0]):
+        total[k] = keep[k] + received[k] * sign
+        moves.begin(total.at[k], out.at[k])
+    moves.wait()
+
+
+def pair_sum(keep, received):
+    return pl.pallas_call(
+        pair_kernel,
+        out_shape=jax.ShapeDtypeStruct(keep.shape, F32),
+        in_specs=[VMEM] * 2,
+        out_specs=FREE,
+        scratch_shapes=[pltpu.VMEM(keep.shape, F32), pltpu.SemaphoreType.DMA((keep.shape[0],))],
+        compiler_params=pltpu.CompilerParams(vmem_limit_bytes=8 * MIB),
+        cost_estimate=pl.CostEstimate(flops=600_000, bytes_accessed=3 * MIB, transcendentals=0),
+        name="pair_sum",
+    )(keep, received)
+
+
+def stash_kernel(totals, out, sems):
+    moves = Moves(sems)
+    for j in range(totals.shape[1]):
+        moves.begin(totals.at[:, j], out.at[:, pl.ds(0, totals.shape[2]), pl.ds(j * LANES, LANES)])
+    moves.wait()
+
+
+def stash(totals):
+    planes, blocks, rows, lanes = totals.shape
+    return pl.pallas_call(
+        stash_kernel,
+        out_shape=jax.ShapeDtypeStruct((planes, SPARE * rows, blocks * lanes), F32),
+        in_specs=[VMEM],
+        out_specs=FREE,
+        scratch_shapes=[pltpu.SemaphoreType.DMA((blocks,))],
+        compiler_params=pltpu.CompilerParams(vmem_limit_bytes=6 * MIB),
+        cost_estimate=pl.CostEstimate(flops=0, bytes_accessed=9 * MIB, transcendentals=0),
+        name="stash",
+    )(totals)
+
+
 def add_sides(add, inner, outer, last):
     core = lax.axis_index(CORE)
 
@@ -449,92 +489,114 @@
         add(outer, last)
 
 
-def mix_kernel(totals, inner, outer, keep, received, top, bottom, pair):
+def load(sources, targets, sems):
+    moves = Moves(sems)
+    for source, target in zip(sources, targets):
+        moves.begin(source, target)
+    moves.wait()
+
+
+def turn_kernel(
+    pieces_in, grown, inner_in, outer_in,
+    copies_out, top_out, bottom_out, inner_out, outer_out,
+    pieces, top, bottom, inner, outer, inner_side, outer_side, sems, out_sems,
+):
     margin = top.shape[1]
-    blocks = totals.shape[1] - 2
-    low_end = totals.shape[2] - margin
-    sign = jnp.where(lax.axis_index(CORE) == 0, -1.0, 1.0).astype(F32)
-    for k in range(keep.shape[0]):
-        pair[k] = keep[k] + received[k] * sign
-    for j in range(blocks):
-        lanes = pl.ds(j * LANES, LANES)
-        top[:, :, lanes] = totals[:, 1 + j, :margin, :]
-        bottom[:, :, lanes] = totals[:, 1 + j, low_end:, :]
-
-    def add(side, j):
-        lanes = pl.ds(j * LANES, LANES)
+    rows = inner_side.shape[1]
+    cols = top.shape[2]
+    core = lax.axis_index(CORE)
+    center = pl.ds(LANES, cols)
+    middle = pl.ds(margin, rows)
+
+    def column(j):
+        return pl.ds(pl.multiple_of(j * (cols + LANES), LANES), LANES)
+
+    first = Moves(sems)
+    first.begin(pieces_in, pieces)
+    first.begin(inner_in, inner)
+    first.begin(outer_in, outer)
+    first.begin(grown.at[:, pl.ds(0, margin), center], top)
+    first.begin(grown.at[:, pl.ds(margin + rows, margin), center], bottom)
+    first.begin(grown.at[:, middle, column(1 - core)], inner_side)
+    first.begin(grown.at[:, middle, column(core)], outer_side)
+    first.wait()
+    last = Moves(out_sems)
+    last.begin(inner_side, inner_out)
+    last.begin(outer_side, outer_out)
+
+    def add(side, start):
+        lanes = pl.ds(start, LANES)
         top[:, :, lanes] += side[:, :margin, :]
         bottom[:, :, lanes] += side[:, margin:, :]
 
-    add_sides(add, inner, outer, blocks - 1)
-
-
-def mix(totals, inner, outer, keep, received):
-    margin = inner.shape[1] // 2
-    strip = (2, margin, (totals.shape[1] - 2) * LANES)
-    return pl.pallas_call(
-        mix_kernel,
-        out_shape=shapes(strip, strip, keep.shape),
-        in_specs=[VMEM] * 5,
-        out_specs=[VMEM] * 3,
-        compiler_params=pltpu.CompilerParams(vmem_limit_bytes=12 * MIB),
-        cost_estimate=pl.CostEstimate(flops=600_000, bytes_accessed=6 * MIB, transcendentals=0),
-        name="mix",
-    )(totals, inner, outer, keep, received)
-
-
-def fold_kernel(pieces, out):
+    add_sides(add, inner, outer, cols - LANES)
+    last.begin(top, top_out)
+    last.begin(bottom, bottom_out)
     total = pieces[0]
     for n in range(1, pieces.shape[0]):
         total = total + pieces[n]
     for n in range(pieces.shape[0]):
-        out[n] = total
-
-
-def fold(pieces):
-    return pl.pallas_call(
-        fold_kernel,
-        out_shape=jax.ShapeDtypeStruct(pieces.shape, F32),
-        in_specs=[VMEM],
-        out_specs=VMEM,
-        compiler_params=pltpu.CompilerParams(vmem_limit_bytes=4 * MIB),
-        cost_estimate=pl.CostEstimate(flops=300_000, bytes_accessed=2 * MIB, transcendentals=0),
-        name="fold",
-    )(pieces)
-
-
-def finish_kernel(totals, inner, outer, above, below, out, result, sems):
+        pieces[n] = total
+    last.begin(pieces, copies_out)
+    last.wait()
+
+
+def turn(pieces, grown, inner, outer):
+    margin = inner.shape[1] // 2
+    rows, cols = grown.shape[1] // SPARE - 2 * margin, grown.shape[2] - 2 * LANES
+    strip, side = (2, margin, cols), (2, rows, LANES)
+    made = [pieces.shape, strip, strip, inner.shape, outer.shape, side, side]
+    return pl.pallas_call(
+        turn_kernel,
+        out_shape=shapes(pieces.shape, strip, strip, side, side),
+        in_specs=[FREE] * 4,
+        out_specs=[FREE] * 5,
+        scratch_shapes=[pltpu.VMEM(x, F32) for x in made]
+        + [pltpu.SemaphoreType.DMA((7,)), pltpu.SemaphoreType.DMA((5,))],
+        compiler_params=pltpu.CompilerParams(vmem_limit_bytes=8 * MIB),
+        cost_estimate=pl.CostEstimate(flops=600_000, bytes_accessed=7 * MIB, transcendentals=0),
+        name="turn",
+    )(pieces, grown, inner, outer)
+
+
+def finish_kernel(
+    grown, inner_in, outer_in, above_in, below_in, out,
+    center, inner, outer, above, below, sems,
+):
     margin = above.shape[1]
-    rows = inner.shape[1]
-    blocks = totals.shape[1] - 2
+    rows, cols = center.shape[1:]
+    middle = grown.at[:, pl.ds(margin, rows), pl.ds(LANES, cols)]
+    load(
+        (middle, inner_in, outer_in, above_in, below_in),
+        (center, inner, outer, above, below),
+        sems,
+    )
     moves = Moves(sems)
     for p in range(2):
-        for j in range(blocks):
-            lanes = pl.ds(j * LANES, LANES)
-            result[p, :, lanes] = totals[p, 1 + j, margin : margin + rows, :]
-        result[p, :margin, :] += above[p]
-        result[p, rows - margin :, :] += below[p]
-
-        def add(side, j):
-            result[p, :, pl.ds(j * LANES, LANES)] += side[p]
-
-        add_sides(add, inner, outer, blocks - 1)
-        moves.begin(result.at[p], out.at[p])
-    moves.wait()
-
-
-def finish(totals, inner, outer, above, below):
-    shape = (2, inner.shape[1], above.shape[2])
+        center[p, :margin, :] += above[p]
+        center[p, rows - margin :, :] += below[p]
+
+        def add(side, start):
+            center[p, :, pl.ds(start, LANES)] += side[p]
+
+        add_sides(add, inner, outer, cols - LANES)
+        moves.begin(center.at[p], out.at[p])
+    moves.wait()
+
+
+def finish(grown, inner, outer, above, below):
+    center = (2, inner.shape[1], above.shape[2])
+    made = (center, inner.shape, outer.shape, above.shape, below.shape)
     return pl.pallas_call(
         finish_kernel,
-        out_shape=jax.ShapeDtypeStruct(shape, F32),
-        in_specs=[VMEM] * 5,
+        out_shape=jax.ShapeDtypeStruct(center, F32),
+        in_specs=[FREE] * 5,
         out_specs=FREE,
-        scratch_shapes=[pltpu.VMEM(shape, F32), pltpu.SemaphoreType.DMA((2,))],
-        compiler_params=pltpu.CompilerParams(vmem_limit_bytes=14 * MIB),
+        scratch_shapes=[pltpu.VMEM(x, F32) for x in made] + [pltpu.SemaphoreType.DMA((5,))],
+        compiler_params=pltpu.CompilerParams(vmem_limit_bytes=8 * MIB),
         cost_estimate=pl.CostEstimate(flops=600_000, bytes_accessed=7 * MIB, transcendentals=0),
         name="finish",
-    )(totals, inner, outer, above, below)
+    )(grown, inner, outer, above, below)
 
 
 def join_kernel(own, other, out, sems):
@@ -579,6 +641,13 @@
     return lax.ppermute(block, axes, pairs + [(j, i) for i, j in pairs])
 
 
+def exchange(counts, pieces):
+    def send(given):
+        return lax.all_to_all(given, CHIP, 0, 0, tiled=True)
+
+    return lax.cond(counts[0, 0] > 0, send, jnp.zeros_like, pieces)
+
+
 def on_device(object_field, probe, patterns, offsets, counts):
     rows = object_field.shape[1]
     width = patterns.shape[1]
@@ -604,26 +673,30 @@
         offsets, counts, object_field, inner, outer, measured, wide, table
     )
     sides = (from_above, from_below, corner_above, corner_below)
-    totals, keep, send, inner, outer, inner_ends, outer_ends = second_slots(
+    totals, keep, send, inner_ends, outer_ends = second_slots(
         offsets, counts, sides, ext, totals, keep, send, measured, wide, table
     )
 
-    outer_ends = swap_outer(outer_ends, COL)
-    inner_ends = swap_inner(inner_ends, COL)
     received = swap_inner(send, COL)
-    top, bottom, pair = mix(totals, inner_ends, outer_ends, keep, received)
+    grown = stash(totals)
+    received, grown = lax.optimization_barrier((received, grown))
+    pair = pair_sum(keep, received)
     chips = lax.axis_size(CHIP)
     pieces = pair.reshape(chips, modes * width // chips, width)
     pieces = lax.all_to_all(pieces, CHIP, 0, 0, tiled=True)
+    outer_ends = swap_outer(outer_ends, COL)
+    inner_ends = swap_inner(inner_ends, COL)
+    copies, top, bottom, inner, outer = turn(pieces, grown, inner_ends, outer_ends)
     from_above = up(bottom, ROW)
     from_below = down(top, ROW)
     outer = swap_outer(outer, COL)
     inner = swap_inner(inner, COL)
-    pieces, from_above, from_below = lax.optimization_barrier((pieces, from_above, from_below))
-    gathered = lax.all_to_all(fold(pieces), CHIP, 0, 0, tiled=True).reshape(modes, width, width)
-    object_grad = finish(totals, inner, outer, from_above, from_below)
-    gathered, object_grad = lax.optimization_barrier((gathered, object_grad))
+    gathered = exchange(counts, copies).reshape(modes, width, width)
+    gathered, inner, outer, from_above, from_below = lax.optimization_barrier(
+        (gathered, inner, outer, from_above, from_below)
+    )
     other = swap_inner(gathered, COL)
+    object_grad = finish(grown, inner, outer, from_above, from_below)
     return (object_grad, join(gathered, other))
 
 

time: 137 us -> 132 us (0.964); the launches traced: 137 us -> 130 us
  blocking collectives: 0 us -> 26.4 us
  waiting for transfers between devices: 42.5 us -> 16.9 us
  Pallas kernels: 28.6 us -> 20.8 us
  starting transfers between devices: 58.4 us -> 61.7 us
  local copies, waits for them, and re-layouts: 6.16 us -> 3.01 us
    all_to_all x0 -> x1, blocking collectives: none -> 26.4 us  [send(): return lax.all_to_all(given, CHIP, 0, 0, tiled=True)]
    ppermute x3, waiting for transfers between devices: 18.1 us -> 0.01 us  [up(): return lax.ppermute(block, axes, [(i, i + 1) for i in range(count - 1)])]
    all_to_all x1, starting transfers between devices: 21.2 us -> 32.4 us  [on_device(): pieces = lax.all_to_all(pieces, CHIP, 0, 0, tiled=True)]
    pallas_call x1, Pallas kernels: 14.5 us -> 4.75 us  [first_slots(): pl.pallas_call(first_kernel, out_shape=shapes(grown, grown, plane, plane)...]
    all_to_all x1 -> x0, starting transfers between devices: 9.55 us -> none  [on_device(): lax.all_to_all(fold(pieces), CHIP, 0, 0, tiled=True)]
    ppermute x3, waiting for transfers between devices: 19.9 us -> 13.4 us  [swap_outer(): return lax.ppermute(block, axes, pairs + [(j, i) for i, j in pairs])]
    pallas_call x3 -> x4, Pallas kernels: 4.2 us -> 9.56 us  [the longest x1 3.1 us: finish(): pl.pallas_call(finish_kernel, out_shape=jax.ShapeDtypeStruct(center, F32)...]
    ppermute x5, starting transfers between devices: 3.37 us -> 7.4 us  [swap_inner(): return lax.ppermute(block, axes, [(i, i ^ 1) for i in range(count)])]
  transfers between devices with their start and end apart: 16 -> 15, of which waited for: 5 -> 3; matrix products, arithmetic and copies ran while one was open for 0% -> 0% of each run, Pallas kernels for 14% -> 10%
where the time goes in v3:
time: 132 us; the launch traced here: 130 us
  starting transfers between devices  61.7 us (47%)
  blocking collectives  26.4 us (20%)
  Pallas kernels  20.8 us (16%)
  waiting for transfers between devices  16.9 us (13%)
  local copies, waits for them, and re-layouts  3.01 us (2%)
  between operations  1.61 us (1%)
    all_to_all x1, starting transfers between devices, on_device(): pieces = lax.all_to_all(pieces, CHIP, 0, 0, tiled=True)  32.4 us
    all_to_all x1, blocking collectives, send(): return lax.all_to_all(given, CHIP, 0, 0, tiled=True)  26.4 us
    ppermute x3, waiting for transfers between devices, swap_outer(): return lax.ppermute(block, axes, pairs + [(j, i) for i, j in pairs])  13.4 us
    ppermute x3, starting transfers between devices, up(): return lax.ppermute(block, axes, [(i, i + 1) for i in range(count - 1)])  9.3 us
    ppermute x3, starting transfers between devices, swap_outer(): return lax.ppermute(block, axes, pairs + [(j, i) for i, j in pairs])  8.73 us
    ppermute x5, starting transfers between devices, swap_inner(): return lax.ppermute(block, axes, [(i, i ^ 1) for i in range(count)])  7.4 us
    pallas_call x1, Pallas kernels, first_slots(): pl.pallas_call(first_kernel, out_shape=shapes(grown, grown, plane, plane)...  4.75 us
    ppermute x3, starting transfers between devices, down(): return lax.ppermute(block, axes, [(i + 1, i) for i in range(count - 1)])  3.88 us
  transfers between devices with their start and end apart: 15, of which 3 were waited for; matrix products, arithmetic and copies ran while one was open for 0% of the time, Pallas kernels for 10%

profile of v3, /device:TPU:1, one launch (start us, length us, event | category | flops | bytes accessed | tf_op | source)
XLA Modules:
  0.0 130.4 jit_solution(2765174583303145820)
XLA Ops:
  0.6 0.0 copy-start
  0.6 0.0 copy-start.1
  0.7 1.7 %copy-done.1 = f32[2,512,512]{2,1,0:T(8,128)S(1)} copy-done((f32[2,512,512]{2,1,0:T(8,128)S(1)}, f32[2,512,512]{2,1,0:T(8,128)}, u32[]{:S(2)}) %copy-start.1) | copy-done | bytes 2097176
  2.4 0.3 cut.1
  2.6 1.5 %collective-permute-start.2 = (f32[2,512,128]{2,1,0:T(8,128)S(1)}, f32[2,512,128]{2,1,0:T(8,128)S(1)}, u32[]{:S(2)}, u32[]{:S(2)}) collective-permute-start(f32[2,512,128]{2,1,0:T(8,128)S(1)} %get-tuple-element.36), channel_id=1, source_target_pairs={{0,1},{1,0},{2,3},{3,2},{4,5},{5,4},{6,7},{7,6},{8,9},{9,8},{10,11... | collective-permute-start | bytes 1572872 | tf_op jit(solution)/shard_map/ppermute | solution.py:635
  4.1 3.5 %collective-permute-start.3 = (f32[2,512,128]{2,1,0:T(8,128)S(1)}, f32[2,512,128]{2,1,0:T(8,128)S(1)}, u32[]{:S(2)}, u32[]{:S(2)}) collective-permute-start(f32[2,512,128]{2,1,0:T(8,128)S(1)} %get-tuple-element.37), channel_id=1, source_target_pairs={{1,2},{3,4},{5,6},{2,1},{4,3},{6,5},{9,10},{11,12},{13,14},{10,9},... | collective-permute-start | bytes 1572872 | tf_op jit(solution)/shard_map/ppermute | solution.py:641
  7.7 3.2 %collective-permute-start = (f32[2,128,512]{2,1,0:T(8,128)S(1)}, f32[2,128,512]{2,1,0:T(8,128)S(1)}, u32[]{:S(2)}, u32[]{:S(2)}) collective-permute-start(f32[2,128,512]{2,1,0:T(8,128)S(1)} %get-tuple-element.34), channel_id=1, source_target_pairs={{0,8},{8,16},{16,24},{24,32},{32,40},{40,48},{48,56},{56,64},{64,7... | collective-permute-start | bytes 1572872 | tf_op jit(solution)/shard_map/ppermute | solution.py:625
  10.9 1.3 collective-permute-start.1
  12.9 0.0 copy-done
  12.9 0.0 copy-start.3
  12.9 1.2 copy-done.3
  14.1 2.5 %prepare.1 = (f32[8,256,256]{2,1,0:T(8,128)S(1)}, f32[2,4,256,256]{3,2,1,0:T(8,128)S(1)}) custom-call(f32[8,256,256]{2,1,0:T(8,128)S(1)} %copy-done, bf16[2,4,256,256]{3,2,1,0:T(8,128)(2,1)S(1)} %copy-done.3), custom_call_target="tpu_custom_call" | custom-call | flops 805306368 | bytes 9437184 | tf_op jit(solution)/shard_map/prepare/pallas_call | solution.py:391
  16.7 0.0 collective-permute-done.2.inner
  16.7 0.0 collective-permute-done.3.outer
  16.8 4.0 %collective-permute-start.4 = (f32[2,128,256]{2,1,0:T(8,128)S(1)}, f32[2,128,256]{2,1,0:T(8,128)S(1)}, u32[]{:S(2)}, u32[]{:S(2)}) collective-permute-start(f32[2,128,256]{2,1,0:T(8,128)S(1)} %pad_maximum_fusion), channel_id=1, source_target_pairs={{0,8},{8,16},{16,24},{24,32},{32,40},{40,48},{48,56},{56,64},{64,7... | collective-permute-start | bytes 786440 | tf_op jit(solution)/shard_map/ppermute | solution.py:625
  20.8 1.3 collective-permute-start.5
  22.1 0.0 copy-done.2
  22.1 4.8 %slots_first.1 = (f32[2,6,768,128]{3,2,1,0:T(8,128)S(1)}, f32[2,6,768,128]{3,2,1,0:T(8,128)S(1)}, f32[4,256,256]{2,1,0:T(8,128)S(1)}, f32[4,256,256]{2,1,0:T(8,128)S(1)}) custom-call(s32[2,8]{1,0:T(2,128)S(1)} %copy-done.5, s32[1,1]{1,0:T(1,128)S(6)} %copy.16.counts, f32[2,512,512]{2,1,0:T(8,128)S(1)} %copy-done.2, ...), custom_call_target="tpu_custom_call" | custom-call | flops 4294967296 | bytes 31457280 | tf_op jit(solution)/shard_map/slots_first/pallas_call | solution.py:334
  26.9 0.0 collective-permute-done.above
  26.9 0.0 collective-permute-done.1.below
  26.9 0.0 collective-permute-done.4.corner_above
  26.9 3.2 %collective-permute-done.5.corner_below = f32[2,128,256]{2,1,0:T(8,128)S(1)} collective-permute-done((f32[2,128,256]{2,1,0:T(8,128)S(1)}, f32[2,128,256]{2,1,0:T(8,128)S(1)}, u32[]{:S(2)}, u32[]{:S(2)}) %collective-permute-start.5) | collective-permute-done | bytes 262176 | tf_op jit(solution)/shard_map/ppermute | solution.py:630
  30.1 2.4 %slots_second.1 = (f32[2,6,768,128]{3,2,1,0:T(8,128)S(1)}, f32[4,256,256]{2,1,0:T(8,128)S(1)}, f32[4,256,256]{2,1,0:T(8,128)S(1)}, f32[2,256,128]{2,1,0:T(8,128)S(1)}, f32[2,256,128]{2,1,0:T(8,128)S(1)}) custom-call(s32[2,8]{1,0:T(2,128)S(1)} %copy-done.5, s32[1,1]{1,0:T(1,128)S(6)} %copy.16.counts, ...), custom_call_target="tpu_custom_call", output_to_operand_aliasing={{0}: (7, {}), {1}: (8, {}), {2}: (9, {})} | custom-call | flops 4294967296 | bytes 31457280 | tf_op jit(solution)/shard_map/slots_second/pallas_call | solution.py:350
  32.5 0.1 collective-permute-start.6
  32.6 2.4 %stash.1.grown = f32[2,11520,768]{2,1,0:T(8,128)} custom-call(f32[2,6,768,128]{3,2,1,0:T(8,128)S(1)} %get-tuple-element.45.totals), custom_call_target="tpu_custom_call" | custom-call | bytes 9437184 | tf_op jit(solution)/shard_map/stash/pallas_call | solution.py:466
  34.9 0.3 collective-permute-done.6.received
  35.2 1.0 pair_sum.1
  36.2 32.4 %all-to-all-start.1 = ((f32[64,16,256]{2,1,0:T(8,128)}), f32[64,16,256]{2,1,0:T(8,128)S(1)}, u32[]{:S(2)}, u32[]{:S(2)}) async-start(f32[64,16,256]{2,1,0:T(8,128)} %bitcast.2), calls=%async_computation.1 | async-start | bytes 2097152 | tf_op jit(solution)/shard_map/all_to_all | solution.py:686
  68.6 0.6 collective-permute-start.7
  69.3 3.1 %collective-permute-start.8 = (f32[2,256,128]{2,1,0:T(8,128)S(1)}, f32[2,256,128]{2,1,0:T(8,128)S(1)}, u32[]{:S(2)}, u32[]{:S(2)}) collective-permute-start(f32[2,256,128]{2,1,0:T(8,128)S(1)} %get-tuple-element.50), channel_id=1, source_target_pairs={{1,2},{3,4},{5,6},{2,1},{4,3},{6,5},{9,10},{11,12},{13,14},{10,9},... | collective-permute-start | bytes 786440 | tf_op jit(solution)/shard_map/ppermute | solution.py:641
  72.4 0.0 collective-permute-done.7.inner_in
  72.4 13.4 %collective-permute-done.8.outer_in = f32[2,256,128]{2,1,0:T(8,128)S(1)} collective-permute-done((f32[2,256,128]{2,1,0:T(8,128)S(1)}, f32[2,256,128]{2,1,0:T(8,128)S(1)}, u32[]{:S(2)}, u32[]{:S(2)}) %collective-permute-start.8) | collective-permute-done | bytes 262176 | tf_op jit(solution)/shard_map/ppermute | solution.py:641
  85.8 0.0 all-to-all-done.1.pieces_in
  85.8 3.1 %turn.1 = (f32[64,16,256]{2,1,0:T(8,128)}, f32[2,128,512]{2,1,0:T(8,128)S(1)}, f32[2,128,512]{2,1,0:T(8,128)S(1)}, f32[2,512,128]{2,1,0:T(8,128)}, f32[2,512,128]{2,1,0:T(8,128)}) custom-call(f32[64,16,256]{2,1,0:T(8,128)S(1)} %all-to-all-done.1.pieces_in, f32[2,11520,768]{2,1,0:T(8,128)} %stash.1.grown, f32[2,256,128]{2,1,0:T(8,128)S(1)} %collective-permute-done.7.inner_in, ...), custom_call_target="tpu_custom_call" | custom-call | flops 600000 | bytes 7340032 | tf_op jit(solution)/shard_map/turn/pallas_call | solution.py:549
  88.8 2.4 %collective-permute-start.9 = (f32[2,512,128]{2,1,0:T(8,128)}, f32[2,512,128]{2,1,0:T(8,128)S(1)}, u32[]{:S(2)}, u32[]{:S(2)}) collective-permute-start(f32[2,512,128]{2,1,0:T(8,128)} %get-tuple-element.52), channel_id=1, source_target_pairs={{0,1},{1,0},{2,3},{3,2},{4,5},{5,4},{6,7},{7,6},{8,9},{9,8},{10,11... | collective-permute-start | bytes 1572872 | tf_op jit(solution)/shard_map/ppermute | solution.py:635
  91.3 2.1 %collective-permute-start.10 = (f32[2,512,128]{2,1,0:T(8,128)}, f32[2,512,128]{2,1,0:T(8,128)S(1)}, u32[]{:S(2)}, u32[]{:S(2)}) collective-permute-start(f32[2,512,128]{2,1,0:T(8,128)} %get-tuple-element.53), channel_id=1, source_target_pairs={{1,2},{3,4},{5,6},{2,1},{4,3},{6,5},{9,10},{11,12},{13,14},{10,9},... | collective-permute-start | bytes 1572872 | tf_op jit(solution)/shard_map/ppermute | solution.py:641
  93.4 2.1 %collective-permute-start.11 = (f32[2,128,512]{2,1,0:T(8,128)S(1)}, f32[2,128,512]{2,1,0:T(8,128)S(1)}, u32[]{:S(2)}, u32[]{:S(2)}) collective-permute-start(f32[2,128,512]{2,1,0:T(8,128)S(1)} %get-tuple-element.54), channel_id=1, source_target_pairs={{0,8},{8,16},{16,24},{24,32},{32,40},{40,48},{48,56},{56,64},{64,7... | collective-permute-start | bytes 1572872 | tf_op jit(solution)/shard_map/ppermute | solution.py:625
  95.5 1.3 collective-permute-start.12
  96.8 26.4 %conditional.1 = (f32[4,256,256]{2,1,0:T(8,128)}) conditional(s32[]{:T(128)} %bitcast.1, () %tuple.19, f32[64,16,256]{2,1,0:T(8,128)} %get-tuple-element.51), branch_computations={%region_0.0_spmd, %region_1.0_spmd} | conditional | bytes 2097160 | solution.py:648
  96.8 26.4 %all_to_all.9 = f32[64,16,256]{2,1,0:T(8,128)} all-to-all(f32[64,16,256]{2,1,0:T(8,128)} %param.1), channel_id=1, replica_groups=mesh['x'=4,'y'=4,'z'=4,'core'=2] {'x','y','z'}, dimensions={0} | all-to-all | bytes 2097152 | tf_op jit(solution)/shard_map/cond/branch_1_fun/all_to_all | solution.py:646
  123.2 0.0 collective-permute-done.9.inner_in
  123.2 0.0 collective-permute-done.10.outer_in
  123.2 0.0 collective-permute-done.11.above_in
  123.2 0.0 collective-permute-done.12.below_in
  123.2 2.7 %collective-permute-start.13 = (f32[4,256,256]{2,1,0:T(8,128)}, f32[4,256,256]{2,1,0:T(8,128)S(1)}, u32[]{:S(2)}, u32[]{:S(2)}) collective-permute-start(f32[4,256,256]{2,1,0:T(8,128)} %get-tuple-element.65.own), channel_id=1, source_target_pairs={{0,1},{1,0},{2,3},{3,2},{4,5},{5,4},{6,7},{7,6},{8,9},{9,8},{10,11... | collective-permute-start | bytes 3145736 | tf_op jit(solution)/shard_map/ppermute | solution.py:635
  125.9 3.1 %finish.1 = f32[2,512,512]{2,1,0:T(8,128)} custom-call(f32[2,11520,768]{2,1,0:T(8,128)} %stash.1.grown, f32[2,512,128]{2,1,0:T(8,128)S(1)} %collective-permute-done.9.inner_in, f32[2,512,128]{2,1,0:T(8,128)S(1)} %collective-permute-done.10.outer_in, f32[2,128,512]{2,1,0:T(8,128)S(1)} %collective-permute-done.11.above_in, ...), custom_call_target="tpu_custom_call" | custom-call | flops 600000 | bytes 7340032 | tf_op jit(solution)/shard_map/finish/pallas_call | solution.py:590
  129.1 0.0 collective-permute-done.13.other
  129.1 1.3 %join.1 = f32[2,4,256,256]{3,2,1,0:T(8,128)} custom-call(f32[4,256,256]{2,1,0:T(8,128)S(1)} %copy-done.6, f32[4,256,256]{2,1,0:T(8,128)S(1)} %collective-permute-done.13.other), custom_call_target="tpu_custom_call" | custom-call | bytes 4194304 | tf_op jit(solution)/shard_map/join/pallas_call | solution.py:611
  (11 shorter events, 0.1 us)
Async XLA Ops:
  0.6 12.2 %copy-start = (f32[8,256,256]{2,1,0:T(8,128)S(1)}, f32[8,256,256]{2,1,0:T(8,128)}, u32[]{:S(2)}) copy-start(f32[8,256,256]{2,1,0:T(8,128)} %patterns.1) | copy-start | bytes 6291460
  0.6 1.7 %copy-start.1 = (f32[2,512,512]{2,1,0:T(8,128)S(1)}, f32[2,512,512]{2,1,0:T(8,128)}, u32[]{:S(2)}) copy-start(f32[2,512,512]{2,1,0:T(8,128)} %tile.3) | copy-start | bytes 6291460
  2.6 14.0 %collective-permute-start.2 = (f32[2,512,128]{2,1,0:T(8,128)S(1)}, f32[2,512,128]{2,1,0:T(8,128)S(1)}, u32[]{:S(2)}, u32[]{:S(2)}) collective-permute-start(f32[2,512,128]{2,1,0:T(8,128)S(1)} %get-tuple-element.36), channel_id=1, source_target_pairs={{0,1},{1,0},{2,3},{3,2},{4,5},{5,4},{6,7},{7,6},{8,9},{9,8},{10,11... | collective-permute-start | bytes 1572872 | tf_op jit(solution)/shard_map/ppermute | solution.py:635
  4.1 12.6 %collective-permute-start.3 = (f32[2,512,128]{2,1,0:T(8,128)S(1)}, f32[2,512,128]{2,1,0:T(8,128)S(1)}, u32[]{:S(2)}, u32[]{:S(2)}) collective-permute-start(f32[2,512,128]{2,1,0:T(8,128)S(1)} %get-tuple-element.37), channel_id=1, source_target_pairs={{1,2},{3,4},{5,6},{2,1},{4,3},{6,5},{9,10},{11,12},{13,14},{10,9},... | collective-permute-start | bytes 1572872 | tf_op jit(solution)/shard_map/ppermute | solution.py:641
  7.7 19.2 %collective-permute-start = (f32[2,128,512]{2,1,0:T(8,128)S(1)}, f32[2,128,512]{2,1,0:T(8,128)S(1)}, u32[]{:S(2)}, u32[]{:S(2)}) collective-permute-start(f32[2,128,512]{2,1,0:T(8,128)S(1)} %get-tuple-element.34), channel_id=1, source_target_pairs={{0,8},{8,16},{16,24},{24,32},{32,40},{40,48},{48,56},{56,64},{64,7... | collective-permute-start | bytes 1572872 | tf_op jit(solution)/shard_map/ppermute | solution.py:625
  10.9 16.0 %collective-permute-start.1 = (f32[2,128,512]{2,1,0:T(8,128)S(1)}, f32[2,128,512]{2,1,0:T(8,128)S(1)}, u32[]{:S(2)}, u32[]{:S(2)}) collective-permute-start(f32[2,128,512]{2,1,0:T(8,128)S(1)} %get-tuple-element.35), channel_id=1, source_target_pairs={{8,0},{16,8},{24,16},{32,24},{40,32},{48,40},{56,48},{64,56},{72,6... | collective-permute-start | bytes 1572872 | tf_op jit(solution)/shard_map/ppermute | solution.py:630
  12.9 1.2 copy-start.3
  14.1 8.0 %copy-start.2 = (f32[2,512,512]{2,1,0:T(8,128)S(1)}, f32[2,512,512]{2,1,0:T(8,128)}, u32[]{:S(2)}) copy-start(f32[2,512,512]{2,1,0:T(8,128)} %tile.3) | copy-start | bytes 6291460
  14.1 8.0 %copy-start.4 = (bf16[4,256,256]{2,1,0:T(8,128)(2,1)S(1)}, bf16[4,256,256]{2,1,0:T(8,128)(2,1)}, u32[]{:S(2)}) copy-start(bf16[4,256,256]{2,1,0:T(8,128)(2,1)} %constant.7.clone.table) | copy-start | bytes 1572868
  14.1 8.0 %copy-start.5 = (s32[2,8]{1,0:T(2,128)S(1)}, s32[2,8]{1,0:T(2,128)}, u32[]{:S(2)}) copy-start(s32[2,8]{1,0:T(2,128)} %offsets.3) | copy-start | bytes 196
  16.8 10.1 %collective-permute-start.4 = (f32[2,128,256]{2,1,0:T(8,128)S(1)}, f32[2,128,256]{2,1,0:T(8,128)S(1)}, u32[]{:S(2)}, u32[]{:S(2)}) collective-permute-start(f32[2,128,256]{2,1,0:T(8,128)S(1)} %pad_maximum_fusion), channel_id=1, source_target_pairs={{0,8},{8,16},{16,24},{24,32},{32,40},{40,48},{48,56},{56,64},{64,7... | collective-permute-start | bytes 786440 | tf_op jit(solution)/shard_map/ppermute | solution.py:625
  20.8 9.3 %collective-permute-start.5 = (f32[2,128,256]{2,1,0:T(8,128)S(1)}, f32[2,128,256]{2,1,0:T(8,128)S(1)}, u32[]{:S(2)}, u32[]{:S(2)}) collective-permute-start(f32[2,128,256]{2,1,0:T(8,128)S(1)} %pad_maximum_fusion.1), channel_id=1, source_target_pairs={{8,0},{16,8},{24,16},{32,24},{40,32},{48,40},{56,48},{64,56},{72,6... | collective-permute-start | bytes 786440 | tf_op jit(solution)/shard_map/ppermute | solution.py:630
  32.5 2.7 %collective-permute-start.6 = (f32[4,256,256]{2,1,0:T(8,128)S(1)}, f32[4,256,256]{2,1,0:T(8,128)S(1)}, u32[]{:S(2)}, u32[]{:S(2)}) collective-permute-start(f32[4,256,256]{2,1,0:T(8,128)S(1)} %get-tuple-element.44), channel_id=1, source_target_pairs={{0,1},{1,0},{2,3},{3,2},{4,5},{5,4},{6,7},{7,6},{8,9},{9,8},{10,11... | collective-permute-start | bytes 3145736 | tf_op jit(solution)/shard_map/ppermute | solution.py:635
  36.2 49.5 %all-to-all-start.1 = ((f32[64,16,256]{2,1,0:T(8,128)}), f32[64,16,256]{2,1,0:T(8,128)S(1)}, u32[]{:S(2)}, u32[]{:S(2)}) async-start(f32[64,16,256]{2,1,0:T(8,128)} %bitcast.2), calls=%async_computation.1 | async-start | bytes 2097152 | tf_op jit(solution)/shard_map/all_to_all | solution.py:686
  68.6 3.8 %collective-permute-start.7 = (f32[2,256,128]{2,1,0:T(8,128)S(1)}, f32[2,256,128]{2,1,0:T(8,128)S(1)}, u32[]{:S(2)}, u32[]{:S(2)}) collective-permute-start(f32[2,256,128]{2,1,0:T(8,128)S(1)} %get-tuple-element.49), channel_id=1, source_target_pairs={{0,1},{1,0},{2,3},{3,2},{4,5},{5,4},{6,7},{7,6},{8,9},{9,8},{10,11... | collective-permute-start | bytes 786440 | tf_op jit(solution)/shard_map/ppermute | solution.py:635
  69.3 16.5 %collective-permute-start.8 = (f32[2,256,128]{2,1,0:T(8,128)S(1)}, f32[2,256,128]{2,1,0:T(8,128)S(1)}, u32[]{:S(2)}, u32[]{:S(2)}) collective-permute-start(f32[2,256,128]{2,1,0:T(8,128)S(1)} %get-tuple-element.50), channel_id=1, source_target_pairs={{1,2},{3,4},{5,6},{2,1},{4,3},{6,5},{9,10},{11,12},{13,14},{10,9},... | collective-permute-start | bytes 786440 | tf_op jit(solution)/shard_map/ppermute | solution.py:641
  88.8 34.3 %collective-permute-start.9 = (f32[2,512,128]{2,1,0:T(8,128)}, f32[2,512,128]{2,1,0:T(8,128)S(1)}, u32[]{:S(2)}, u32[]{:S(2)}) collective-permute-start(f32[2,512,128]{2,1,0:T(8,128)} %get-tuple-element.52), channel_id=1, source_target_pairs={{0,1},{1,0},{2,3},{3,2},{4,5},{5,4},{6,7},{7,6},{8,9},{9,8},{10,11... | collective-permute-start | bytes 1572872 | tf_op jit(solution)/shard_map/ppermute | solution.py:635
  91.3 31.9 %collective-permute-start.10 = (f32[2,512,128]{2,1,0:T(8,128)}, f32[2,512,128]{2,1,0:T(8,128)S(1)}, u32[]{:S(2)}, u32[]{:S(2)}) collective-permute-start(f32[2,512,128]{2,1,0:T(8,128)} %get-tuple-element.53), channel_id=1, source_target_pairs={{1,2},{3,4},{5,6},{2,1},{4,3},{6,5},{9,10},{11,12},{13,14},{10,9},... | collective-permute-start | bytes 1572872 | tf_op jit(solution)/shard_map/ppermute | solution.py:641
  93.4 29.8 %collective-permute-start.11 = (f32[2,128,512]{2,1,0:T(8,128)S(1)}, f32[2,128,512]{2,1,0:T(8,128)S(1)}, u32[]{:S(2)}, u32[]{:S(2)}) collective-permute-start(f32[2,128,512]{2,1,0:T(8,128)S(1)} %get-tuple-element.54), channel_id=1, source_target_pairs={{0,8},{8,16},{16,24},{24,32},{32,40},{40,48},{48,56},{56,64},{64,7... | collective-permute-start | bytes 1572872 | tf_op jit(solution)/shard_map/ppermute | solution.py:625
  95.5 27.7 %collective-permute-start.12 = (f32[2,128,512]{2,1,0:T(8,128)S(1)}, f32[2,128,512]{2,1,0:T(8,128)S(1)}, u32[]{:S(2)}, u32[]{:S(2)}) collective-permute-start(f32[2,128,512]{2,1,0:T(8,128)S(1)} %get-tuple-element.55), channel_id=1, source_target_pairs={{8,0},{16,8},{24,16},{32,24},{40,32},{48,40},{56,48},{64,56},{72,6... | collective-permute-start | bytes 1572872 | tf_op jit(solution)/shard_map/ppermute | solution.py:630
  123.2 5.9 %copy-start.6 = (f32[4,256,256]{2,1,0:T(8,128)S(1)}, f32[4,256,256]{2,1,0:T(8,128)}, u32[]{:S(2)}) copy-start(f32[4,256,256]{2,1,0:T(8,128)} %get-tuple-element.65.own) | copy-start | bytes 3145732
  123.2 5.8 %collective-permute-start.13 = (f32[4,256,256]{2,1,0:T(8,128)}, f32[4,256,256]{2,1,0:T(8,128)S(1)}, u32[]{:S(2)}, u32[]{:S(2)}) collective-permute-start(f32[4,256,256]{2,1,0:T(8,128)} %get-tuple-element.65.own), channel_id=1, source_target_pairs={{0,1},{1,0},{2,3},{3,2},{4,5},{5,4},{6,7},{7,6},{8,9},{9,8},{10,11... | collective-permute-start | bytes 3145736 | tf_op jit(solution)/shard_map/ppermute | solution.py:635

commit v4 on v3

--- a/solution.py
+++ b/solution.py
@@ -42,7 +42,7 @@
 
 
 def one_slot(number, row, col, ext, pat, probe, table, totals, keep, send, work):
-    obj, term, psi, half, field, ratio = work
+    obj, psi, half, field = work
     width = pat.shape[1]
     modes = probe.shape[1]
     mid = width // 2
@@ -77,62 +77,65 @@
                 )
             for side, lanes in enumerate((low, high)):
                 re, im = patch[0][side], patch[1][side]
-                obj[0, span(c), lanes] = re
-                obj[1, span(c), lanes] = im
-
-    def make_psi(k):
-        for c in range(width // CHUNK):
-            waves = []
-            for lanes in (low, high):
-                o_re, o_im = obj[0, span(c), lanes], obj[1, span(c), lanes]
-                p_re = probe[0, k, span(c), lanes]
-                p_im = probe[1, k, span(c), lanes]
-                waves.append((p_re * o_re - p_im * o_im, p_re * o_im + p_im * o_re))
-            for part, lanes in enumerate((low, high)):
-                a, b = waves[0][part], waves[1][part]
-                psi[k, 0, span(c), lanes] = (a + b).astype(BF16)
-                psi[k, 1, span(c), lanes] = (a - b).astype(BF16)
-
-    def right_forward(k):
+                obj[0, span(c), lanes] = jnp.where(turn, re, -im)
+                obj[1, span(c), lanes] = jnp.where(turn, im, re)
+            for k in range(modes):
+                waves = []
+                for side, lanes in enumerate((low, high)):
+                    o_re, o_im = patch[0][side], patch[1][side]
+                    p_re, p_im = probe[0, k, span(c), lanes], probe[1, k, span(c), lanes]
+                    waves.append((p_re * o_re - p_im * o_im, p_re * o_im + p_im * o_re))
+                for part, lanes in enumerate((low, high)):
+                    a, b = waves[0][part], waves[1][part]
+                    psi[k, 0, span(c), lanes] = (a + b).astype(BF16)
+                    psi[k, 1, span(c), lanes] = (a - b).astype(BF16)
+
+    def right_forward_all():
         for parity, lanes in enumerate((low, high)):
-            y = dot(psi[k, parity], table[RIGHT[parity]])
-            top, bottom = y[:mid], y[mid:]
-            total, difference = (top + bottom).astype(BF16), (top - bottom).astype(BF16)
-            half[k, 0, low, lanes] = total[:, :mid]
-            half[k, 0, high, lanes] = total[:, mid:]
-            half[k, 1, low, lanes] = difference[:, :mid]
-            half[k, 1, high, lanes] = difference[:, mid:]
+            whole = dot(psi[:, parity].reshape(modes * width, width), table[RIGHT[parity]])
+            for k in range(modes):
+                right_forward(k, lanes, whole[k * width : (k + 1) * width])
+
+    def right_forward(k, lanes, y):
+        top, bottom = y[:mid], y[mid:]
+        total, difference = (top + bottom).astype(BF16), (top - bottom).astype(BF16)
+        half[k, 0, low, lanes] = total[:, :mid]
+        half[k, 0, high, lanes] = total[:, mid:]
+        half[k, 1, low, lanes] = difference[:, :mid]
+        half[k, 1, high, lanes] = difference[:, mid:]
 
     def left_forward(k):
         for parity in range(2):
             field[k, parity] = dot(table[LEFT[parity]], half[k, parity])
 
-    def make_ratio():
+    def make_all_chi():
         for parity in range(2):
             for c in range(mid // CHUNK):
+                values = [
+                    (field[k, parity, span(c), :], field[k, parity, span(c, mid), :])
+                    for k in range(modes)
+                ]
                 total = None
-                for k in range(modes):
-                    re, im = field[k, parity, span(c), :], field[k, parity, span(c, mid), :]
+                for re, im in values:
                     square = re * re + im * im
                     total = square if total is None else total + square
                 measured = pat[number, span(c, parity * mid), :]
-                ratio[parity, span(c), :] = 1.0 - measured * lax.rsqrt(jnp.maximum(total, 1.0))
-
-    def make_chi(k):
-        for parity in range(2):
-            for c in range(mid // CHUNK):
-                scale = ratio[parity, span(c), :]
-                re = (field[k, parity, span(c), :] * scale).astype(BF16)
-                im = (field[k, parity, span(c, mid), :] * scale).astype(BF16)
+                scale = 1.0 - measured * lax.rsqrt(jnp.maximum(total, 1.0))
                 rows = span(c, parity * mid)
-                psi[k, 0, rows, low] = re[:, :mid]
-                psi[k, 0, rows, high] = im[:, :mid]
-                psi[k, 1, rows, low] = re[:, mid:]
-                psi[k, 1, rows, high] = im[:, mid:]
-
-    def right_backward(k):
-        even = dot(psi[k, 0], table[LEFT[0]])
-        odd = dot(psi[k, 1], table[LEFT[1]])
+                for k, (re, im) in enumerate(values):
+                    re, im = (re * scale).astype(BF16), (im * scale).astype(BF16)
+                    psi[k, 0, rows, low] = re[:, :mid]
+                    psi[k, 0, rows, high] = im[:, :mid]
+                    psi[k, 1, rows, low] = re[:, mid:]
+                    psi[k, 1, rows, high] = im[:, mid:]
+
+    def right_backward_all():
+        evens = dot(psi[:, 0].reshape(modes * width, width), table[LEFT[0]])
+        odds = dot(psi[:, 1].reshape(modes * width, width), table[LEFT[1]])
+        for k in range(modes):
+            right_backward(k, evens[k * width : (k + 1) * width], odds[k * width : (k + 1) * width])
+
+    def right_backward(k, even, odd):
         for value, lanes in (((even + odd).astype(BF16), low), ((even - odd).astype(BF16), high)):
             for parity in range(2):
                 rows = value[parity * mid : parity * mid + mid]
@@ -143,71 +146,39 @@
         for parity in range(2):
             field[k, parity] = dot(table[RIGHT[parity]], half[k, parity])
 
-    def collect(k):
+    def collect_all():
         for c in range(mid // CHUNK):
-            even_re, odd_re = field[k, 0, span(c), :], field[k, 1, span(c), :]
-            even_im, odd_im = field[k, 0, span(c, mid), :], field[k, 1, span(c, mid), :]
-            for rows, re, im in (
-                (span(c), even_re + odd_re, even_im + odd_im),
-                (span(c, mid), even_re - odd_re, even_im - odd_im),
-            ):
-                p_re, p_im = probe[0, k, rows, :], probe[1, k, rows, :]
-                add_re = p_re * re + p_im * im
-                add_im = p_re * im - p_im * re
-                if k == 0:
-                    term[0, rows, :] = add_re
-                    term[1, rows, :] = add_im
-                else:
-                    term[0, rows, :] += add_re
-                    term[1, rows, :] += add_im
+            for top in range(2):
+                rows = span(c, top * mid)
+                target = pl.ds(row + top * mid + c * CHUNK, CHUNK)
                 o_re, o_im = obj[0, rows, :], obj[1, rows, :]
-                keep[k, rows, :] += o_re * re + o_im * im
-                send[k, rows, :] += o_re * im - o_im * re
-
-    def turn_patch():
-        for c in range(width // CHUNK):
-            for lanes in (low, high):
-                re, im = obj[0, span(c), lanes], obj[1, span(c), lanes]
-                obj[0, span(c), lanes] = jnp.where(turn, re, -im)
-                obj[1, span(c), lanes] = jnp.where(turn, im, re)
-
-    def add_term():
-        for c in range(width // CHUNK):
-            target = pl.ds(row + c * CHUNK, CHUNK)
-            for p in range(2):
-                first = pltpu.roll(term[p, span(c), low], shift, 1)
-                second = pltpu.roll(term[p, span(c), high], shift, 1)
-                totals[p, block, target, :] += jnp.where(at_or_after, first, 0.0)
-                totals[p, block + 1, target, :] += jnp.where(at_or_after, second, first)
-                totals[p, block + 2, target, :] += jnp.where(at_or_after, 0.0, second)
+                sums = [None, None]
+                for k in range(modes):
+                    even_re, odd_re = field[k, 0, span(c), :], field[k, 1, span(c), :]
+                    even_im, odd_im = field[k, 0, span(c, mid), :], field[k, 1, span(c, mid), :]
+                    re = even_re - odd_re if top else even_re + odd_re
+                    im = even_im - odd_im if top else even_im + odd_im
+                    p_re, p_im = probe[0, k, rows, :], probe[1, k, rows, :]
+                    adds = (p_re * re + p_im * im, p_re * im - p_im * re)
+                    sums = [x if k == 0 else t + x for t, x in zip(sums, adds)]
+                    keep[k, rows, :] += o_re * re + o_im * im
+                    send[k, rows, :] += o_re * im - o_im * re
+                for p in range(2):
+                    first = pltpu.roll(sums[p][:, :LANES], shift, 1)
+                    second = pltpu.roll(sums[p][:, LANES:], shift, 1)
+                    totals[p, block, target, :] += jnp.where(at_or_after, first, 0.0)
+                    totals[p, block + 1, target, :] += jnp.where(at_or_after, second, first)
+                    totals[p, block + 2, target, :] += jnp.where(at_or_after, 0.0, second)
 
     gather_patch()
-    make_psi(0)
-    make_psi(1)
+    right_forward_all()
     for k in range(modes):
-        right_forward(k)
-        if k + 2 < modes:
-            make_psi(k + 2)
-        if k == modes - 2:
-            turn_patch()
-        if k >= 1:
-            left_forward(k - 1)
-    left_forward(modes - 1)
-    make_ratio()
-    make_chi(0)
-    make_chi(1)
+        left_forward(k)
+    make_all_chi()
+    right_backward_all()
     for k in range(modes):
-        right_backward(k)
-        if k + 2 < modes:
-            make_chi(k + 2)
-        if k >= 1:
-            left_backward(k - 1)
-        if k >= 2:
-            collect(k - 2)
-    left_backward(modes - 1)
-    collect(modes - 2)
-    collect(modes - 1)
-    add_term()
+        left_backward(k)
+    collect_all()
 
 
 class Moves:
@@ -247,7 +218,7 @@
 
 def first_kernel(
     offsets, counts, tile, inner, outer, pat, probe, table,
-    ext, totals, keep, send, obj, term, psi, half, field, ratio, sems,
+    ext, totals, keep, send, obj, psi, half, field, sems,
 ):
     rows, cols = tile.shape[1:]
     margin = inner.shape[2]
@@ -263,15 +234,15 @@
     keep[...] = jnp.zeros_like(keep)
     send[...] = jnp.zeros_like(send)
     moves.wait()
-    work = (obj, term, psi, half, field, ratio)
+    work = (obj, psi, half, field)
     visit_all(False, offsets, counts, rows, cols, ext, pat, probe, table, totals, keep, send, work)
 
 
 def second_kernel(
     offsets, counts, above, below, corner_above, corner_below, ext_in, totals_in, keep_in,
     send_in, pat, probe, table,
-    totals, keep, send, inner_ends, outer_ends,
-    ext, obj, term, psi, half, field, ratio, sems,
+    totals, keep, send, inner_out, outer_out,
+    ext, obj, psi, half, field, sems,
 ):
     margin, cols = above.shape[1:]
     last = ext.shape[1] - 1
@@ -293,23 +264,20 @@
     keep[...] = keep_in[...]
     send[...] = send_in[...]
     moves.wait()
-    work = (obj, term, psi, half, field, ratio)
+    work = (obj, psi, half, field)
     visit_all(True, offsets, counts, rows, cols, ext, pat, probe, table, totals, keep, send, work)
     moves = Moves(sems)
-    for ends, j in ((outer_ends, outer_block), (inner_ends, inner_block)):
-        moves.begin(totals.at[:, j, top, :], ends.at[:, pl.ds(0, margin), :])
-        moves.begin(totals.at[:, j, bottom, :], ends.at[:, pl.ds(margin, margin), :])
+    moves.begin(totals.at[:, outer_block], outer_out)
+    moves.begin(totals.at[:, inner_block], inner_out)
     moves.wait()
 
 
 def slot_scratch(modes, width):
     return [
-        pltpu.VMEM((2, width, width), F32),
         pltpu.VMEM((2, width, width), F32),
         pltpu.VMEM((modes, 2, width, width), BF16),
         pltpu.VMEM((modes, 2, width, width), BF16),
         pltpu.VMEM((modes, 2, width, width), F32),
-        pltpu.VMEM((2, width // 2, width), F32),
         pltpu.SemaphoreType.DMA((16,)),
     ]
 
@@ -346,10 +314,10 @@
 def second_slots(offsets, counts, sides, ext, totals, keep, send, patterns, probe, table):
     modes, width = probe.shape[1:3]
     margin = sides[0].shape[1]
-    ends = (2, 2 * margin, LANES)
+    side = (2, ext.shape[2], LANES)
     return pl.pallas_call(
         second_kernel,
-        out_shape=shapes(totals.shape, keep.shape, send.shape, ends, ends),
+        out_shape=shapes(totals.shape, keep.shape, send.shape, side, side),
         in_specs=[SMEM] * 2 + [FREE] * 5 + [VMEM] * 6,
         out_specs=[VMEM] * 3 + [FREE] * 2,
         scratch_shapes=[pltpu.VMEM(ext.shape, F32)] + slot_scratch(modes, width),
@@ -372,7 +340,7 @@
     def one(number, carry):
         value = patterns[number]
         total = None
-        for _ in range(3):
+        for _ in range(2):
             part = value.astype(BF16)
             value = value - part.astype(F32)
             moved = dot(part, pick)
@@ -497,32 +465,22 @@
 
 
 def turn_kernel(
-    pieces_in, grown, inner_in, outer_in,
-    copies_out, top_out, bottom_out, inner_out, outer_out,
-    pieces, top, bottom, inner, outer, inner_side, outer_side, sems, out_sems,
+    pieces_in, grown, inner_in, outer_in, copies_out, top_out, bottom_out,
+    pieces, top, bottom, inner, outer, sems, out_sems,
 ):
-    margin = top.shape[1]
-    rows = inner_side.shape[1]
-    cols = top.shape[2]
-    core = lax.axis_index(CORE)
+    margin, cols = top.shape[1:]
+    rows = inner_in.shape[1] - 2 * margin
+    low, high = pl.ds(0, margin), pl.ds(margin + rows, margin)
     center = pl.ds(LANES, cols)
-    middle = pl.ds(margin, rows)
-
-    def column(j):
-        return pl.ds(pl.multiple_of(j * (cols + LANES), LANES), LANES)
-
     first = Moves(sems)
     first.begin(pieces_in, pieces)
-    first.begin(inner_in, inner)
-    first.begin(outer_in, outer)
-    first.begin(grown.at[:, pl.ds(0, margin), center], top)
-    first.begin(grown.at[:, pl.ds(margin + rows, margin), center], bottom)
-    first.begin(grown.at[:, middle, column(1 - core)], inner_side)
-    first.begin(grown.at[:, middle, column(core)], outer_side)
+    for side_in, side in ((inner_in, inner), (outer_in, outer)):
+        first.begin(side_in.at[:, low, :], side.at[:, low, :])
+        first.begin(side_in.at[:, high, :], side.at[:, pl.ds(margin, margin), :])
+    first.begin(grown.at[:, low, center], top)
+    first.begin(grown.at[:, high, center], bottom)
     first.wait()
     last = Moves(out_sems)
-    last.begin(inner_side, inner_out)
-    last.begin(outer_side, outer_out)
 
     def add(side, start):
         lanes = pl.ds(start, LANES)
@@ -542,17 +500,15 @@
 
 
 def turn(pieces, grown, inner, outer):
-    margin = inner.shape[1] // 2
-    rows, cols = grown.shape[1] // SPARE - 2 * margin, grown.shape[2] - 2 * LANES
-    strip, side = (2, margin, cols), (2, rows, LANES)
-    made = [pieces.shape, strip, strip, inner.shape, outer.shape, side, side]
+    margin = inner.shape[2]
+    strip, ends = (2, margin, grown.shape[2] - 2 * LANES), (2, 2 * margin, margin)
     return pl.pallas_call(
         turn_kernel,
-        out_shape=shapes(pieces.shape, strip, strip, side, side),
+        out_shape=shapes(pieces.shape, strip, strip),
         in_specs=[FREE] * 4,
-        out_specs=[FREE] * 5,
-        scratch_shapes=[pltpu.VMEM(x, F32) for x in made]
-        + [pltpu.SemaphoreType.DMA((7,)), pltpu.SemaphoreType.DMA((5,))],
+        out_specs=[FREE] * 3,
+        scratch_shapes=[pltpu.VMEM(x, F32) for x in (pieces.shape, strip, strip, ends, ends)]
+        + [pltpu.SemaphoreType.DMA((7,)), pltpu.SemaphoreType.DMA((3,))],
         compiler_params=pltpu.CompilerParams(vmem_limit_bytes=8 * MIB),
         cost_estimate=pl.CostEstimate(flops=600_000, bytes_accessed=7 * MIB, transcendentals=0),
         name="turn",
@@ -565,9 +521,10 @@
 ):
     margin = above.shape[1]
     rows, cols = center.shape[1:]
-    middle = grown.at[:, pl.ds(margin, rows), pl.ds(LANES, cols)]
+    middle = pl.ds(margin, rows)
+    core_part = grown.at[:, middle, pl.ds(LANES, cols)]
     load(
-        (middle, inner_in, outer_in, above_in, below_in),
+        (core_part, inner_in.at[:, middle], outer_in.at[:, middle], above_in, below_in),
         (center, inner, outer, above, below),
         sems,
     )
@@ -585,8 +542,9 @@
 
 
 def finish(grown, inner, outer, above, below):
-    center = (2, inner.shape[1], above.shape[2])
-    made = (center, inner.shape, outer.shape, above.shape, below.shape)
+    center = (2, inner.shape[1] - 2 * above.shape[1], above.shape[2])
+    side = (2, center[1], LANES)
+    made = (center, side, side, above.shape, below.shape)
     return pl.pallas_call(
         finish_kernel,
         out_shape=jax.ShapeDtypeStruct(center, F32),
@@ -673,28 +631,24 @@
         offsets, counts, object_field, inner, outer, measured, wide, table
     )
     sides = (from_above, from_below, corner_above, corner_below)
-    totals, keep, send, inner_ends, outer_ends = second_slots(
+    totals, keep, send, inner, outer = second_slots(
         offsets, counts, sides, ext, totals, keep, send, measured, wide, table
     )
 
     received = swap_inner(send, COL)
+    outer = swap_outer(outer, COL)
+    inner = swap_inner(inner, COL)
     grown = stash(totals)
     received, grown = lax.optimization_barrier((received, grown))
     pair = pair_sum(keep, received)
     chips = lax.axis_size(CHIP)
-    pieces = pair.reshape(chips, modes * width // chips, width)
-    pieces = lax.all_to_all(pieces, CHIP, 0, 0, tiled=True)
-    outer_ends = swap_outer(outer_ends, COL)
-    inner_ends = swap_inner(inner_ends, COL)
-    copies, top, bottom, inner, outer = turn(pieces, grown, inner_ends, outer_ends)
+    pieces = exchange(counts, pair.reshape(chips, modes * width // chips, width))
+    pieces, inner, outer = lax.optimization_barrier((pieces, inner, outer))
+    copies, top, bottom = turn(pieces, grown, inner, outer)
     from_above = up(bottom, ROW)
     from_below = down(top, ROW)
-    outer = swap_outer(outer, COL)
-    inner = swap_inner(inner, COL)
     gathered = exchange(counts, copies).reshape(modes, width, width)
-    gathered, inner, outer, from_above, from_below = lax.optimization_barrier(
-        (gathered, inner, outer, from_above, from_below)
-    )
+    gathered, from_above, from_below = lax.optimization_barrier((gathered, from_above, from_below))
     other = swap_inner(gathered, COL)
     object_grad = finish(grown, inner, outer, from_above, from_below)
     return (object_grad, join(gathered, other))

time: 132 us -> 132 us (level)
  the two profiles are of different devices: /device:TPU:1 before, /device:TPU:29 now
where the time goes in v4:
time: 132 us; the launch traced here: 130 us
  blocking collectives  68 us (52%)
  Pallas kernels  28.9 us (22%)
  starting transfers between devices  27.8 us (21%)
  local copies, waits for them, and re-layouts  3.01 us (2%)
  between operations  1.58 us (1%)
    all_to_all x2, blocking collectives, send(): return lax.all_to_all(given, CHIP, 0, 0, tiled=True)  68 us
    ppermute x3, starting transfers between devices, up(): return lax.ppermute(block, axes, [(i, i + 1) for i in range(count - 1)])  11.5 us
    pallas_call x1, Pallas kernels, second_slots(): pl.pallas_call(second_kernel, out_shape=shapes(totals.shape, keep.shape,...  8.13 us
    pallas_call x1, Pallas kernels, first_slots(): pl.pallas_call(first_kernel, out_shape=shapes(grown, grown, plane, plane)...  7.58 us
    ppermute x3, starting transfers between devices, down(): return lax.ppermute(block, axes, [(i + 1, i) for i in range(count - 1)])  6.64 us
    ppermute x2, starting transfers between devices, swap_outer(): return lax.ppermute(block, axes, pairs + [(j, i) for i, j in pairs])  5.91 us
    ppermute x4, starting transfers between devices, swap_inner(): return lax.ppermute(block, axes, [(i, i ^ 1) for i in range(count)])  3.69 us
    pallas_call x1, Pallas kernels, finish(): pl.pallas_call(finish_kernel, out_shape=jax.ShapeDtypeStruct(center, F32)...  3.1 us
  transfers between devices with their start and end apart: 12, of which 1 were waited for; matrix products, arithmetic and copies ran while one was open for 0% of the time, Pallas kernels for 12%

profile of v4, /device:TPU:29, one launch (start us, length us, event | category | flops | bytes accessed | tf_op | source)
XLA Modules:
  0.0 130.5 jit_solution(7683457898876407456)
XLA Ops:
  0.6 0.0 copy-start
  0.6 0.0 copy-start.1
  0.7 1.7 %copy-done.1 = f32[2,512,512]{2,1,0:T(8,128)S(1)} copy-done((f32[2,512,512]{2,1,0:T(8,128)S(1)}, f32[2,512,512]{2,1,0:T(8,128)}, u32[]{:S(2)}) %copy-start.1) | copy-done | bytes 2097176
  2.4 0.3 cut.1
  2.6 0.8 collective-permute-start.2
  3.4 3.4 %collective-permute-start.3 = (f32[2,512,128]{2,1,0:T(8,128)S(1)}, f32[2,512,128]{2,1,0:T(8,128)S(1)}, u32[]{:S(2)}, u32[]{:S(2)}) collective-permute-start(f32[2,512,128]{2,1,0:T(8,128)S(1)} %get-tuple-element.41), channel_id=1, source_target_pairs={{1,2},{3,4},{5,6},{2,1},{4,3},{6,5},{9,10},{11,12},{13,14},{10,9},... | collective-permute-start | bytes 1572872 | tf_op jit(solution)/shard_map/ppermute | solution.py:599
  6.8 2.5 %collective-permute-start = (f32[2,128,512]{2,1,0:T(8,128)S(1)}, f32[2,128,512]{2,1,0:T(8,128)S(1)}, u32[]{:S(2)}, u32[]{:S(2)}) collective-permute-start(f32[2,128,512]{2,1,0:T(8,128)S(1)} %get-tuple-element.38), channel_id=1, source_target_pairs={{0,8},{8,16},{16,24},{24,32},{32,40},{40,48},{48,56},{56,64},{64,7... | collective-permute-start | bytes 1572872 | tf_op jit(solution)/shard_map/ppermute | solution.py:583
  9.3 2.8 %collective-permute-start.1 = (f32[2,128,512]{2,1,0:T(8,128)S(1)}, f32[2,128,512]{2,1,0:T(8,128)S(1)}, u32[]{:S(2)}, u32[]{:S(2)}) collective-permute-start(f32[2,128,512]{2,1,0:T(8,128)S(1)} %get-tuple-element.39), channel_id=1, source_target_pairs={{8,0},{16,8},{24,16},{32,24},{40,32},{48,40},{56,48},{64,56},{72,6... | collective-permute-start | bytes 1572872 | tf_op jit(solution)/shard_map/ppermute | solution.py:588
  12.8 0.0 copy-done
  12.8 0.0 copy-start.3
  12.8 1.2 copy-done.3
  14.0 0.0 copy-start.2
  14.0 2.2 %prepare.1 = (f32[8,256,256]{2,1,0:T(8,128)S(1)}, f32[2,4,256,256]{3,2,1,0:T(8,128)S(1)}) custom-call(f32[8,256,256]{2,1,0:T(8,128)S(1)} %copy-done, bf16[2,4,256,256]{3,2,1,0:T(8,128)(2,1)S(1)} %copy-done.3), custom_call_target="tpu_custom_call" | custom-call | flops 805306368 | bytes 9437184 | tf_op jit(solution)/shard_map/prepare/pallas_call | solution.py:359
  16.2 0.0 collective-permute-done.2.inner
  16.2 0.0 collective-permute-done.3.outer
  16.3 4.6 %collective-permute-start.4 = (f32[2,128,256]{2,1,0:T(8,128)S(1)}, f32[2,128,256]{2,1,0:T(8,128)S(1)}, u32[]{:S(2)}, u32[]{:S(2)}) collective-permute-start(f32[2,128,256]{2,1,0:T(8,128)S(1)} %pad_maximum_fusion), channel_id=1, source_target_pairs={{0,8},{8,16},{16,24},{24,32},{32,40},{40,48},{48,56},{56,64},{64,7... | collective-permute-start | bytes 786440 | tf_op jit(solution)/shard_map/ppermute | solution.py:583
  20.9 1.9 %collective-permute-start.5 = (f32[2,128,256]{2,1,0:T(8,128)S(1)}, f32[2,128,256]{2,1,0:T(8,128)S(1)}, u32[]{:S(2)}, u32[]{:S(2)}) collective-permute-start(f32[2,128,256]{2,1,0:T(8,128)S(1)} %pad_maximum_fusion.1), channel_id=1, source_target_pairs={{8,0},{16,8},{24,16},{32,24},{40,32},{48,40},{56,48},{64,56},{72,6... | collective-permute-start | bytes 786440 | tf_op jit(solution)/shard_map/ppermute | solution.py:588
  22.9 0.0 copy-done.2
  22.9 0.0 copy-done.4
  22.9 0.0 copy-done.5
  22.9 7.6 %slots_first.1 = (f32[2,6,768,128]{3,2,1,0:T(8,128)S(1)}, f32[2,6,768,128]{3,2,1,0:T(8,128)S(1)}, f32[4,256,256]{2,1,0:T(8,128)S(1)}, f32[4,256,256]{2,1,0:T(8,128)S(1)}) custom-call(s32[2,8]{1,0:T(2,128)S(1)} %copy-done.5, s32[1,1]{1,0:T(1,128)S(6)} %copy.18.counts, f32[2,512,512]{2,1,0:T(8,128)S(1)} %copy-done.2, ...), custom_call_target="tpu_custom_call" | custom-call | flops 4294967296 | bytes 31457280 | tf_op jit(solution)/shard_map/slots_first/pallas_call | solution.py:302
  30.5 0.0 collective-permute-done.above
  30.5 0.0 collective-permute-done.1.below
  30.5 0.0 collective-permute-done.4.corner_above
  30.5 1.0 collective-permute-done.5.corner_below
  31.5 8.1 %slots_second.1 = (f32[2,6,768,128]{3,2,1,0:T(8,128)S(1)}, f32[4,256,256]{2,1,0:T(8,128)S(1)}, f32[4,256,256]{2,1,0:T(8,128)S(1)}, f32[2,768,128]{2,1,0:T(8,128)S(1)}, f32[2,768,128]{2,1,0:T(8,128)S(1)}) custom-call(s32[2,8]{1,0:T(2,128)S(1)} %copy-done.5, s32[1,1]{1,0:T(1,128)S(6)} %copy.18.counts, ...), custom_call_target="tpu_custom_call", output_to_operand_aliasing={{0}: (7, {}), {1}: (8, {}), {2}: (9, {})} | custom-call | flops 4294967296 | bytes 31457280 | tf_op jit(solution)/shard_map/slots_second/pallas_call | solution.py:318
  39.7 0.1 collective-permute-start.6
  39.8 0.5 collective-permute-start.7
  40.3 2.5 %collective-permute-start.8 = (f32[2,768,128]{2,1,0:T(8,128)S(1)}, f32[2,768,128]{2,1,0:T(8,128)S(1)}, u32[]{:S(2)}, u32[]{:S(2)}) collective-permute-start(f32[2,768,128]{2,1,0:T(8,128)S(1)} %get-tuple-element.54), channel_id=1, source_target_pairs={{1,2},{3,4},{5,6},{2,1},{4,3},{6,5},{9,10},{11,12},{13,14},{10,9},... | collective-permute-start | bytes 2359304 | tf_op jit(solution)/shard_map/ppermute | solution.py:599
  42.7 2.4 %stash.1.grown = f32[2,11520,768]{2,1,0:T(8,128)} custom-call(f32[2,6,768,128]{3,2,1,0:T(8,128)S(1)} %get-tuple-element.49.totals), custom_call_target="tpu_custom_call" | custom-call | bytes 9437184 | tf_op jit(solution)/shard_map/stash/pallas_call | solution.py:434
  45.1 0.0 collective-permute-done.6.received
  45.1 1.0 pair_sum.1
  46.2 36.2 %conditional.2 = (f32[64,16,256]{2,1,0:T(8,128)}) conditional(s32[]{:T(128)} %bitcast.2, () %tuple.26, f32[4,256,256]{2,1,0:T(8,128)} %pair_sum.1), branch_computations={%region_0.0_spmd, %region_1.0_spmd} | conditional | bytes 2097160 | solution.py:606
  46.2 36.2 %all_to_all.8 = f32[64,16,256]{2,1,0:T(8,128)} all-to-all(f32[64,16,256]{2,1,0:T(8,128)} %bitcast.3), channel_id=1, replica_groups=mesh['x'=4,'y'=4,'z'=4,'core'=2] {'x','y','z'}, dimensions={0} | all-to-all | bytes 2097152 | tf_op jit(solution)/shard_map/cond/branch_1_fun/all_to_all | solution.py:604
  82.4 0.0 collective-permute-done.7.inner_in
  82.4 0.0 collective-permute-done.8.outer_in
  82.4 3.0 %turn.1 = (f32[64,16,256]{2,1,0:T(8,128)}, f32[2,128,512]{2,1,0:T(8,128)S(1)}, f32[2,128,512]{2,1,0:T(8,128)}) custom-call(f32[64,16,256]{2,1,0:T(8,128)} %get-tuple-element.68.pieces_in, f32[2,11520,768]{2,1,0:T(8,128)} %stash.1.grown, f32[2,768,128]{2,1,0:T(8,128)S(1)} %collective-permute-done.7.inner_in, f32[2,768,128]{2,1,0:T(8,128)S(1)} %collective-permute-done.8.outer_in), custom_call_target="tpu_custom_call" | custom-call | flops 600000 | bytes 7340032 | tf_op jit(solution)/shard_map/turn/pallas_call | solution.py:505
  85.4 4.5 %collective-permute-start.9 = (f32[2,128,512]{2,1,0:T(8,128)}, f32[2,128,512]{2,1,0:T(8,128)S(1)}, u32[]{:S(2)}, u32[]{:S(2)}) collective-permute-start(f32[2,128,512]{2,1,0:T(8,128)} %get-tuple-element.59), channel_id=1, source_target_pairs={{0,8},{8,16},{16,24},{24,32},{32,40},{40,48},{48,56},{56,64},{64,7... | collective-permute-start | bytes 1572872 | tf_op jit(solution)/shard_map/ppermute | solution.py:583
  89.9 1.9 %collective-permute-start.10 = (f32[2,128,512]{2,1,0:T(8,128)S(1)}, f32[2,128,512]{2,1,0:T(8,128)S(1)}, u32[]{:S(2)}, u32[]{:S(2)}) collective-permute-start(f32[2,128,512]{2,1,0:T(8,128)S(1)} %get-tuple-element.60), channel_id=1, source_target_pairs={{8,0},{16,8},{24,16},{32,24},{40,32},{48,40},{56,48},{64,56},{72,6... | collective-permute-start | bytes 1572872 | tf_op jit(solution)/shard_map/ppermute | solution.py:588
  91.8 31.9 %conditional.3 = (f32[4,256,256]{2,1,0:T(8,128)}) conditional(s32[]{:T(128)} %bitcast.2, () %tuple.28, f32[64,16,256]{2,1,0:T(8,128)} %get-tuple-element.58), branch_computations={%region_2.0_spmd, %region_3.0_spmd} | conditional | bytes 2097160 | solution.py:606
  91.8 31.8 %all_to_all.9 = f32[64,16,256]{2,1,0:T(8,128)} all-to-all(f32[64,16,256]{2,1,0:T(8,128)} %param.3), channel_id=1, replica_groups=mesh['x'=4,'y'=4,'z'=4,'core'=2] {'x','y','z'}, dimensions={0} | all-to-all | bytes 2097152 | tf_op jit(solution)/shard_map/cond/branch_1_fun/all_to_all | solution.py:604
  123.6 0.0 collective-permute-done.9.above_in
  123.6 0.0 collective-permute-done.10.below_in
  123.6 2.4 %collective-permute-start.11 = (f32[4,256,256]{2,1,0:T(8,128)}, f32[4,256,256]{2,1,0:T(8,128)S(1)}, u32[]{:S(2)}, u32[]{:S(2)}) collective-permute-start(f32[4,256,256]{2,1,0:T(8,128)} %get-tuple-element.69.own), channel_id=1, source_target_pairs={{0,1},{1,0},{2,3},{3,2},{4,5},{5,4},{6,7},{7,6},{8,9},{9,8},{10,11... | collective-permute-start | bytes 3145736 | tf_op jit(solution)/shard_map/ppermute | solution.py:593
  126.0 3.1 %finish.1 = f32[2,512,512]{2,1,0:T(8,128)} custom-call(f32[2,11520,768]{2,1,0:T(8,128)} %stash.1.grown, f32[2,768,128]{2,1,0:T(8,128)S(1)} %collective-permute-done.7.inner_in, f32[2,768,128]{2,1,0:T(8,128)S(1)} %collective-permute-done.8.outer_in, f32[2,128,512]{2,1,0:T(8,128)S(1)} %collective-permute-done.9.above_in, ...), custom_call_target="tpu_custom_call" | custom-call | flops 600000 | bytes 7340032 | tf_op jit(solution)/shard_map/finish/pallas_call | solution.py:548
  129.1 0.0 collective-permute-done.11.other
  129.1 0.0 copy-done.6
  129.1 1.3 %join.1 = f32[2,4,256,256]{3,2,1,0:T(8,128)} custom-call(f32[4,256,256]{2,1,0:T(8,128)S(1)} %copy-done.6, f32[4,256,256]{2,1,0:T(8,128)S(1)} %collective-permute-done.11.other), custom_call_target="tpu_custom_call" | custom-call | bytes 4194304 | tf_op jit(solution)/shard_map/join/pallas_call | solution.py:569
  (7 shorter events, 0.1 us)
Async XLA Ops:
  0.6 12.2 %copy-start = (f32[8,256,256]{2,1,0:T(8,128)S(1)}, f32[8,256,256]{2,1,0:T(8,128)}, u32[]{:S(2)}) copy-start(f32[8,256,256]{2,1,0:T(8,128)} %patterns.1) | copy-start | bytes 6291460
  0.6 1.7 %copy-start.1 = (f32[2,512,512]{2,1,0:T(8,128)S(1)}, f32[2,512,512]{2,1,0:T(8,128)}, u32[]{:S(2)}) copy-start(f32[2,512,512]{2,1,0:T(8,128)} %tile.3) | copy-start | bytes 6291460
  2.6 13.6 %collective-permute-start.2 = (f32[2,512,128]{2,1,0:T(8,128)S(1)}, f32[2,512,128]{2,1,0:T(8,128)S(1)}, u32[]{:S(2)}, u32[]{:S(2)}) collective-permute-start(f32[2,512,128]{2,1,0:T(8,128)S(1)} %get-tuple-element.40), channel_id=1, source_target_pairs={{0,1},{1,0},{2,3},{3,2},{4,5},{5,4},{6,7},{7,6},{8,9},{9,8},{10,11... | collective-permute-start | bytes 1572872 | tf_op jit(solution)/shard_map/ppermute | solution.py:593
  3.4 12.8 %collective-permute-start.3 = (f32[2,512,128]{2,1,0:T(8,128)S(1)}, f32[2,512,128]{2,1,0:T(8,128)S(1)}, u32[]{:S(2)}, u32[]{:S(2)}) collective-permute-start(f32[2,512,128]{2,1,0:T(8,128)S(1)} %get-tuple-element.41), channel_id=1, source_target_pairs={{1,2},{3,4},{5,6},{2,1},{4,3},{6,5},{9,10},{11,12},{13,14},{10,9},... | collective-permute-start | bytes 1572872 | tf_op jit(solution)/shard_map/ppermute | solution.py:599
  6.8 23.6 %collective-permute-start = (f32[2,128,512]{2,1,0:T(8,128)S(1)}, f32[2,128,512]{2,1,0:T(8,128)S(1)}, u32[]{:S(2)}, u32[]{:S(2)}) collective-permute-start(f32[2,128,512]{2,1,0:T(8,128)S(1)} %get-tuple-element.38), channel_id=1, source_target_pairs={{0,8},{8,16},{16,24},{24,32},{32,40},{40,48},{48,56},{56,64},{64,7... | collective-permute-start | bytes 1572872 | tf_op jit(solution)/shard_map/ppermute | solution.py:583
  9.3 21.1 %collective-permute-start.1 = (f32[2,128,512]{2,1,0:T(8,128)S(1)}, f32[2,128,512]{2,1,0:T(8,128)S(1)}, u32[]{:S(2)}, u32[]{:S(2)}) collective-permute-start(f32[2,128,512]{2,1,0:T(8,128)S(1)} %get-tuple-element.39), channel_id=1, source_target_pairs={{8,0},{16,8},{24,16},{32,24},{40,32},{48,40},{56,48},{64,56},{72,6... | collective-permute-start | bytes 1572872 | tf_op jit(solution)/shard_map/ppermute | solution.py:588
  12.8 1.2 copy-start.3
  14.0 8.8 %copy-start.2 = (f32[2,512,512]{2,1,0:T(8,128)S(1)}, f32[2,512,512]{2,1,0:T(8,128)}, u32[]{:S(2)}) copy-start(f32[2,512,512]{2,1,0:T(8,128)} %tile.3) | copy-start | bytes 6291460
  14.0 8.8 %copy-start.4 = (bf16[4,256,256]{2,1,0:T(8,128)(2,1)S(1)}, bf16[4,256,256]{2,1,0:T(8,128)(2,1)}, u32[]{:S(2)}) copy-start(bf16[4,256,256]{2,1,0:T(8,128)(2,1)} %constant.9.clone.table) | copy-start | bytes 1572868
  14.0 8.8 %copy-start.5 = (s32[2,8]{1,0:T(2,128)S(1)}, s32[2,8]{1,0:T(2,128)}, u32[]{:S(2)}) copy-start(s32[2,8]{1,0:T(2,128)} %offsets.3) | copy-start | bytes 196
  16.3 14.2 %collective-permute-start.4 = (f32[2,128,256]{2,1,0:T(8,128)S(1)}, f32[2,128,256]{2,1,0:T(8,128)S(1)}, u32[]{:S(2)}, u32[]{:S(2)}) collective-permute-start(f32[2,128,256]{2,1,0:T(8,128)S(1)} %pad_maximum_fusion), channel_id=1, source_target_pairs={{0,8},{8,16},{16,24},{24,32},{32,40},{40,48},{48,56},{56,64},{64,7... | collective-permute-start | bytes 786440 | tf_op jit(solution)/shard_map/ppermute | solution.py:583
  20.9 10.6 %collective-permute-start.5 = (f32[2,128,256]{2,1,0:T(8,128)S(1)}, f32[2,128,256]{2,1,0:T(8,128)S(1)}, u32[]{:S(2)}, u32[]{:S(2)}) collective-permute-start(f32[2,128,256]{2,1,0:T(8,128)S(1)} %pad_maximum_fusion.1), channel_id=1, source_target_pairs={{8,0},{16,8},{24,16},{32,24},{40,32},{48,40},{56,48},{64,56},{72,6... | collective-permute-start | bytes 786440 | tf_op jit(solution)/shard_map/ppermute | solution.py:588
  39.7 5.4 %collective-permute-start.6 = (f32[4,256,256]{2,1,0:T(8,128)S(1)}, f32[4,256,256]{2,1,0:T(8,128)S(1)}, u32[]{:S(2)}, u32[]{:S(2)}) collective-permute-start(f32[4,256,256]{2,1,0:T(8,128)S(1)} %get-tuple-element.48), channel_id=1, source_target_pairs={{0,1},{1,0},{2,3},{3,2},{4,5},{5,4},{6,7},{7,6},{8,9},{9,8},{10,11... | collective-permute-start | bytes 3145736 | tf_op jit(solution)/shard_map/ppermute | solution.py:593
  39.8 42.6 %collective-permute-start.7 = (f32[2,768,128]{2,1,0:T(8,128)S(1)}, f32[2,768,128]{2,1,0:T(8,128)S(1)}, u32[]{:S(2)}, u32[]{:S(2)}) collective-permute-start(f32[2,768,128]{2,1,0:T(8,128)S(1)} %get-tuple-element.53), channel_id=1, source_target_pairs={{0,1},{1,0},{2,3},{3,2},{4,5},{5,4},{6,7},{7,6},{8,9},{9,8},{10,11... | collective-permute-start | bytes 2359304 | tf_op jit(solution)/shard_map/ppermute | solution.py:593
  40.3 42.1 %collective-permute-start.8 = (f32[2,768,128]{2,1,0:T(8,128)S(1)}, f32[2,768,128]{2,1,0:T(8,128)S(1)}, u32[]{:S(2)}, u32[]{:S(2)}) collective-permute-start(f32[2,768,128]{2,1,0:T(8,128)S(1)} %get-tuple-element.54), channel_id=1, source_target_pairs={{1,2},{3,4},{5,6},{2,1},{4,3},{6,5},{9,10},{11,12},{13,14},{10,9},... | collective-permute-start | bytes 2359304 | tf_op jit(solution)/shard_map/ppermute | solution.py:599
  85.4 38.3 %collective-permute-start.9 = (f32[2,128,512]{2,1,0:T(8,128)}, f32[2,128,512]{2,1,0:T(8,128)S(1)}, u32[]{:S(2)}, u32[]{:S(2)}) collective-permute-start(f32[2,128,512]{2,1,0:T(8,128)} %get-tuple-element.59), channel_id=1, source_target_pairs={{0,8},{8,16},{16,24},{24,32},{32,40},{40,48},{48,56},{56,64},{64,7... | collective-permute-start | bytes 1572872 | tf_op jit(solution)/shard_map/ppermute | solution.py:583
  89.9 33.8 %collective-permute-start.10 = (f32[2,128,512]{2,1,0:T(8,128)S(1)}, f32[2,128,512]{2,1,0:T(8,128)S(1)}, u32[]{:S(2)}, u32[]{:S(2)}) collective-permute-start(f32[2,128,512]{2,1,0:T(8,128)S(1)} %get-tuple-element.60), channel_id=1, source_target_pairs={{8,0},{16,8},{24,16},{32,24},{40,32},{48,40},{56,48},{64,56},{72,6... | collective-permute-start | bytes 1572872 | tf_op jit(solution)/shard_map/ppermute | solution.py:588
  123.6 5.5 %copy-start.6 = (f32[4,256,256]{2,1,0:T(8,128)S(1)}, f32[4,256,256]{2,1,0:T(8,128)}, u32[]{:S(2)}) copy-start(f32[4,256,256]{2,1,0:T(8,128)} %get-tuple-element.69.own) | copy-start | bytes 3145732
  123.6 5.5 %collective-permute-start.11 = (f32[4,256,256]{2,1,0:T(8,128)}, f32[4,256,256]{2,1,0:T(8,128)S(1)}, u32[]{:S(2)}, u32[]{:S(2)}) collective-permute-start(f32[4,256,256]{2,1,0:T(8,128)} %get-tuple-element.69.own), channel_id=1, source_target_pairs={{0,1},{1,0},{2,3},{3,2},{4,5},{5,4},{6,7},{7,6},{8,9},{9,8},{10,11... | collective-permute-start | bytes 3145736 | tf_op jit(solution)/shard_map/ppermute | solution.py:593

commit v5 on v4

--- a/solution.py
+++ b/solution.py
@@ -239,27 +239,32 @@
 
 
 def second_kernel(
-    offsets, counts, above, below, corner_above, corner_below, ext_in, totals_in, keep_in,
+    offsets, counts, near, far, corner_near, corner_far, ext_in, totals_in, keep_in,
     send_in, pat, probe, table,
     totals, keep, send, inner_out, outer_out,
     ext, obj, psi, half, field, sems,
 ):
-    margin, cols = above.shape[1:]
+    margin, cols = near.shape[1:]
     last = ext.shape[1] - 1
     rows = ext.shape[2] - 2 * margin
     core = lax.axis_index(CORE)
     inner_block, outer_block = (1 - core) * last, core * last
-    top, middle, bottom = pl.ds(0, margin), pl.ds(margin, rows), pl.ds(margin + rows, margin)
+    middle = pl.ds(margin, rows)
     moves = Moves(sems)
     moves.begin(ext_in.at[:, :, middle, :], ext.at[:, :, middle, :])
+    odd = odd_row()
+    near_rows, far_rows = (
+        pl.ds(pl.multiple_of(start, LANES), margin)
+        for start in ((1 - odd) * (margin + rows), odd * (margin + rows))
+    )
     for j in range(1, last):
         lanes = pl.ds((j - 1) * LANES, LANES)
-        moves.begin(above.at[:, :, lanes], ext.at[:, j, top, :])
-        moves.begin(below.at[:, :, lanes], ext.at[:, j, bottom, :])
+        moves.begin(near.at[:, :, lanes], ext.at[:, j, near_rows, :])
+        moves.begin(far.at[:, :, lanes], ext.at[:, j, far_rows, :])
     for n, j in enumerate((inner_block, outer_block)):
         lanes = pl.ds(n * margin, margin)
-        moves.begin(corner_above.at[:, :, lanes], ext.at[:, j, top, :])
-        moves.begin(corner_below.at[:, :, lanes], ext.at[:, j, bottom, :])
+        moves.begin(corner_near.at[:, :, lanes], ext.at[:, j, near_rows, :])
+        moves.begin(corner_far.at[:, :, lanes], ext.at[:, j, far_rows, :])
     totals[...] = totals_in[...]
     keep[...] = keep_in[...]
     send[...] = send_in[...]
@@ -370,17 +375,25 @@
     )(patterns, probe)
 
 
-def cut_kernel(tile, top, bottom, inner, outer, sems):
-    margin = top.shape[1]
+def odd_row():
+    return lax.rem(lax.axis_index(ROW), 2)
+
+
+def cut_kernel(tile, near, far, inner, outer, sems):
+    margin = near.shape[1]
     rows, cols = tile.shape[1:]
     core = lax.axis_index(CORE)
+    odd = odd_row()
+
+    def band(start):
+        return tile.at[:, pl.ds(pl.multiple_of(start, LANES), margin), :]
 
     def strip(start):
         return tile.at[:, :, pl.ds(pl.multiple_of(start, LANES), margin)]
 
     moves = Moves(sems)
-    moves.begin(tile.at[:, pl.ds(rows - margin, margin), :], bottom)
-    moves.begin(tile.at[:, pl.ds(0, margin), :], top)
+    moves.begin(band((1 - odd) * (rows - margin)), near)
+    moves.begin(band(odd * (rows - margin)), far)
     moves.begin(strip(core * (cols - margin)), outer)
     moves.begin(strip((1 - core) * (cols - margin)), inner)
     moves.wait()
@@ -443,6 +456,32 @@
     )(totals)
 
 
+def corners_kernel(inner, outer, near, far, sems):
+    margin = near.shape[1]
+    start = inner.shape[1] - margin
+    odd = odd_row()
+    moves = Moves(sems)
+    for target, begin in ((near, (1 - odd) * start), (far, odd * start)):
+        rows = pl.ds(pl.multiple_of(begin, LANES), margin)
+        moves.begin(inner.at[:, rows, :], target.at[:, :, pl.ds(0, LANES)])
+        moves.begin(outer.at[:, rows, :], target.at[:, :, pl.ds(LANES, LANES)])
+    moves.wait()
+
+
+def corners(inner, outer):
+    shape = (2, inner.shape[2], 2 * LANES)
+    return pl.pallas_call(
+        corners_kernel,
+        out_shape=shapes(shape, shape),
+        in_specs=[FREE] * 2,
+        out_specs=[FREE] * 2,
+        scratch_shapes=[pltpu.SemaphoreType.DMA((4,))],
+        compiler_params=pltpu.CompilerParams(vmem_limit_bytes=MIB),
+        cost_estimate=pl.CostEstimate(flops=0, bytes_accessed=MIB, transcendentals=0),
+        name="corners",
+    )(inner, outer)
+
+
 def add_sides(add, inner, outer, last):
     core = lax.axis_index(CORE)
 
@@ -457,18 +496,11 @@
         add(outer, last)
 
 
-def load(sources, targets, sems):
-    moves = Moves(sems)
-    for source, target in zip(sources, targets):
-        moves.begin(source, target)
-    moves.wait()
-
-
 def turn_kernel(
-    pieces_in, grown, inner_in, outer_in, copies_out, top_out, bottom_out,
-    pieces, top, bottom, inner, outer, sems, out_sems,
+    pieces_in, grown, inner_in, outer_in, copies_out, near_out, far_out,
+    pieces, strips, inner, outer, sems, out_sems,
 ):
-    margin, cols = top.shape[1:]
+    margin, cols = strips.shape[2:]
     rows = inner_in.shape[1] - 2 * margin
     low, high = pl.ds(0, margin), pl.ds(margin + rows, margin)
     center = pl.ds(LANES, cols)
@@ -477,19 +509,20 @@
     for side_in, side in ((inner_in, inner), (outer_in, outer)):
         first.begin(side_in.at[:, low, :], side.at[:, low, :])
         first.begin(side_in.at[:, high, :], side.at[:, pl.ds(margin, margin), :])
-    first.begin(grown.at[:, low, center], top)
-    first.begin(grown.at[:, high, center], bottom)
+    first.begin(grown.at[:, low, center], strips.at[0])
+    first.begin(grown.at[:, high, center], strips.at[1])
     first.wait()
     last = Moves(out_sems)
 
     def add(side, start):
         lanes = pl.ds(start, LANES)
-        top[:, :, lanes] += side[:, :margin, :]
-        bottom[:, :, lanes] += side[:, margin:, :]
+        strips[0, :, :, lanes] += side[:, :margin, :]
+        strips[1, :, :, lanes] += side[:, margin:, :]
 
     add_sides(add, inner, outer, cols - LANES)
-    last.begin(top, top_out)
-    last.begin(bottom, bottom_out)
+    odd = odd_row()
+    last.begin(strips.at[1 - odd], near_out)
+    last.begin(strips.at[odd], far_out)
     total = pieces[0]
     for n in range(1, pieces.shape[0]):
         total = total + pieces[n]
@@ -507,7 +540,7 @@
         out_shape=shapes(pieces.shape, strip, strip),
         in_specs=[FREE] * 4,
         out_specs=[FREE] * 3,
-        scratch_shapes=[pltpu.VMEM(x, F32) for x in (pieces.shape, strip, strip, ends, ends)]
+        scratch_shapes=[pltpu.VMEM(x, F32) for x in (pieces.shape, (2,) + strip, ends, ends)]
         + [pltpu.SemaphoreType.DMA((7,)), pltpu.SemaphoreType.DMA((3,))],
         compiler_params=pltpu.CompilerParams(vmem_limit_bytes=8 * MIB),
         cost_estimate=pl.CostEstimate(flops=600_000, bytes_accessed=7 * MIB, transcendentals=0),
@@ -515,23 +548,22 @@
     )(pieces, grown, inner, outer)
 
 
-def finish_kernel(
-    grown, inner_in, outer_in, above_in, below_in, out,
-    center, inner, outer, above, below, sems,
-):
-    margin = above.shape[1]
+def finish_kernel(grown, inner_in, outer_in, near, far, out, center, inner, outer, strips, sems):
+    margin = near.shape[1]
     rows, cols = center.shape[1:]
     middle = pl.ds(margin, rows)
-    core_part = grown.at[:, middle, pl.ds(LANES, cols)]
-    load(
-        (core_part, inner_in.at[:, middle], outer_in.at[:, middle], above_in, below_in),
-        (center, inner, outer, above, below),
-        sems,
-    )
+    odd = odd_row()
+    loads = Moves(sems)
+    loads.begin(grown.at[:, middle, pl.ds(LANES, cols)], center)
+    loads.begin(inner_in.at[:, middle], inner)
+    loads.begin(outer_in.at[:, middle], outer)
+    loads.begin(near, strips.at[1 - odd])
+    loads.begin(far, strips.at[odd])
+    loads.wait()
     moves = Moves(sems)
     for p in range(2):
-        center[p, :margin, :] += above[p]
-        center[p, rows - margin :, :] += below[p]
+        center[p, :margin, :] += strips[0, p]
+        center[p, rows - margin :, :] += strips[1, p]
 
         def add(side, start):
             center[p, :, pl.ds(start, LANES)] += side[p]
@@ -541,10 +573,10 @@
     moves.wait()
 
 
-def finish(grown, inner, outer, above, below):
-    center = (2, inner.shape[1] - 2 * above.shape[1], above.shape[2])
+def finish(grown, inner, outer, near, far):
+    center = (2, inner.shape[1] - 2 * near.shape[1], near.shape[2])
     side = (2, center[1], LANES)
-    made = (center, side, side, above.shape, below.shape)
+    made = (center, side, side, (2,) + near.shape)
     return pl.pallas_call(
         finish_kernel,
         out_shape=jax.ShapeDtypeStruct(center, F32),
@@ -554,7 +586,7 @@
         compiler_params=pltpu.CompilerParams(vmem_limit_bytes=8 * MIB),
         cost_estimate=pl.CostEstimate(flops=600_000, bytes_accessed=7 * MIB, transcendentals=0),
         name="finish",
-    )(grown, inner, outer, above, below)
+    )(grown, inner, outer, near, far)
 
 
 def join_kernel(own, other, out, sems):
@@ -578,16 +610,6 @@
     )(own, other)
 
 
-def up(block, axes):
-    count = lax.axis_size(axes)
-    return lax.ppermute(block, axes, [(i, i + 1) for i in range(count - 1)])
-
-
-def down(block, axes):
-    count = lax.axis_size(axes)
-    return lax.ppermute(block, axes, [(i + 1, i) for i in range(count - 1)])
-
-
 def swap_inner(block, axes):
     count = lax.axis_size(axes)
     return lax.ppermute(block, axes, [(i, i ^ 1) for i in range(count)])
@@ -607,30 +629,24 @@
 
 
 def on_device(object_field, probe, patterns, offsets, counts):
-    rows = object_field.shape[1]
     width = patterns.shape[1]
     modes = probe.shape[1]
-    margin = width // 2
-
-    top, bottom, inner, outer = cut(object_field, margin)
-    from_above = up(bottom, ROW)
-    from_below = down(top, ROW)
+
+    near, far, inner, outer = cut(object_field, width // 2)
+    near = swap_inner(near, ROW)
+    far = swap_outer(far, ROW)
     outer = swap_outer(outer, COL)
     inner = swap_inner(inner, COL)
-
-    def corners(start):
-        span = slice(start, start + margin)
-        return jnp.concatenate([inner[:, span], outer[:, span]], axis=2)
-
-    corner_above = up(corners(rows - margin), ROW)
-    corner_below = down(corners(0), ROW)
+    corner_near, corner_far = corners(inner, outer)
+    corner_near = swap_inner(corner_near, ROW)
+    corner_far = swap_outer(corner_far, ROW)
 
     table = jnp.asarray(tables(width))
     measured, wide = prepare(patterns, probe)
     ext, totals, keep, send = first_slots(
         offsets, counts, object_field, inner, outer, measured, wide, table
     )
-    sides = (from_above, from_below, corner_above, corner_below)
+    sides = (near, far, corner_near, corner_far)
     totals, keep, send, inner, outer = second_slots(
         offsets, counts, sides, ext, totals, keep, send, measured, wide, table
     )
@@ -644,13 +660,13 @@
     chips = lax.axis_size(CHIP)
     pieces = exchange(counts, pair.reshape(chips, modes * width // chips, width))
     pieces, inner, outer = lax.optimization_barrier((pieces, inner, outer))
-    copies, top, bottom = turn(pieces, grown, inner, outer)
-    from_above = up(bottom, ROW)
-    from_below = down(top, ROW)
+    copies, near, far = turn(pieces, grown, inner, outer)
+    near = swap_inner(near, ROW)
+    far = swap_outer(far, ROW)
     gathered = exchange(counts, copies).reshape(modes, width, width)
-    gathered, from_above, from_below = lax.optimization_barrier((gathered, from_above, from_below))
+    gathered, near, far = lax.optimization_barrier((gathered, near, far))
     other = swap_inner(gathered, COL)
-    object_grad = finish(grown, inner, outer, from_above, from_below)
+    object_grad = finish(grown, inner, outer, near, far)
     return (object_grad, join(gathered, other))
 
 

time: 132 us -> 121 us (0.917)
  the two profiles are of different devices: /device:TPU:29 before, /device:TPU:1 now
where the time goes in v5:
time: 121 us; the launch traced here: 120 us
  blocking collectives  69.5 us (57%)
  starting transfers between devices  20.1 us (17%)
  Pallas kernels  19.9 us (16%)
  waiting for transfers between devices  6.05 us (5%)
  local copies, waits for them, and re-layouts  2.97 us (2%)
  between operations  1.66 us (1%)
    all_to_all x2, blocking collectives, send(): return lax.all_to_all(given, CHIP, 0, 0, tiled=True)  69.5 us
    ppermute x5, starting transfers between devices, swap_outer(): return lax.ppermute(block, axes, pairs + [(j, i) for i, j in pairs])  10.5 us
    ppermute x7, starting transfers between devices, swap_inner(): return lax.ppermute(block, axes, [(i, i ^ 1) for i in range(count)])  9.67 us
    pallas_call x1, Pallas kernels, second_slots(): pl.pallas_call(second_kernel, out_shape=shapes(totals.shape, keep.shape,...  4.95 us
    ppermute x7, waiting for transfers between devices, swap_inner(): return lax.ppermute(block, axes, [(i, i ^ 1) for i in range(count)])  4.92 us
    pallas_call x1, Pallas kernels, turn(): pl.pallas_call(turn_kernel, out_shape=shapes(pieces.shape, strip, strip),...  3.17 us
    pallas_call x1, Pallas kernels, finish(): pl.pallas_call(finish_kernel, out_shape=jax.ShapeDtypeStruct(center, F32)...  3.1 us
    unnamed x14, local copies, waits for them, and re-layouts  2.97 us
  transfers between devices with their start and end apart: 12, of which 3 were waited for; matrix products, arithmetic and copies ran while one was open for 0% of the time, Pallas kernels for 8%

profile of v5, /device:TPU:1, one launch (start us, length us, event | category | flops | bytes accessed | tf_op | source)
XLA Modules:
  0.0 120.3 jit_solution(1316143221380132828)
XLA Ops:
  0.6 0.0 copy-start
  0.6 0.0 copy-start.1
  0.7 1.7 %copy-done.1 = f32[2,512,512]{2,1,0:T(8,128)S(1)} copy-done((f32[2,512,512]{2,1,0:T(8,128)S(1)}, f32[2,512,512]{2,1,0:T(8,128)}, u32[]{:S(2)}) %copy-start.1) | copy-done | bytes 2097176
  2.4 0.3 cut.1
  2.6 1.5 %collective-permute-start.2 = (f32[2,512,128]{2,1,0:T(8,128)S(1)}, f32[2,512,128]{2,1,0:T(8,128)S(1)}, u32[]{:S(2)}, u32[]{:S(2)}) collective-permute-start(f32[2,512,128]{2,1,0:T(8,128)S(1)} %get-tuple-element.42), channel_id=1, source_target_pairs={{0,1},{1,0},{2,3},{3,2},{4,5},{5,4},{6,7},{7,6},{8,9},{9,8},{10,11... | collective-permute-start | bytes 1572872 | tf_op jit(solution)/shard_map/ppermute | solution.py:615
  4.1 3.5 %collective-permute-start.3 = (f32[2,512,128]{2,1,0:T(8,128)S(1)}, f32[2,512,128]{2,1,0:T(8,128)S(1)}, u32[]{:S(2)}, u32[]{:S(2)}) collective-permute-start(f32[2,512,128]{2,1,0:T(8,128)S(1)} %get-tuple-element.43), channel_id=1, source_target_pairs={{1,2},{3,4},{5,6},{2,1},{4,3},{6,5},{9,10},{11,12},{13,14},{10,9},... | collective-permute-start | bytes 1572872 | tf_op jit(solution)/shard_map/ppermute | solution.py:621
  7.7 1.4 %collective-permute-start = (f32[2,128,512]{2,1,0:T(8,128)S(1)}, f32[2,128,512]{2,1,0:T(8,128)S(1)}, u32[]{:S(2)}, u32[]{:S(2)}) collective-permute-start(f32[2,128,512]{2,1,0:T(8,128)S(1)} %get-tuple-element.40), channel_id=1, source_target_pairs={{0,8},{8,0},{16,24},{24,16},{32,40},{40,32},{48,56},{56,48},{64,72... | collective-permute-start | bytes 1572872 | tf_op jit(solution)/shard_map/ppermute | solution.py:615
  9.1 0.7 collective-permute-start.1
  10.4 0.0 copy-done
  10.4 0.0 copy-start.3
  10.4 1.2 %copy-done.3 = bf16[2,4,256,256]{3,2,1,0:T(8,128)(2,1)S(1)} copy-done((bf16[2,4,256,256]{3,2,1,0:T(8,128)(2,1)S(1)}, bf16[2,4,256,256]{3,2,1,0:T(8,128)(2,1)}, u32[]{:S(2)}) %copy-start.3) | copy-done | bytes 1048600
  11.6 2.2 %prepare.1 = (f32[8,256,256]{2,1,0:T(8,128)S(1)}, f32[2,4,256,256]{3,2,1,0:T(8,128)S(1)}) custom-call(f32[8,256,256]{2,1,0:T(8,128)S(1)} %copy-done, bf16[2,4,256,256]{3,2,1,0:T(8,128)(2,1)S(1)} %copy-done.3), custom_call_target="tpu_custom_call" | custom-call | flops 805306368 | bytes 9437184 | tf_op jit(solution)/shard_map/prepare/pallas_call | solution.py:364
  13.8 0.0 collective-permute-done.2.inner
  13.8 1.1 collective-permute-done.3.outer
  14.9 0.1 corners.1
  15.0 2.5 %collective-permute-start.4 = (f32[2,128,256]{2,1,0:T(8,128)S(1)}, f32[2,128,256]{2,1,0:T(8,128)S(1)}, u32[]{:S(2)}, u32[]{:S(2)}) collective-permute-start(f32[2,128,256]{2,1,0:T(8,128)S(1)} %get-tuple-element.44), channel_id=1, source_target_pairs={{0,8},{8,0},{16,24},{24,16},{32,40},{40,32},{48,56},{56,48},{64,72... | collective-permute-start | bytes 786440 | tf_op jit(solution)/shard_map/ppermute | solution.py:615
  17.5 0.7 collective-permute-start.5
  18.2 0.0 copy-done.2
  18.2 0.0 copy-done.4
  18.2 0.0 copy-done.5
  18.2 1.5 %slots_first.1 = (f32[2,6,768,128]{3,2,1,0:T(8,128)S(1)}, f32[2,6,768,128]{3,2,1,0:T(8,128)S(1)}, f32[4,256,256]{2,1,0:T(8,128)S(1)}, f32[4,256,256]{2,1,0:T(8,128)S(1)}) custom-call(s32[2,8]{1,0:T(2,128)S(1)} %copy-done.5, s32[1,1]{1,0:T(1,128)S(6)} %copy.18.counts, f32[2,512,512]{2,1,0:T(8,128)S(1)} %copy-done.2, ...), custom_call_target="tpu_custom_call" | custom-call | flops 4294967296 | bytes 31457280 | tf_op jit(solution)/shard_map/slots_first/pallas_call | solution.py:307
  19.8 2.0 %collective-permute-done.near = f32[2,128,512]{2,1,0:T(8,128)S(1)} collective-permute-done((f32[2,128,512]{2,1,0:T(8,128)S(1)}, f32[2,128,512]{2,1,0:T(8,128)S(1)}, u32[]{:S(2)}, u32[]{:S(2)}) %collective-permute-start) | collective-permute-done | bytes 524320 | tf_op jit(solution)/shard_map/ppermute | solution.py:615
  21.8 0.0 collective-permute-done.1.far
  21.8 2.9 %collective-permute-done.4.corner_near = f32[2,128,256]{2,1,0:T(8,128)S(1)} collective-permute-done((f32[2,128,256]{2,1,0:T(8,128)S(1)}, f32[2,128,256]{2,1,0:T(8,128)S(1)}, u32[]{:S(2)}, u32[]{:S(2)}) %collective-permute-start.4) | collective-permute-done | bytes 262176 | tf_op jit(solution)/shard_map/ppermute | solution.py:615
  24.7 0.0 collective-permute-done.5.corner_far
  24.7 5.0 %slots_second.1 = (f32[2,6,768,128]{3,2,1,0:T(8,128)S(1)}, f32[4,256,256]{2,1,0:T(8,128)S(1)}, f32[4,256,256]{2,1,0:T(8,128)S(1)}, f32[2,768,128]{2,1,0:T(8,128)S(1)}, f32[2,768,128]{2,1,0:T(8,128)S(1)}) custom-call(s32[2,8]{1,0:T(2,128)S(1)} %copy-done.5, s32[1,1]{1,0:T(1,128)S(6)} %copy.18.counts, ...), custom_call_target="tpu_custom_call", output_to_operand_aliasing={{0}: (7, {}), {1}: (8, {}), {2}: (9, {})} | custom-call | flops 4294967296 | bytes 31457280 | tf_op jit(solution)/shard_map/slots_second/pallas_call | solution.py:323
  29.6 0.1 collective-permute-start.6
  29.7 0.5 collective-permute-start.7
  30.2 4.9 %collective-permute-start.8 = (f32[2,768,128]{2,1,0:T(8,128)S(1)}, f32[2,768,128]{2,1,0:T(8,128)S(1)}, u32[]{:S(2)}, u32[]{:S(2)}) collective-permute-start(f32[2,768,128]{2,1,0:T(8,128)S(1)} %get-tuple-element.58), channel_id=1, source_target_pairs={{1,2},{3,4},{5,6},{2,1},{4,3},{6,5},{9,10},{11,12},{13,14},{10,9},... | collective-permute-start | bytes 2359304 | tf_op jit(solution)/shard_map/ppermute | solution.py:621
  35.2 2.3 %stash.1.grown = f32[2,11520,768]{2,1,0:T(8,128)} custom-call(f32[2,6,768,128]{3,2,1,0:T(8,128)S(1)} %get-tuple-element.53.totals), custom_call_target="tpu_custom_call" | custom-call | bytes 9437184 | tf_op jit(solution)/shard_map/stash/pallas_call | solution.py:447
  37.5 0.0 collective-permute-done.6.received
  37.5 1.0 pair_sum.1
  38.5 42.1 %conditional.2 = (f32[64,16,256]{2,1,0:T(8,128)}) conditional(s32[]{:T(128)} %bitcast.2, () %tuple.26, f32[4,256,256]{2,1,0:T(8,128)} %pair_sum.1), branch_computations={%region_0.0_spmd, %region_1.0_spmd} | conditional | bytes 2097160 | solution.py:628
  38.6 42.1 %all_to_all.8 = f32[64,16,256]{2,1,0:T(8,128)} all-to-all(f32[64,16,256]{2,1,0:T(8,128)} %bitcast.3), channel_id=1, replica_groups=mesh['x'=4,'y'=4,'z'=4,'core'=2] {'x','y','z'}, dimensions={0} | all-to-all | bytes 2097152 | tf_op jit(solution)/shard_map/cond/branch_1_fun/all_to_all | solution.py:626
  80.7 0.0 collective-permute-done.7.inner_in
  80.7 0.0 collective-permute-done.8.outer_in
  80.7 3.2 %turn.1 = (f32[64,16,256]{2,1,0:T(8,128)}, f32[2,128,512]{2,1,0:T(8,128)}, f32[2,128,512]{2,1,0:T(8,128)S(1)}) custom-call(f32[64,16,256]{2,1,0:T(8,128)} %get-tuple-element.68.pieces_in, f32[2,11520,768]{2,1,0:T(8,128)} %stash.1.grown, f32[2,768,128]{2,1,0:T(8,128)S(1)} %collective-permute-done.7.inner_in, f32[2,768,128]{2,1,0:T(8,128)S(1)} %collective-permute-done.8.outer_in), custom_call_target="tpu_custom_call" | custom-call | flops 600000 | bytes 7340032 | tf_op jit(solution)/shard_map/turn/pallas_call | solution.py:538
  83.9 0.9 collective-permute-start.9
  84.8 0.7 collective-permute-start.10
  85.5 27.4 %conditional.3 = (f32[4,256,256]{2,1,0:T(8,128)}) conditional(s32[]{:T(128)} %bitcast.2, () %tuple.28, f32[64,16,256]{2,1,0:T(8,128)} %get-tuple-element.62), branch_computations={%region_2.0_spmd, %region_3.0_spmd} | conditional | bytes 2097160 | solution.py:628
  85.5 27.4 %all_to_all.9 = f32[64,16,256]{2,1,0:T(8,128)} all-to-all(f32[64,16,256]{2,1,0:T(8,128)} %param.3), channel_id=1, replica_groups=mesh['x'=4,'y'=4,'z'=4,'core'=2] {'x','y','z'}, dimensions={0} | all-to-all | bytes 2097152 | tf_op jit(solution)/shard_map/cond/branch_1_fun/all_to_all | solution.py:626
  112.9 0.0 collective-permute-done.9.near
  112.9 0.0 collective-permute-done.10.far
  112.9 2.8 %collective-permute-start.11 = (f32[4,256,256]{2,1,0:T(8,128)}, f32[4,256,256]{2,1,0:T(8,128)S(1)}, u32[]{:S(2)}, u32[]{:S(2)}) collective-permute-start(f32[4,256,256]{2,1,0:T(8,128)} %get-tuple-element.69.own), channel_id=1, source_target_pairs={{0,1},{1,0},{2,3},{3,2},{4,5},{5,4},{6,7},{7,6},{8,9},{9,8},{10,11... | collective-permute-start | bytes 3145736 | tf_op jit(solution)/shard_map/ppermute | solution.py:615
  115.7 3.1 %finish.1 = f32[2,512,512]{2,1,0:T(8,128)} custom-call(f32[2,11520,768]{2,1,0:T(8,128)} %stash.1.grown, f32[2,768,128]{2,1,0:T(8,128)S(1)} %collective-permute-done.7.inner_in, f32[2,768,128]{2,1,0:T(8,128)S(1)} %collective-permute-done.8.outer_in, f32[2,128,512]{2,1,0:T(8,128)S(1)} %collective-permute-done.9.near, ...), custom_call_target="tpu_custom_call" | custom-call | flops 600000 | bytes 7340032 | tf_op jit(solution)/shard_map/finish/pallas_call | solution.py:580
  118.8 0.0 collective-permute-done.11.other
  118.8 0.0 copy-done.6
  118.8 1.3 %join.1 = f32[2,4,256,256]{3,2,1,0:T(8,128)} custom-call(f32[4,256,256]{2,1,0:T(8,128)S(1)} %copy-done.6, f32[4,256,256]{2,1,0:T(8,128)S(1)} %collective-permute-done.11.other), custom_call_target="tpu_custom_call" | custom-call | bytes 4194304 | tf_op jit(solution)/shard_map/join/pallas_call | solution.py:601
  (4 shorter events, 0.0 us)
Async XLA Ops:
  0.6 9.8 %copy-start = (f32[8,256,256]{2,1,0:T(8,128)S(1)}, f32[8,256,256]{2,1,0:T(8,128)}, u32[]{:S(2)}) copy-start(f32[8,256,256]{2,1,0:T(8,128)} %patterns.1) | copy-start | bytes 6291460
  0.6 1.7 %copy-start.1 = (f32[2,512,512]{2,1,0:T(8,128)S(1)}, f32[2,512,512]{2,1,0:T(8,128)}, u32[]{:S(2)}) copy-start(f32[2,512,512]{2,1,0:T(8,128)} %tile.3) | copy-start | bytes 6291460
  2.6 11.2 %collective-permute-start.2 = (f32[2,512,128]{2,1,0:T(8,128)S(1)}, f32[2,512,128]{2,1,0:T(8,128)S(1)}, u32[]{:S(2)}, u32[]{:S(2)}) collective-permute-start(f32[2,512,128]{2,1,0:T(8,128)S(1)} %get-tuple-element.42), channel_id=1, source_target_pairs={{0,1},{1,0},{2,3},{3,2},{4,5},{5,4},{6,7},{7,6},{8,9},{9,8},{10,11... | collective-permute-start | bytes 1572872 | tf_op jit(solution)/shard_map/ppermute | solution.py:615
  4.1 10.8 %collective-permute-start.3 = (f32[2,512,128]{2,1,0:T(8,128)S(1)}, f32[2,512,128]{2,1,0:T(8,128)S(1)}, u32[]{:S(2)}, u32[]{:S(2)}) collective-permute-start(f32[2,512,128]{2,1,0:T(8,128)S(1)} %get-tuple-element.43), channel_id=1, source_target_pairs={{1,2},{3,4},{5,6},{2,1},{4,3},{6,5},{9,10},{11,12},{13,14},{10,9},... | collective-permute-start | bytes 1572872 | tf_op jit(solution)/shard_map/ppermute | solution.py:621
  7.7 14.1 %collective-permute-start = (f32[2,128,512]{2,1,0:T(8,128)S(1)}, f32[2,128,512]{2,1,0:T(8,128)S(1)}, u32[]{:S(2)}, u32[]{:S(2)}) collective-permute-start(f32[2,128,512]{2,1,0:T(8,128)S(1)} %get-tuple-element.40), channel_id=1, source_target_pairs={{0,8},{8,0},{16,24},{24,16},{32,40},{40,32},{48,56},{56,48},{64,72... | collective-permute-start | bytes 1572872 | tf_op jit(solution)/shard_map/ppermute | solution.py:615
  9.1 12.7 %collective-permute-start.1 = (f32[2,128,512]{2,1,0:T(8,128)S(1)}, f32[2,128,512]{2,1,0:T(8,128)S(1)}, u32[]{:S(2)}, u32[]{:S(2)}) collective-permute-start(f32[2,128,512]{2,1,0:T(8,128)S(1)} %get-tuple-element.41), channel_id=1, source_target_pairs={{8,16},{24,32},{40,48},{56,64},{72,80},{88,96},{104,112},{16,8},{3... | collective-permute-start | bytes 1572872 | tf_op jit(solution)/shard_map/ppermute | solution.py:621
  10.4 1.2 %copy-start.3 = (bf16[2,4,256,256]{3,2,1,0:T(8,128)(2,1)S(1)}, bf16[2,4,256,256]{3,2,1,0:T(8,128)(2,1)}, u32[]{:S(2)}) copy-start(bf16[2,4,256,256]{3,2,1,0:T(8,128)(2,1)} %probe.1) | copy-start | bytes 3145732
  11.6 6.6 %copy-start.2 = (f32[2,512,512]{2,1,0:T(8,128)S(1)}, f32[2,512,512]{2,1,0:T(8,128)}, u32[]{:S(2)}) copy-start(f32[2,512,512]{2,1,0:T(8,128)} %tile.3) | copy-start | bytes 6291460
  11.6 6.6 %copy-start.4 = (bf16[4,256,256]{2,1,0:T(8,128)(2,1)S(1)}, bf16[4,256,256]{2,1,0:T(8,128)(2,1)}, u32[]{:S(2)}) copy-start(bf16[4,256,256]{2,1,0:T(8,128)(2,1)} %constant.9.clone.table) | copy-start | bytes 1572868
  11.6 6.6 %copy-start.5 = (s32[2,8]{1,0:T(2,128)S(1)}, s32[2,8]{1,0:T(2,128)}, u32[]{:S(2)}) copy-start(s32[2,8]{1,0:T(2,128)} %offsets.3) | copy-start | bytes 196
  15.0 9.6 %collective-permute-start.4 = (f32[2,128,256]{2,1,0:T(8,128)S(1)}, f32[2,128,256]{2,1,0:T(8,128)S(1)}, u32[]{:S(2)}, u32[]{:S(2)}) collective-permute-start(f32[2,128,256]{2,1,0:T(8,128)S(1)} %get-tuple-element.44), channel_id=1, source_target_pairs={{0,8},{8,0},{16,24},{24,16},{32,40},{40,32},{48,56},{56,48},{64,72... | collective-permute-start | bytes 786440 | tf_op jit(solution)/shard_map/ppermute | solution.py:615
  17.5 7.1 %collective-permute-start.5 = (f32[2,128,256]{2,1,0:T(8,128)S(1)}, f32[2,128,256]{2,1,0:T(8,128)S(1)}, u32[]{:S(2)}, u32[]{:S(2)}) collective-permute-start(f32[2,128,256]{2,1,0:T(8,128)S(1)} %get-tuple-element.45), channel_id=1, source_target_pairs={{8,16},{24,32},{40,48},{56,64},{72,80},{88,96},{104,112},{16,8},{3... | collective-permute-start | bytes 786440 | tf_op jit(solution)/shard_map/ppermute | solution.py:621
  29.6 7.9 %collective-permute-start.6 = (f32[4,256,256]{2,1,0:T(8,128)S(1)}, f32[4,256,256]{2,1,0:T(8,128)S(1)}, u32[]{:S(2)}, u32[]{:S(2)}) collective-permute-start(f32[4,256,256]{2,1,0:T(8,128)S(1)} %get-tuple-element.52), channel_id=1, source_target_pairs={{0,1},{1,0},{2,3},{3,2},{4,5},{5,4},{6,7},{7,6},{8,9},{9,8},{10,11... | collective-permute-start | bytes 3145736 | tf_op jit(solution)/shard_map/ppermute | solution.py:615
  29.7 51.0 %collective-permute-start.7 = (f32[2,768,128]{2,1,0:T(8,128)S(1)}, f32[2,768,128]{2,1,0:T(8,128)S(1)}, u32[]{:S(2)}, u32[]{:S(2)}) collective-permute-start(f32[2,768,128]{2,1,0:T(8,128)S(1)} %get-tuple-element.57), channel_id=1, source_target_pairs={{0,1},{1,0},{2,3},{3,2},{4,5},{5,4},{6,7},{7,6},{8,9},{9,8},{10,11... | collective-permute-start | bytes 2359304 | tf_op jit(solution)/shard_map/ppermute | solution.py:615
  30.2 50.5 %collective-permute-start.8 = (f32[2,768,128]{2,1,0:T(8,128)S(1)}, f32[2,768,128]{2,1,0:T(8,128)S(1)}, u32[]{:S(2)}, u32[]{:S(2)}) collective-permute-start(f32[2,768,128]{2,1,0:T(8,128)S(1)} %get-tuple-element.58), channel_id=1, source_target_pairs={{1,2},{3,4},{5,6},{2,1},{4,3},{6,5},{9,10},{11,12},{13,14},{10,9},... | collective-permute-start | bytes 2359304 | tf_op jit(solution)/shard_map/ppermute | solution.py:621
  83.9 29.0 %collective-permute-start.9 = (f32[2,128,512]{2,1,0:T(8,128)}, f32[2,128,512]{2,1,0:T(8,128)S(1)}, u32[]{:S(2)}, u32[]{:S(2)}) collective-permute-start(f32[2,128,512]{2,1,0:T(8,128)} %get-tuple-element.63), channel_id=1, source_target_pairs={{0,8},{8,0},{16,24},{24,16},{32,40},{40,32},{48,56},{56,48},{64,72... | collective-permute-start | bytes 1572872 | tf_op jit(solution)/shard_map/ppermute | solution.py:615
  84.8 28.1 %collective-permute-start.10 = (f32[2,128,512]{2,1,0:T(8,128)S(1)}, f32[2,128,512]{2,1,0:T(8,128)S(1)}, u32[]{:S(2)}, u32[]{:S(2)}) collective-permute-start(f32[2,128,512]{2,1,0:T(8,128)S(1)} %get-tuple-element.64), channel_id=1, source_target_pairs={{8,16},{24,32},{40,48},{56,64},{72,80},{88,96},{104,112},{16,8},{3... | collective-permute-start | bytes 1572872 | tf_op jit(solution)/shard_map/ppermute | solution.py:621
  112.9 5.9 %copy-start.6 = (f32[4,256,256]{2,1,0:T(8,128)S(1)}, f32[4,256,256]{2,1,0:T(8,128)}, u32[]{:S(2)}) copy-start(f32[4,256,256]{2,1,0:T(8,128)} %get-tuple-element.69.own) | copy-start | bytes 3145732
  112.9 5.9 %collective-permute-start.11 = (f32[4,256,256]{2,1,0:T(8,128)}, f32[4,256,256]{2,1,0:T(8,128)S(1)}, u32[]{:S(2)}, u32[]{:S(2)}) collective-permute-start(f32[4,256,256]{2,1,0:T(8,128)} %get-tuple-element.69.own), channel_id=1, source_target_pairs={{0,1},{1,0},{2,3},{3,2},{4,5},{5,4},{6,7},{7,6},{8,9},{9,8},{10,11... | collective-permute-start | bytes 3145736 | tf_op jit(solution)/shard_map/ppermute | solution.py:615

commit v6 on v5

--- a/solution.py
+++ b/solution.py
@@ -15,7 +15,7 @@
 RIGHT = (0, 2)
 LEFT = (1, 3)
 MIB = 1024 * 1024
-SPARE = 15
+SPARE = 23
 FREE = pl.BlockSpec(memory_space=pl.ANY)
 VMEM = pl.BlockSpec(memory_space=pltpu.VMEM)
 ROW, COL, CORE = ("x", "y"), ("z", "core"), "core"
@@ -436,9 +436,10 @@
 
 
 def stash_kernel(totals, out, sems):
-    moves = Moves(sems)
-    for j in range(totals.shape[1]):
-        moves.begin(totals.at[:, j], out.at[:, pl.ds(0, totals.shape[2]), pl.ds(j * LANES, LANES)])
+    rows = pl.ds(0, totals.shape[2])
+    moves = Moves(sems)
+    for j in range(totals.shape[1] - 2):
+        moves.begin(totals.at[:, 1 + j], out.at[:, rows, pl.ds(j * LANES, LANES)])
     moves.wait()
 
 
@@ -446,12 +447,12 @@
     planes, blocks, rows, lanes = totals.shape
     return pl.pallas_call(
         stash_kernel,
-        out_shape=jax.ShapeDtypeStruct((planes, SPARE * rows, blocks * lanes), F32),
+        out_shape=jax.ShapeDtypeStruct((planes, SPARE * rows, (blocks - 2) * lanes), F32),
         in_specs=[VMEM],
         out_specs=FREE,
         scratch_shapes=[pltpu.SemaphoreType.DMA((blocks,))],
         compiler_params=pltpu.CompilerParams(vmem_limit_bytes=6 * MIB),
-        cost_estimate=pl.CostEstimate(flops=0, bytes_accessed=9 * MIB, transcendentals=0),
+        cost_estimate=pl.CostEstimate(flops=0, bytes_accessed=6 * MIB, transcendentals=0),
         name="stash",
     )(totals)
 
@@ -496,23 +497,17 @@
         add(outer, last)
 
 
-def turn_kernel(
-    pieces_in, grown, inner_in, outer_in, copies_out, near_out, far_out,
-    pieces, strips, inner, outer, sems, out_sems,
-):
+def spread_kernel(grown, inner_in, outer_in, near_out, far_out, strips, inner, outer, sems):
     margin, cols = strips.shape[2:]
-    rows = inner_in.shape[1] - 2 * margin
-    low, high = pl.ds(0, margin), pl.ds(margin + rows, margin)
-    center = pl.ds(LANES, cols)
+    low, high = pl.ds(0, margin), pl.ds(inner_in.shape[1] - margin, margin)
     first = Moves(sems)
-    first.begin(pieces_in, pieces)
     for side_in, side in ((inner_in, inner), (outer_in, outer)):
         first.begin(side_in.at[:, low, :], side.at[:, low, :])
         first.begin(side_in.at[:, high, :], side.at[:, pl.ds(margin, margin), :])
-    first.begin(grown.at[:, low, center], strips.at[0])
-    first.begin(grown.at[:, high, center], strips.at[1])
+    first.begin(grown.at[:, low, :], strips.at[0])
+    first.begin(grown.at[:, high, :], strips.at[1])
     first.wait()
-    last = Moves(out_sems)
+    last = Moves(sems)
 
     def add(side, start):
         lanes = pl.ds(start, LANES)
@@ -523,29 +518,51 @@
     odd = odd_row()
     last.begin(strips.at[1 - odd], near_out)
     last.begin(strips.at[odd], far_out)
+    last.wait()
+
+
+def spread(grown, inner, outer):
+    margin = inner.shape[2]
+    strip, ends = (2, margin, grown.shape[2]), (2, 2 * margin, margin)
+    return pl.pallas_call(
+        spread_kernel,
+        out_shape=shapes(strip, strip),
+        in_specs=[FREE] * 3,
+        out_specs=[FREE] * 2,
+        scratch_shapes=[pltpu.VMEM(x, F32) for x in ((2,) + strip, ends, ends)]
+        + [pltpu.SemaphoreType.DMA((6,))],
+        compiler_params=pltpu.CompilerParams(vmem_limit_bytes=6 * MIB),
+        cost_estimate=pl.CostEstimate(flops=600_000, bytes_accessed=4 * MIB, transcendentals=0),
+        name="spread",
+    )(grown, inner, outer)
+
+
+def fold_kernel(pieces, copies_out, copies, sems):
+    count = pieces.shape[0]
     total = pieces[0]
-    for n in range(1, pieces.shape[0]):
+    for n in range(1, count):
         total = total + pieces[n]
-    for n in range(pieces.shape[0]):
-        pieces[n] = total
-    last.begin(pieces, copies_out)
-    last.wait()
-
-
-def turn(pieces, grown, inner, outer):
-    margin = inner.shape[2]
-    strip, ends = (2, margin, grown.shape[2] - 2 * LANES), (2, 2 * margin, margin)
-    return pl.pallas_call(
-        turn_kernel,
-        out_shape=shapes(pieces.shape, strip, strip),
-        in_specs=[FREE] * 4,
-        out_specs=[FREE] * 3,
-        scratch_shapes=[pltpu.VMEM(x, F32) for x in (pieces.shape, (2,) + strip, ends, ends)]
-        + [pltpu.SemaphoreType.DMA((7,)), pltpu.SemaphoreType.DMA((3,))],
-        compiler_params=pltpu.CompilerParams(vmem_limit_bytes=8 * MIB),
-        cost_estimate=pl.CostEstimate(flops=600_000, bytes_accessed=7 * MIB, transcendentals=0),
-        name="turn",
-    )(pieces, grown, inner, outer)
+    moves = Moves(sems)
+    part = count // 4
+    for q in range(4):
+        for n in range(part):
+            copies[q * part + n] = total
+        span = pl.ds(q * part, part)
+        moves.begin(copies.at[span], copies_out.at[span])
+    moves.wait()
+
+
+def fold(pieces):
+    return pl.pallas_call(
+        fold_kernel,
+        out_shape=jax.ShapeDtypeStruct(pieces.shape, F32),
+        in_specs=[VMEM],
+        out_specs=FREE,
+        scratch_shapes=[pltpu.VMEM(pieces.shape, F32), pltpu.SemaphoreType.DMA((4,))],
+        compiler_params=pltpu.CompilerParams(vmem_limit_bytes=4 * MIB),
+        cost_estimate=pl.CostEstimate(flops=300_000, bytes_accessed=2 * MIB, transcendentals=0),
+        name="fold",
+    )(pieces)
 
 
 def finish_kernel(grown, inner_in, outer_in, near, far, out, center, inner, outer, strips, sems):
@@ -553,15 +570,18 @@
     rows, cols = center.shape[1:]
     middle = pl.ds(margin, rows)
     odd = odd_row()
-    loads = Moves(sems)
-    loads.begin(grown.at[:, middle, pl.ds(LANES, cols)], center)
-    loads.begin(inner_in.at[:, middle], inner)
-    loads.begin(outer_in.at[:, middle], outer)
-    loads.begin(near, strips.at[1 - odd])
-    loads.begin(far, strips.at[odd])
-    loads.wait()
-    moves = Moves(sems)
+    loads = []
     for p in range(2):
+        moves = Moves(sems.at[p])
+        moves.begin(grown.at[p, middle, :], center.at[p])
+        moves.begin(inner_in.at[p, middle], inner.at[p])
+        moves.begin(outer_in.at[p, middle], outer.at[p])
+        moves.begin(near.at[p], strips.at[1 - odd, p])
+        moves.begin(far.at[p], strips.at[odd, p])
+        loads.append(moves)
+    stores = Moves(sems.at[2])
+    for p in range(2):
+        loads[p].wait()
         center[p, :margin, :] += strips[0, p]
         center[p, rows - margin :, :] += strips[1, p]
 
@@ -569,8 +589,8 @@
             center[p, :, pl.ds(start, LANES)] += side[p]
 
         add_sides(add, inner, outer, cols - LANES)
-        moves.begin(center.at[p], out.at[p])
-    moves.wait()
+        stores.begin(center.at[p], out.at[p])
+    stores.wait()
 
 
 def finish(grown, inner, outer, near, far):
@@ -582,7 +602,7 @@
         out_shape=jax.ShapeDtypeStruct(center, F32),
         in_specs=[FREE] * 5,
         out_specs=FREE,
-        scratch_shapes=[pltpu.VMEM(x, F32) for x in made] + [pltpu.SemaphoreType.DMA((5,))],
+        scratch_shapes=[pltpu.VMEM(x, F32) for x in made] + [pltpu.SemaphoreType.DMA((3, 5))],
         compiler_params=pltpu.CompilerParams(vmem_limit_bytes=8 * MIB),
         cost_estimate=pl.CostEstimate(flops=600_000, bytes_accessed=7 * MIB, transcendentals=0),
         name="finish",
@@ -660,10 +680,11 @@
     chips = lax.axis_size(CHIP)
     pieces = exchange(counts, pair.reshape(chips, modes * width // chips, width))
     pieces, inner, outer = lax.optimization_barrier((pieces, inner, outer))
-    copies, near, far = turn(pieces, grown, inner, outer)
+    near, far = spread(grown, inner, outer)
+    pieces, near, far = lax.optimization_barrier((pieces, near, far))
     near = swap_inner(near, ROW)
     far = swap_outer(far, ROW)
-    gathered = exchange(counts, copies).reshape(modes, width, width)
+    gathered = exchange(counts, fold(pieces)).reshape(modes, width, width)
     gathered, near, far = lax.optimization_barrier((gathered, near, far))
     other = swap_inner(gathered, COL)
     object_grad = finish(grown, inner, outer, near, far)

time: 121 us -> 122 us (level)
  Pallas kernels: 19.9 us -> 33.8 us
  blocking collectives: 69.5 us -> 63.4 us
  waiting for transfers between devices: 6.05 us -> 1.15 us
  starting transfers between devices: 20.1 us -> 17.7 us
    pallas_call x1, Pallas kernels: 4.95 us -> 13.6 us  [second_slots(): pl.pallas_call(second_kernel, out_shape=shapes(totals.shape, keep.shape,...]
    all_to_all x2, blocking collectives: 69.5 us -> 63.4 us  [send(): return lax.all_to_all(given, CHIP, 0, 0, tiled=True)]
    pallas_call x1, Pallas kernels: 1.52 us -> 7.26 us  [first_slots(): pl.pallas_call(first_kernel, out_shape=shapes(grown, grown, plane, plane)...]
    ppermute x7, waiting for transfers between devices: 4.92 us -> 0.02 us  [swap_inner(): return lax.ppermute(block, axes, [(i, i ^ 1) for i in range(count)])]
    ppermute x5, starting transfers between devices: 10.5 us -> 7.47 us  [swap_outer(): return lax.ppermute(block, axes, pairs + [(j, i) for i, j in pairs])]
    pallas_call x1 -> x2, Pallas kernels: 3.17 us -> 3.57 us  [the longest x1 2.47 us: spread(): pl.pallas_call(spread_kernel, out_shape=shapes(strip, strip), in_specs=[F...]
    unnamed x14 -> x16, local copies, waits for them, and re-layouts: 2.97 us -> 2.98 us
  transfers between devices with their start and end apart: 12 -> 12, of which waited for: 3 -> 1; matrix products, arithmetic and copies ran while one was open for 0% -> 0% of each run, Pallas kernels for 8% -> 13%
where the time goes in v6:
time: 122 us; the launch traced here: 121 us
  blocking collectives  63.4 us (52%)
  Pallas kernels  33.8 us (28%)
  starting transfers between devices  17.7 us (15%)
  local copies, waits for them, and re-layouts  2.98 us (2%)
  between operations  1.71 us (1%)
    all_to_all x2, blocking collectives, send(): return lax.all_to_all(given, CHIP, 0, 0, tiled=True)  63.4 us
    pallas_call x1, Pallas kernels, second_slots(): pl.pallas_call(second_kernel, out_shape=shapes(totals.shape, keep.shape,...  13.6 us
    ppermute x7, starting transfers between devices, swap_inner(): return lax.ppermute(block, axes, [(i, i ^ 1) for i in range(count)])  10.3 us
    ppermute x5, starting transfers between devices, swap_outer(): return lax.ppermute(block, axes, pairs + [(j, i) for i, j in pairs])  7.47 us
    pallas_call x1, Pallas kernels, first_slots(): pl.pallas_call(first_kernel, out_shape=shapes(grown, grown, plane, plane)...  7.26 us
    unnamed x16, local copies, waits for them, and re-layouts  2.98 us
    pallas_call x1, Pallas kernels, finish(): pl.pallas_call(finish_kernel, out_shape=jax.ShapeDtypeStruct(center, F32)...  2.81 us
    pallas_call x1, Pallas kernels, spread(): pl.pallas_call(spread_kernel, out_shape=shapes(strip, strip), in_specs=[F...  2.47 us
  transfers between devices with their start and end apart: 12, of which 1 were waited for; matrix products, arithmetic and copies ran while one was open for 0% of the time, Pallas kernels for 13%

profile of v6, /device:TPU:1, one launch (start us, length us, event | category | flops | bytes accessed | tf_op | source)
XLA Modules:
  0.0 120.7 jit_solution(13162498363393914735)
XLA Ops:
  0.6 0.0 copy-start
  0.6 0.0 copy-start.1
  0.7 1.7 %copy-done.1 = f32[2,512,512]{2,1,0:T(8,128)S(1)} copy-done((f32[2,512,512]{2,1,0:T(8,128)S(1)}, f32[2,512,512]{2,1,0:T(8,128)}, u32[]{:S(2)}) %copy-start.1) | copy-done | bytes 2097176
  2.4 0.3 cut.1
  2.6 1.5 %collective-permute-start.2 = (f32[2,512,128]{2,1,0:T(8,128)S(1)}, f32[2,512,128]{2,1,0:T(8,128)S(1)}, u32[]{:S(2)}, u32[]{:S(2)}) collective-permute-start(f32[2,512,128]{2,1,0:T(8,128)S(1)} %get-tuple-element.44), channel_id=1, source_target_pairs={{0,1},{1,0},{2,3},{3,2},{4,5},{5,4},{6,7},{7,6},{8,9},{9,8},{10,11... | collective-permute-start | bytes 1572872 | tf_op jit(solution)/shard_map/ppermute | solution.py:635
  4.1 3.5 %collective-permute-start.3 = (f32[2,512,128]{2,1,0:T(8,128)S(1)}, f32[2,512,128]{2,1,0:T(8,128)S(1)}, u32[]{:S(2)}, u32[]{:S(2)}) collective-permute-start(f32[2,512,128]{2,1,0:T(8,128)S(1)} %get-tuple-element.45), channel_id=1, source_target_pairs={{1,2},{3,4},{5,6},{2,1},{4,3},{6,5},{9,10},{11,12},{13,14},{10,9},... | collective-permute-start | bytes 1572872 | tf_op jit(solution)/shard_map/ppermute | solution.py:641
  7.7 1.4 %collective-permute-start = (f32[2,128,512]{2,1,0:T(8,128)S(1)}, f32[2,128,512]{2,1,0:T(8,128)S(1)}, u32[]{:S(2)}, u32[]{:S(2)}) collective-permute-start(f32[2,128,512]{2,1,0:T(8,128)S(1)} %get-tuple-element.42), channel_id=1, source_target_pairs={{0,8},{8,0},{16,24},{24,16},{32,40},{40,32},{48,56},{56,48},{64,72... | collective-permute-start | bytes 1572872 | tf_op jit(solution)/shard_map/ppermute | solution.py:635
  9.1 0.7 collective-permute-start.1
  10.4 0.0 copy-done
  10.4 0.0 copy-start.3
  10.4 1.2 %copy-done.3 = bf16[2,4,256,256]{3,2,1,0:T(8,128)(2,1)S(1)} copy-done((bf16[2,4,256,256]{3,2,1,0:T(8,128)(2,1)S(1)}, bf16[2,4,256,256]{3,2,1,0:T(8,128)(2,1)}, u32[]{:S(2)}) %copy-start.3) | copy-done | bytes 1048600
  11.6 2.2 %prepare.1 = (f32[8,256,256]{2,1,0:T(8,128)S(1)}, f32[2,4,256,256]{3,2,1,0:T(8,128)S(1)}) custom-call(f32[8,256,256]{2,1,0:T(8,128)S(1)} %copy-done, bf16[2,4,256,256]{3,2,1,0:T(8,128)(2,1)S(1)} %copy-done.3), custom_call_target="tpu_custom_call" | custom-call | flops 805306368 | bytes 9437184 | tf_op jit(solution)/shard_map/prepare/pallas_call | solution.py:364
  13.8 0.0 collective-permute-done.2.inner
  13.8 1.1 collective-permute-done.3.outer
  14.9 0.1 corners.1
  15.0 2.5 %collective-permute-start.4 = (f32[2,128,256]{2,1,0:T(8,128)S(1)}, f32[2,128,256]{2,1,0:T(8,128)S(1)}, u32[]{:S(2)}, u32[]{:S(2)}) collective-permute-start(f32[2,128,256]{2,1,0:T(8,128)S(1)} %get-tuple-element.46), channel_id=1, source_target_pairs={{0,8},{8,0},{16,24},{24,16},{32,40},{40,32},{48,56},{56,48},{64,72... | collective-permute-start | bytes 786440 | tf_op jit(solution)/shard_map/ppermute | solution.py:635
  17.5 0.7 collective-permute-start.5
  18.2 0.0 copy-done.2
  18.2 0.0 copy-done.4
  18.2 0.0 copy-done.5
  18.2 7.3 %slots_first.1 = (f32[2,6,768,128]{3,2,1,0:T(8,128)S(1)}, f32[2,6,768,128]{3,2,1,0:T(8,128)S(1)}, f32[4,256,256]{2,1,0:T(8,128)S(1)}, f32[4,256,256]{2,1,0:T(8,128)S(1)}) custom-call(s32[2,8]{1,0:T(2,128)S(1)} %copy-done.5, s32[1,1]{1,0:T(1,128)S(6)} %copy.18.counts, f32[2,512,512]{2,1,0:T(8,128)S(1)} %copy-done.2, ...), custom_call_target="tpu_custom_call" | custom-call | flops 4294967296 | bytes 31457280 | tf_op jit(solution)/shard_map/slots_first/pallas_call | solution.py:307
  25.5 0.0 collective-permute-done.near
  25.5 0.0 collective-permute-done.1.far
  25.5 0.0 collective-permute-done.4.corner_near
  25.5 0.0 collective-permute-done.5.corner_far
  25.5 13.6 %slots_second.1 = (f32[2,6,768,128]{3,2,1,0:T(8,128)S(1)}, f32[4,256,256]{2,1,0:T(8,128)S(1)}, f32[4,256,256]{2,1,0:T(8,128)S(1)}, f32[2,768,128]{2,1,0:T(8,128)S(1)}, f32[2,768,128]{2,1,0:T(8,128)S(1)}) custom-call(s32[2,8]{1,0:T(2,128)S(1)} %copy-done.5, s32[1,1]{1,0:T(1,128)S(6)} %copy.18.counts, ...), custom_call_target="tpu_custom_call", output_to_operand_aliasing={{0}: (7, {}), {1}: (8, {}), {2}: (9, {})} | custom-call | flops 4294967296 | bytes 31457280 | tf_op jit(solution)/shard_map/slots_second/pallas_call | solution.py:323
  39.1 0.1 collective-permute-start.6
  39.2 0.5 collective-permute-start.7
  39.7 1.9 %collective-permute-start.8 = (f32[2,768,128]{2,1,0:T(8,128)S(1)}, f32[2,768,128]{2,1,0:T(8,128)S(1)}, u32[]{:S(2)}, u32[]{:S(2)}) collective-permute-start(f32[2,768,128]{2,1,0:T(8,128)S(1)} %get-tuple-element.60), channel_id=1, source_target_pairs={{1,2},{3,4},{5,6},{2,1},{4,3},{6,5},{9,10},{11,12},{13,14},{10,9},... | collective-permute-start | bytes 2359304 | tf_op jit(solution)/shard_map/ppermute | solution.py:641
  41.6 1.7 %stash.1.grown = f32[2,17664,512]{2,1,0:T(8,128)} custom-call(f32[2,6,768,128]{3,2,1,0:T(8,128)S(1)} %get-tuple-element.55.totals), custom_call_target="tpu_custom_call" | custom-call | bytes 6291456 | tf_op jit(solution)/shard_map/stash/pallas_call | solution.py:448
  43.3 0.0 collective-permute-done.6.received
  43.3 1.0 pair_sum.1
  44.4 36.9 %conditional.2 = (f32[64,16,256]{2,1,0:T(8,128)}) conditional(s32[]{:T(128)} %bitcast.2, () %tuple.27, f32[4,256,256]{2,1,0:T(8,128)} %pair_sum.1), branch_computations={%region_0.0_spmd, %region_1.0_spmd} | conditional | bytes 2097160 | solution.py:648
  44.4 36.9 %all_to_all.8 = f32[64,16,256]{2,1,0:T(8,128)} all-to-all(f32[64,16,256]{2,1,0:T(8,128)} %bitcast.3), channel_id=1, replica_groups=mesh['x'=4,'y'=4,'z'=4,'core'=2] {'x','y','z'}, dimensions={0} | all-to-all | bytes 2097152 | tf_op jit(solution)/shard_map/cond/branch_1_fun/all_to_all | solution.py:646
  81.3 0.0 collective-permute-done.7.inner_in
  81.3 0.0 collective-permute-done.8.outer_in
  81.3 2.5 %spread.1 = (f32[2,128,512]{2,1,0:T(8,128)}, f32[2,128,512]{2,1,0:T(8,128)S(1)}) custom-call(f32[2,17664,512]{2,1,0:T(8,128)} %stash.1.grown, f32[2,768,128]{2,1,0:T(8,128)S(1)} %collective-permute-done.7.inner_in, f32[2,768,128]{2,1,0:T(8,128)S(1)} %collective-permute-done.8.outer_in), custom_call_target="tpu_custom_call" | custom-call | flops 600000 | bytes 4194304 | tf_op jit(solution)/shard_map/spread/pallas_call | solution.py:527
  83.8 1.0 collective-permute-start.9
  84.8 0.7 collective-permute-start.10
  85.5 1.1 fold.1
  86.6 26.5 %conditional.3 = (f32[4,256,256]{2,1,0:T(8,128)}) conditional(s32[]{:T(128)} %bitcast.2, () %tuple.29, f32[64,16,256]{2,1,0:T(8,128)} %fold.1), branch_computations={%region_2.0_spmd, %region_3.0_spmd} | conditional | bytes 2097160 | solution.py:648
  86.6 26.5 %all_to_all.9 = f32[64,16,256]{2,1,0:T(8,128)} all-to-all(f32[64,16,256]{2,1,0:T(8,128)} %param.3), channel_id=1, replica_groups=mesh['x'=4,'y'=4,'z'=4,'core'=2] {'x','y','z'}, dimensions={0} | all-to-all | bytes 2097152 | tf_op jit(solution)/shard_map/cond/branch_1_fun/all_to_all | solution.py:646
  113.1 0.0 collective-permute-done.9.near
  113.1 0.0 collective-permute-done.10.far
  113.1 3.3 %collective-permute-start.11 = (f32[4,256,256]{2,1,0:T(8,128)}, f32[4,256,256]{2,1,0:T(8,128)S(1)}, u32[]{:S(2)}, u32[]{:S(2)}) collective-permute-start(f32[4,256,256]{2,1,0:T(8,128)} %get-tuple-element.73.own), channel_id=1, source_target_pairs={{0,1},{1,0},{2,3},{3,2},{4,5},{5,4},{6,7},{7,6},{8,9},{9,8},{10,11... | collective-permute-start | bytes 3145736 | tf_op jit(solution)/shard_map/ppermute | solution.py:635
  116.4 2.8 %finish.1 = f32[2,512,512]{2,1,0:T(8,128)} custom-call(f32[2,17664,512]{2,1,0:T(8,128)} %stash.1.grown, f32[2,768,128]{2,1,0:T(8,128)S(1)} %collective-permute-done.7.inner_in, f32[2,768,128]{2,1,0:T(8,128)S(1)} %collective-permute-done.8.outer_in, f32[2,128,512]{2,1,0:T(8,128)S(1)} %collective-permute-done.9.near, ...), custom_call_target="tpu_custom_call" | custom-call | flops 600000 | bytes 7340032 | tf_op jit(solution)/shard_map/finish/pallas_call | solution.py:600
  119.2 0.0 collective-permute-done.11.other
  119.2 1.3 %join.1 = f32[2,4,256,256]{3,2,1,0:T(8,128)} custom-call(f32[4,256,256]{2,1,0:T(8,128)S(1)} %copy-done.7, f32[4,256,256]{2,1,0:T(8,128)S(1)} %collective-permute-done.11.other), custom_call_target="tpu_custom_call" | custom-call | bytes 4194304 | tf_op jit(solution)/shard_map/join/pallas_call | solution.py:621
  (7 shorter events, 0.0 us)
Async XLA Ops:
  0.6 9.8 %copy-start = (f32[8,256,256]{2,1,0:T(8,128)S(1)}, f32[8,256,256]{2,1,0:T(8,128)}, u32[]{:S(2)}) copy-start(f32[8,256,256]{2,1,0:T(8,128)} %patterns.1) | copy-start | bytes 6291460
  0.6 1.7 %copy-start.1 = (f32[2,512,512]{2,1,0:T(8,128)S(1)}, f32[2,512,512]{2,1,0:T(8,128)}, u32[]{:S(2)}) copy-start(f32[2,512,512]{2,1,0:T(8,128)} %tile.3) | copy-start | bytes 6291460
  2.6 11.2 %collective-permute-start.2 = (f32[2,512,128]{2,1,0:T(8,128)S(1)}, f32[2,512,128]{2,1,0:T(8,128)S(1)}, u32[]{:S(2)}, u32[]{:S(2)}) collective-permute-start(f32[2,512,128]{2,1,0:T(8,128)S(1)} %get-tuple-element.44), channel_id=1, source_target_pairs={{0,1},{1,0},{2,3},{3,2},{4,5},{5,4},{6,7},{7,6},{8,9},{9,8},{10,11... | collective-permute-start | bytes 1572872 | tf_op jit(solution)/shard_map/ppermute | solution.py:635
  4.1 10.8 %collective-permute-start.3 = (f32[2,512,128]{2,1,0:T(8,128)S(1)}, f32[2,512,128]{2,1,0:T(8,128)S(1)}, u32[]{:S(2)}, u32[]{:S(2)}) collective-permute-start(f32[2,512,128]{2,1,0:T(8,128)S(1)} %get-tuple-element.45), channel_id=1, source_target_pairs={{1,2},{3,4},{5,6},{2,1},{4,3},{6,5},{9,10},{11,12},{13,14},{10,9},... | collective-permute-start | bytes 1572872 | tf_op jit(solution)/shard_map/ppermute | solution.py:641
  7.7 17.8 %collective-permute-start = (f32[2,128,512]{2,1,0:T(8,128)S(1)}, f32[2,128,512]{2,1,0:T(8,128)S(1)}, u32[]{:S(2)}, u32[]{:S(2)}) collective-permute-start(f32[2,128,512]{2,1,0:T(8,128)S(1)} %get-tuple-element.42), channel_id=1, source_target_pairs={{0,8},{8,0},{16,24},{24,16},{32,40},{40,32},{48,56},{56,48},{64,72... | collective-permute-start | bytes 1572872 | tf_op jit(solution)/shard_map/ppermute | solution.py:635
  9.1 16.4 %collective-permute-start.1 = (f32[2,128,512]{2,1,0:T(8,128)S(1)}, f32[2,128,512]{2,1,0:T(8,128)S(1)}, u32[]{:S(2)}, u32[]{:S(2)}) collective-permute-start(f32[2,128,512]{2,1,0:T(8,128)S(1)} %get-tuple-element.43), channel_id=1, source_target_pairs={{8,16},{24,32},{40,48},{56,64},{72,80},{88,96},{104,112},{16,8},{3... | collective-permute-start | bytes 1572872 | tf_op jit(solution)/shard_map/ppermute | solution.py:641
  10.4 1.2 %copy-start.3 = (bf16[2,4,256,256]{3,2,1,0:T(8,128)(2,1)S(1)}, bf16[2,4,256,256]{3,2,1,0:T(8,128)(2,1)}, u32[]{:S(2)}) copy-start(bf16[2,4,256,256]{3,2,1,0:T(8,128)(2,1)} %probe.1) | copy-start | bytes 3145732
  11.6 6.6 %copy-start.2 = (f32[2,512,512]{2,1,0:T(8,128)S(1)}, f32[2,512,512]{2,1,0:T(8,128)}, u32[]{:S(2)}) copy-start(f32[2,512,512]{2,1,0:T(8,128)} %tile.3) | copy-start | bytes 6291460
  11.6 6.6 %copy-start.4 = (bf16[4,256,256]{2,1,0:T(8,128)(2,1)S(1)}, bf16[4,256,256]{2,1,0:T(8,128)(2,1)}, u32[]{:S(2)}) copy-start(bf16[4,256,256]{2,1,0:T(8,128)(2,1)} %constant.9.clone.table) | copy-start | bytes 1572868
  11.6 6.6 %copy-start.5 = (s32[2,8]{1,0:T(2,128)S(1)}, s32[2,8]{1,0:T(2,128)}, u32[]{:S(2)}) copy-start(s32[2,8]{1,0:T(2,128)} %offsets.3) | copy-start | bytes 196
  15.0 10.5 %collective-permute-start.4 = (f32[2,128,256]{2,1,0:T(8,128)S(1)}, f32[2,128,256]{2,1,0:T(8,128)S(1)}, u32[]{:S(2)}, u32[]{:S(2)}) collective-permute-start(f32[2,128,256]{2,1,0:T(8,128)S(1)} %get-tuple-element.46), channel_id=1, source_target_pairs={{0,8},{8,0},{16,24},{24,16},{32,40},{40,32},{48,56},{56,48},{64,72... | collective-permute-start | bytes 786440 | tf_op jit(solution)/shard_map/ppermute | solution.py:635
  17.5 8.0 %collective-permute-start.5 = (f32[2,128,256]{2,1,0:T(8,128)S(1)}, f32[2,128,256]{2,1,0:T(8,128)S(1)}, u32[]{:S(2)}, u32[]{:S(2)}) collective-permute-start(f32[2,128,256]{2,1,0:T(8,128)S(1)} %get-tuple-element.47), channel_id=1, source_target_pairs={{8,16},{24,32},{40,48},{56,64},{72,80},{88,96},{104,112},{16,8},{3... | collective-permute-start | bytes 786440 | tf_op jit(solution)/shard_map/ppermute | solution.py:641
  39.1 4.2 %collective-permute-start.6 = (f32[4,256,256]{2,1,0:T(8,128)S(1)}, f32[4,256,256]{2,1,0:T(8,128)S(1)}, u32[]{:S(2)}, u32[]{:S(2)}) collective-permute-start(f32[4,256,256]{2,1,0:T(8,128)S(1)} %get-tuple-element.54), channel_id=1, source_target_pairs={{0,1},{1,0},{2,3},{3,2},{4,5},{5,4},{6,7},{7,6},{8,9},{9,8},{10,11... | collective-permute-start | bytes 3145736 | tf_op jit(solution)/shard_map/ppermute | solution.py:635
  39.2 42.1 %collective-permute-start.7 = (f32[2,768,128]{2,1,0:T(8,128)S(1)}, f32[2,768,128]{2,1,0:T(8,128)S(1)}, u32[]{:S(2)}, u32[]{:S(2)}) collective-permute-start(f32[2,768,128]{2,1,0:T(8,128)S(1)} %get-tuple-element.59), channel_id=1, source_target_pairs={{0,1},{1,0},{2,3},{3,2},{4,5},{5,4},{6,7},{7,6},{8,9},{9,8},{10,11... | collective-permute-start | bytes 2359304 | tf_op jit(solution)/shard_map/ppermute | solution.py:635
  39.7 41.6 %collective-permute-start.8 = (f32[2,768,128]{2,1,0:T(8,128)S(1)}, f32[2,768,128]{2,1,0:T(8,128)S(1)}, u32[]{:S(2)}, u32[]{:S(2)}) collective-permute-start(f32[2,768,128]{2,1,0:T(8,128)S(1)} %get-tuple-element.60), channel_id=1, source_target_pairs={{1,2},{3,4},{5,6},{2,1},{4,3},{6,5},{9,10},{11,12},{13,14},{10,9},... | collective-permute-start | bytes 2359304 | tf_op jit(solution)/shard_map/ppermute | solution.py:641
  81.3 4.1 %copy-start.6 = (f32[64,16,256]{2,1,0:T(8,128)S(1)}, f32[64,16,256]{2,1,0:T(8,128)}, u32[]{:S(2)}) copy-start(f32[64,16,256]{2,1,0:T(8,128)} %get-tuple-element.72.pieces) | copy-start | bytes 3145732
  83.8 29.2 %collective-permute-start.9 = (f32[2,128,512]{2,1,0:T(8,128)}, f32[2,128,512]{2,1,0:T(8,128)S(1)}, u32[]{:S(2)}, u32[]{:S(2)}) collective-permute-start(f32[2,128,512]{2,1,0:T(8,128)} %get-tuple-element.67), channel_id=1, source_target_pairs={{0,8},{8,0},{16,24},{24,16},{32,40},{40,32},{48,56},{56,48},{64,72... | collective-permute-start | bytes 1572872 | tf_op jit(solution)/shard_map/ppermute | solution.py:635
  84.8 28.3 %collective-permute-start.10 = (f32[2,128,512]{2,1,0:T(8,128)S(1)}, f32[2,128,512]{2,1,0:T(8,128)S(1)}, u32[]{:S(2)}, u32[]{:S(2)}) collective-permute-start(f32[2,128,512]{2,1,0:T(8,128)S(1)} %get-tuple-element.68), channel_id=1, source_target_pairs={{8,16},{24,32},{40,48},{56,64},{72,80},{88,96},{104,112},{16,8},{3... | collective-permute-start | bytes 1572872 | tf_op jit(solution)/shard_map/ppermute | solution.py:641
  113.1 6.2 %copy-start.7 = (f32[4,256,256]{2,1,0:T(8,128)S(1)}, f32[4,256,256]{2,1,0:T(8,128)}, u32[]{:S(2)}) copy-start(f32[4,256,256]{2,1,0:T(8,128)} %get-tuple-element.73.own) | copy-start | bytes 3145732
  113.1 6.2 %collective-permute-start.11 = (f32[4,256,256]{2,1,0:T(8,128)}, f32[4,256,256]{2,1,0:T(8,128)S(1)}, u32[]{:S(2)}, u32[]{:S(2)}) collective-permute-start(f32[4,256,256]{2,1,0:T(8,128)} %get-tuple-element.73.own), channel_id=1, source_target_pairs={{0,1},{1,0},{2,3},{3,2},{4,5},{5,4},{6,7},{7,6},{8,9},{9,8},{10,11... | collective-permute-start | bytes 3145736 | tf_op jit(solution)/shard_map/ppermute | solution.py:635

commit v7 on v6

--- a/solution.py
+++ b/solution.py
@@ -108,6 +108,14 @@
         for parity in range(2):
             field[k, parity] = dot(table[LEFT[parity]], half[k, parity])
 
+    def left_forward_all():
+        for k in range(modes):
+            left_forward(k)
+
+    def left_backward_all():
+        for k in range(modes):
+            left_backward(k)
+
     def make_all_chi():
         for parity in range(2):
             for c in range(mid // CHUNK):
@@ -170,15 +178,10 @@
                     totals[p, block + 1, target, :] += jnp.where(at_or_after, second, first)
                     totals[p, block + 2, target, :] += jnp.where(at_or_after, 0.0, second)
 
-    gather_patch()
-    right_forward_all()
-    for k in range(modes):
-        left_forward(k)
-    make_all_chi()
-    right_backward_all()
-    for k in range(modes):
-        left_backward(k)
-    collect_all()
+    return (
+        gather_patch, right_forward_all, left_forward_all, make_all_chi, right_backward_all,
+        left_backward_all, collect_all,
+    )
 
 
 class Moves:
@@ -196,29 +199,47 @@
             move.wait()
 
 
-def visit_all(later, offsets, counts, tile_rows, tile_cols, ext, pat, *rest):
+def visit_all(later, offsets, counts, tile_rows, tile_cols, queue, works, ext, pat, *rest):
     width = pat.shape[1]
     margin = width // 2
     base_row = lax.axis_index(ROW) * tile_rows - margin
     base_col = lax.axis_index(COL) * tile_cols - margin
 
-    def visit(number, carry):
+    def enter(number, count):
         row = offsets[0, number] - base_row
-        col = offsets[1, number] - base_col
         beyond = jnp.logical_or(row < margin, row + width > margin + tile_rows)
-
-        @pl.when(beyond if later else jnp.logical_not(beyond))
+        wanted = beyond if later else jnp.logical_not(beyond)
+
+        @pl.when(wanted)
         def _():
-            one_slot(number, row, col, ext, pat, *rest)
-
+            queue[count] = number
+
+        return count + wanted.astype(jnp.int32)
+
+    count = lax.fori_loop(0, counts[0, 0], enter, 0)
+
+    def phases(place, work):
+        number = queue[place]
+        row, col = offsets[0, number] - base_row, offsets[1, number] - base_col
+        return one_slot(number, row, col, ext, pat, *rest, work)
+
+    def two(i, carry):
+        for both in zip(phases(2 * i, works[0]), phases(2 * i + 1, works[1])):
+            for phase in both:
+                phase()
         return carry
 
-    lax.fori_loop(0, counts[0, 0], visit, 0)
+    lax.fori_loop(0, count // 2, two, 0)
+
+    @pl.when(lax.rem(count, 2) == 1)
+    def _():
+        for phase in phases(count - 1, works[0]):
+            phase()
 
 
 def first_kernel(
     offsets, counts, tile, inner, outer, pat, probe, table,
-    ext, totals, keep, send, obj, psi, half, field, sems,
+    ext, totals, keep, send, obj, psi, half, field, queue, sems,
 ):
     rows, cols = tile.shape[1:]
     margin = inner.shape[2]
@@ -234,15 +255,15 @@
     keep[...] = jnp.zeros_like(keep)
     send[...] = jnp.zeros_like(send)
     moves.wait()
-    work = (obj, psi, half, field)
-    visit_all(False, offsets, counts, rows, cols, ext, pat, probe, table, totals, keep, send, work)
+    works = [tuple(x.at[n] for x in (obj, psi, half, field)) for n in range(2)]
+    visit_all(False, offsets, counts, rows, cols, queue, works, ext, pat, probe, table, totals, keep, send)
 
 
 def second_kernel(
     offsets, counts, near, far, corner_near, corner_far, ext_in, totals_in, keep_in,
     send_in, pat, probe, table,
     totals, keep, send, inner_out, outer_out,
-    ext, obj, psi, half, field, sems,
+    ext, obj, psi, half, field, queue, sems,
 ):
     margin, cols = near.shape[1:]
     last = ext.shape[1] - 1
@@ -269,8 +290,8 @@
     keep[...] = keep_in[...]
     send[...] = send_in[...]
     moves.wait()
-    work = (obj, psi, half, field)
-    visit_all(True, offsets, counts, rows, cols, ext, pat, probe, table, totals, keep, send, work)
+    works = [tuple(x.at[n] for x in (obj, psi, half, field)) for n in range(2)]
+    visit_all(True, offsets, counts, rows, cols, queue, works, ext, pat, probe, table, totals, keep, send)
     moves = Moves(sems)
     moves.begin(totals.at[:, outer_block], outer_out)
     moves.begin(totals.at[:, inner_block], inner_out)
@@ -279,10 +300,11 @@
 
 def slot_scratch(modes, width):
     return [
-        pltpu.VMEM((2, width, width), F32),
-        pltpu.VMEM((modes, 2, width, width), BF16),
-        pltpu.VMEM((modes, 2, width, width), BF16),
-        pltpu.VMEM((modes, 2, width, width), F32),
+        pltpu.VMEM((2, 2, width, width), F32),
+        pltpu.VMEM((2, modes, 2, width, width), BF16),
+        pltpu.VMEM((2, modes, 2, width, width), BF16),
+        pltpu.VMEM((2, modes, 2, width, width), F32),
+        pltpu.SMEM((8,), jnp.int32),
         pltpu.SemaphoreType.DMA((16,)),
     ]
 
@@ -310,7 +332,7 @@
         in_specs=[SMEM] * 2 + [FREE] * 3 + [VMEM] * 3,
         out_specs=[VMEM] * 4,
         scratch_shapes=slot_scratch(modes, width),
-        compiler_params=pltpu.CompilerParams(vmem_limit_bytes=24 * MIB),
+        compiler_params=pltpu.CompilerParams(vmem_limit_bytes=28 * MIB),
         cost_estimate=cost(4, modes, width),
         name="slots_first",
     )(offsets, counts, tile, inner, outer, patterns, probe, table)
@@ -327,7 +349,7 @@
         out_specs=[VMEM] * 3 + [FREE] * 2,
         scratch_shapes=[pltpu.VMEM(ext.shape, F32)] + slot_scratch(modes, width),
         input_output_aliases={7: 0, 8: 1, 9: 2},
-        compiler_params=pltpu.CompilerParams(vmem_limit_bytes=24 * MIB),
+        compiler_params=pltpu.CompilerParams(vmem_limit_bytes=28 * MIB),
         cost_estimate=cost(4, modes, width),
         name="slots_second",
     )(offsets, counts, *sides, ext, totals, keep, send, patterns, probe, table)

time: 122 us -> 123 us (level); the launches traced: 121 us -> 123 us
  blocking collectives: 63.4 us -> 68.6 us
  Pallas kernels: 33.8 us -> 29.6 us
  starting transfers between devices: 17.7 us -> 19.1 us
    all_to_all x2, blocking collectives: 63.4 us -> 68.6 us  [send(): return lax.all_to_all(given, CHIP, 0, 0, tiled=True)]
    pallas_call x1, Pallas kernels: 13.6 us -> 10.1 us  [second_slots(): pl.pallas_call(second_kernel, out_shape=shapes(totals.shape, keep.shape,...]
    ppermute x5, starting transfers between devices: 7.47 us -> 8.99 us  [swap_outer(): return lax.ppermute(block, axes, pairs + [(j, i) for i, j in pairs])]
where the time goes in v7:
time: 123 us
  blocking collectives  68.6 us (56%)
  Pallas kernels  29.6 us (24%)
  starting transfers between devices  19.1 us (16%)
  local copies, waits for them, and re-layouts  2.98 us (2%)
  between operations  1.71 us (1%)
    all_to_all x2, blocking collectives, send(): return lax.all_to_all(given, CHIP, 0, 0, tiled=True)  68.6 us
    ppermute x7, starting transfers between devices, swap_inner(): return lax.ppermute(block, axes, [(i, i ^ 1) for i in range(count)])  10.1 us
    pallas_call x1, Pallas kernels, second_slots(): pl.pallas_call(second_kernel, out_shape=shapes(totals.shape, keep.shape,...  10.1 us
    ppermute x5, starting transfers between devices, swap_outer(): return lax.ppermute(block, axes, pairs + [(j, i) for i, j in pairs])  8.99 us
    pallas_call x1, Pallas kernels, first_slots(): pl.pallas_call(first_kernel, out_shape=shapes(grown, grown, plane, plane)...  6.59 us
    unnamed x16, local copies, waits for them, and re-layouts  2.98 us
    pallas_call x1, Pallas kernels, finish(): pl.pallas_call(finish_kernel, out_shape=jax.ShapeDtypeStruct(center, F32)...  2.81 us
    pallas_call x1, Pallas kernels, spread(): pl.pallas_call(spread_kernel, out_shape=shapes(strip, strip), in_specs=[F...  2.47 us
  transfers between devices with their start and end apart: 12, of which 1 were waited for; matrix products, arithmetic and copies ran while one was open for 0% of the time, Pallas kernels for 13%

profile of v7, /device:TPU:1, one launch (start us, length us, event | category | flops | bytes accessed | tf_op | source)
XLA Modules:
  0.0 123.2 jit_solution(13215929756594055164)
XLA Ops:
  0.6 0.0 copy-start.1
  0.7 1.7 %copy-done.1 = f32[2,512,512]{2,1,0:T(8,128)S(1)} copy-done((f32[2,512,512]{2,1,0:T(8,128)S(1)}, f32[2,512,512]{2,1,0:T(8,128)}, u32[]{:S(2)}) %copy-start.1) | copy-done | bytes 2097176
  2.4 0.3 cut.1
  2.6 1.5 %collective-permute-start.2 = (f32[2,512,128]{2,1,0:T(8,128)S(1)}, f32[2,512,128]{2,1,0:T(8,128)S(1)}, u32[]{:S(2)}, u32[]{:S(2)}) collective-permute-start(f32[2,512,128]{2,1,0:T(8,128)S(1)} %get-tuple-element.44), channel_id=1, source_target_pairs={{0,1},{1,0},{2,3},{3,2},{4,5},{5,4},{6,7},{7,6},{8,9},{9,8},{10,11... | collective-permute-start | bytes 1572872 | tf_op jit(solution)/shard_map/ppermute | solution.py:657
  4.1 3.5 %collective-permute-start.3 = (f32[2,512,128]{2,1,0:T(8,128)S(1)}, f32[2,512,128]{2,1,0:T(8,128)S(1)}, u32[]{:S(2)}, u32[]{:S(2)}) collective-permute-start(f32[2,512,128]{2,1,0:T(8,128)S(1)} %get-tuple-element.45), channel_id=1, source_target_pairs={{1,2},{3,4},{5,6},{2,1},{4,3},{6,5},{9,10},{11,12},{13,14},{10,9},... | collective-permute-start | bytes 1572872 | tf_op jit(solution)/shard_map/ppermute | solution.py:663
  7.7 1.4 %collective-permute-start = (f32[2,128,512]{2,1,0:T(8,128)S(1)}, f32[2,128,512]{2,1,0:T(8,128)S(1)}, u32[]{:S(2)}, u32[]{:S(2)}) collective-permute-start(f32[2,128,512]{2,1,0:T(8,128)S(1)} %get-tuple-element.42), channel_id=1, source_target_pairs={{0,8},{8,0},{16,24},{24,16},{32,40},{40,32},{48,56},{56,48},{64,72... | collective-permute-start | bytes 1572872 | tf_op jit(solution)/shard_map/ppermute | solution.py:657
  9.1 0.7 collective-permute-start.1
  10.4 0.0 copy-start.3
  10.4 1.2 copy-done.3
  11.6 2.2 %prepare.1 = (f32[8,256,256]{2,1,0:T(8,128)S(1)}, f32[2,4,256,256]{3,2,1,0:T(8,128)S(1)}) custom-call(f32[8,256,256]{2,1,0:T(8,128)S(1)} %copy-done, bf16[2,4,256,256]{3,2,1,0:T(8,128)(2,1)S(1)} %copy-done.3), custom_call_target="tpu_custom_call" | custom-call | flops 805306368 | bytes 9437184 | tf_op jit(solution)/shard_map/prepare/pallas_call | solution.py:386
  13.8 0.0 collective-permute-done.2.inner
  13.8 1.1 collective-permute-done.3.outer
  14.9 0.1 corners.1
  15.0 2.5 %collective-permute-start.4 = (f32[2,128,256]{2,1,0:T(8,128)S(1)}, f32[2,128,256]{2,1,0:T(8,128)S(1)}, u32[]{:S(2)}, u32[]{:S(2)}) collective-permute-start(f32[2,128,256]{2,1,0:T(8,128)S(1)} %get-tuple-element.46), channel_id=1, source_target_pairs={{0,8},{8,0},{16,24},{24,16},{32,40},{40,32},{48,56},{56,48},{64,72... | collective-permute-start | bytes 786440 | tf_op jit(solution)/shard_map/ppermute | solution.py:657
  17.5 0.7 collective-permute-start.5
  18.2 0.0 copy-done.2
  18.2 0.0 copy-done.4
  18.2 0.0 copy-done.5
  18.2 6.6 %slots_first.1 = (f32[2,6,768,128]{3,2,1,0:T(8,128)S(1)}, f32[2,6,768,128]{3,2,1,0:T(8,128)S(1)}, f32[4,256,256]{2,1,0:T(8,128)S(1)}, f32[4,256,256]{2,1,0:T(8,128)S(1)}) custom-call(s32[2,8]{1,0:T(2,128)S(1)} %copy-done.5, s32[1,1]{1,0:T(1,128)S(6)} %copy.18.counts, f32[2,512,512]{2,1,0:T(8,128)S(1)} %copy-done.2, ...), custom_call_target="tpu_custom_call" | custom-call | flops 4294967296 | bytes 31457280 | tf_op jit(solution)/shard_map/slots_first/pallas_call | solution.py:329
  24.8 0.0 collective-permute-done.near
  24.8 0.0 collective-permute-done.1.far
  24.8 0.0 collective-permute-done.4.corner_near
  24.9 0.0 collective-permute-done.5.corner_far
  24.9 10.1 %slots_second.1 = (f32[2,6,768,128]{3,2,1,0:T(8,128)S(1)}, f32[4,256,256]{2,1,0:T(8,128)S(1)}, f32[4,256,256]{2,1,0:T(8,128)S(1)}, f32[2,768,128]{2,1,0:T(8,128)S(1)}, f32[2,768,128]{2,1,0:T(8,128)S(1)}) custom-call(s32[2,8]{1,0:T(2,128)S(1)} %copy-done.5, s32[1,1]{1,0:T(1,128)S(6)} %copy.18.counts, ...), custom_call_target="tpu_custom_call", output_to_operand_aliasing={{0}: (7, {}), {1}: (8, {}), {2}: (9, {})} | custom-call | flops 4294967296 | bytes 31457280 | tf_op jit(solution)/shard_map/slots_second/pallas_call | solution.py:345
  34.9 0.1 collective-permute-start.6
  35.0 0.5 collective-permute-start.7
  35.5 3.4 %collective-permute-start.8 = (f32[2,768,128]{2,1,0:T(8,128)S(1)}, f32[2,768,128]{2,1,0:T(8,128)S(1)}, u32[]{:S(2)}, u32[]{:S(2)}) collective-permute-start(f32[2,768,128]{2,1,0:T(8,128)S(1)} %get-tuple-element.60), channel_id=1, source_target_pairs={{1,2},{3,4},{5,6},{2,1},{4,3},{6,5},{9,10},{11,12},{13,14},{10,9},... | collective-permute-start | bytes 2359304 | tf_op jit(solution)/shard_map/ppermute | solution.py:663
  39.0 1.7 %stash.1.grown = f32[2,17664,512]{2,1,0:T(8,128)} custom-call(f32[2,6,768,128]{3,2,1,0:T(8,128)S(1)} %get-tuple-element.55.totals), custom_call_target="tpu_custom_call" | custom-call | bytes 6291456 | tf_op jit(solution)/shard_map/stash/pallas_call | solution.py:470
  40.7 0.0 collective-permute-done.6.received
  40.7 1.0 pair_sum.1
  41.7 42.6 %conditional.2 = (f32[64,16,256]{2,1,0:T(8,128)}) conditional(s32[]{:T(128)} %bitcast.2, () %tuple.27, f32[4,256,256]{2,1,0:T(8,128)} %pair_sum.1), branch_computations={%region_0.0_spmd, %region_1.0_spmd} | conditional | bytes 2097160 | solution.py:670
  41.8 42.6 %all_to_all.8 = f32[64,16,256]{2,1,0:T(8,128)} all-to-all(f32[64,16,256]{2,1,0:T(8,128)} %bitcast.3), channel_id=1, replica_groups=mesh['x'=4,'y'=4,'z'=4,'core'=2] {'x','y','z'}, dimensions={0} | all-to-all | bytes 2097152 | tf_op jit(solution)/shard_map/cond/branch_1_fun/all_to_all | solution.py:668
  84.4 0.0 collective-permute-done.7.inner_in
  84.4 0.0 collective-permute-done.8.outer_in
  84.4 2.5 %spread.1 = (f32[2,128,512]{2,1,0:T(8,128)}, f32[2,128,512]{2,1,0:T(8,128)S(1)}) custom-call(f32[2,17664,512]{2,1,0:T(8,128)} %stash.1.grown, f32[2,768,128]{2,1,0:T(8,128)S(1)} %collective-permute-done.7.inner_in, f32[2,768,128]{2,1,0:T(8,128)S(1)} %collective-permute-done.8.outer_in), custom_call_target="tpu_custom_call" | custom-call | flops 600000 | bytes 4194304 | tf_op jit(solution)/shard_map/spread/pallas_call | solution.py:549
  86.8 1.1 collective-permute-start.9
  87.9 0.7 collective-permute-start.10
  88.6 0.0 copy-done.6
  88.6 1.1 fold.1
  89.7 26.1 %conditional.3 = (f32[4,256,256]{2,1,0:T(8,128)}) conditional(s32[]{:T(128)} %bitcast.2, () %tuple.29, f32[64,16,256]{2,1,0:T(8,128)} %fold.1), branch_computations={%region_2.0_spmd, %region_3.0_spmd} | conditional | bytes 2097160 | solution.py:670
  89.8 26.0 %all_to_all.9 = f32[64,16,256]{2,1,0:T(8,128)} all-to-all(f32[64,16,256]{2,1,0:T(8,128)} %param.3), channel_id=1, replica_groups=mesh['x'=4,'y'=4,'z'=4,'core'=2] {'x','y','z'}, dimensions={0} | all-to-all | bytes 2097152 | tf_op jit(solution)/shard_map/cond/branch_1_fun/all_to_all | solution.py:668
  115.8 0.0 collective-permute-done.9.near
  115.8 0.0 collective-permute-done.10.far
  115.8 3.1 %collective-permute-start.11 = (f32[4,256,256]{2,1,0:T(8,128)}, f32[4,256,256]{2,1,0:T(8,128)S(1)}, u32[]{:S(2)}, u32[]{:S(2)}) collective-permute-start(f32[4,256,256]{2,1,0:T(8,128)} %get-tuple-element.73.own), channel_id=1, source_target_pairs={{0,1},{1,0},{2,3},{3,2},{4,5},{5,4},{6,7},{7,6},{8,9},{9,8},{10,11... | collective-permute-start | bytes 3145736 | tf_op jit(solution)/shard_map/ppermute | solution.py:657
  118.9 2.8 %finish.1 = f32[2,512,512]{2,1,0:T(8,128)} custom-call(f32[2,17664,512]{2,1,0:T(8,128)} %stash.1.grown, f32[2,768,128]{2,1,0:T(8,128)S(1)} %collective-permute-done.7.inner_in, f32[2,768,128]{2,1,0:T(8,128)S(1)} %collective-permute-done.8.outer_in, f32[2,128,512]{2,1,0:T(8,128)S(1)} %collective-permute-done.9.near, ...), custom_call_target="tpu_custom_call" | custom-call | flops 600000 | bytes 7340032 | tf_op jit(solution)/shard_map/finish/pallas_call | solution.py:622
  121.7 0.0 collective-permute-done.11.other
  121.7 0.0 copy-done.7
  121.7 1.3 %join.1 = f32[2,4,256,256]{3,2,1,0:T(8,128)} custom-call(f32[4,256,256]{2,1,0:T(8,128)S(1)} %copy-done.7, f32[4,256,256]{2,1,0:T(8,128)S(1)} %collective-permute-done.11.other), custom_call_target="tpu_custom_call" | custom-call | bytes 4194304 | tf_op jit(solution)/shard_map/join/pallas_call | solution.py:643
  (7 shorter events, 0.0 us)
Async XLA Ops:
  0.6 9.8 %copy-start = (f32[8,256,256]{2,1,0:T(8,128)S(1)}, f32[8,256,256]{2,1,0:T(8,128)}, u32[]{:S(2)}) copy-start(f32[8,256,256]{2,1,0:T(8,128)} %patterns.1) | copy-start | bytes 6291460
  0.6 1.7 %copy-start.1 = (f32[2,512,512]{2,1,0:T(8,128)S(1)}, f32[2,512,512]{2,1,0:T(8,128)}, u32[]{:S(2)}) copy-start(f32[2,512,512]{2,1,0:T(8,128)} %tile.3) | copy-start | bytes 6291460
  2.6 11.2 %collective-permute-start.2 = (f32[2,512,128]{2,1,0:T(8,128)S(1)}, f32[2,512,128]{2,1,0:T(8,128)S(1)}, u32[]{:S(2)}, u32[]{:S(2)}) collective-permute-start(f32[2,512,128]{2,1,0:T(8,128)S(1)} %get-tuple-element.44), channel_id=1, source_target_pairs={{0,1},{1,0},{2,3},{3,2},{4,5},{5,4},{6,7},{7,6},{8,9},{9,8},{10,11... | collective-permute-start | bytes 1572872 | tf_op jit(solution)/shard_map/ppermute | solution.py:657
  4.1 10.8 %collective-permute-start.3 = (f32[2,512,128]{2,1,0:T(8,128)S(1)}, f32[2,512,128]{2,1,0:T(8,128)S(1)}, u32[]{:S(2)}, u32[]{:S(2)}) collective-permute-start(f32[2,512,128]{2,1,0:T(8,128)S(1)} %get-tuple-element.45), channel_id=1, source_target_pairs={{1,2},{3,4},{5,6},{2,1},{4,3},{6,5},{9,10},{11,12},{13,14},{10,9},... | collective-permute-start | bytes 1572872 | tf_op jit(solution)/shard_map/ppermute | solution.py:663
  7.7 17.1 %collective-permute-start = (f32[2,128,512]{2,1,0:T(8,128)S(1)}, f32[2,128,512]{2,1,0:T(8,128)S(1)}, u32[]{:S(2)}, u32[]{:S(2)}) collective-permute-start(f32[2,128,512]{2,1,0:T(8,128)S(1)} %get-tuple-element.42), channel_id=1, source_target_pairs={{0,8},{8,0},{16,24},{24,16},{32,40},{40,32},{48,56},{56,48},{64,72... | collective-permute-start | bytes 1572872 | tf_op jit(solution)/shard_map/ppermute | solution.py:657
  9.1 15.8 %collective-permute-start.1 = (f32[2,128,512]{2,1,0:T(8,128)S(1)}, f32[2,128,512]{2,1,0:T(8,128)S(1)}, u32[]{:S(2)}, u32[]{:S(2)}) collective-permute-start(f32[2,128,512]{2,1,0:T(8,128)S(1)} %get-tuple-element.43), channel_id=1, source_target_pairs={{8,16},{24,32},{40,48},{56,64},{72,80},{88,96},{104,112},{16,8},{3... | collective-permute-start | bytes 1572872 | tf_op jit(solution)/shard_map/ppermute | solution.py:663
  10.4 1.2 copy-start.3
  11.6 6.6 %copy-start.2 = (f32[2,512,512]{2,1,0:T(8,128)S(1)}, f32[2,512,512]{2,1,0:T(8,128)}, u32[]{:S(2)}) copy-start(f32[2,512,512]{2,1,0:T(8,128)} %tile.3) | copy-start | bytes 6291460
  11.6 6.6 %copy-start.4 = (bf16[4,256,256]{2,1,0:T(8,128)(2,1)S(1)}, bf16[4,256,256]{2,1,0:T(8,128)(2,1)}, u32[]{:S(2)}) copy-start(bf16[4,256,256]{2,1,0:T(8,128)(2,1)} %constant.9.clone.table) | copy-start | bytes 1572868
  11.6 6.6 %copy-start.5 = (s32[2,8]{1,0:T(2,128)S(1)}, s32[2,8]{1,0:T(2,128)}, u32[]{:S(2)}) copy-start(s32[2,8]{1,0:T(2,128)} %offsets.3) | copy-start | bytes 196
  15.0 9.8 %collective-permute-start.4 = (f32[2,128,256]{2,1,0:T(8,128)S(1)}, f32[2,128,256]{2,1,0:T(8,128)S(1)}, u32[]{:S(2)}, u32[]{:S(2)}) collective-permute-start(f32[2,128,256]{2,1,0:T(8,128)S(1)} %get-tuple-element.46), channel_id=1, source_target_pairs={{0,8},{8,0},{16,24},{24,16},{32,40},{40,32},{48,56},{56,48},{64,72... | collective-permute-start | bytes 786440 | tf_op jit(solution)/shard_map/ppermute | solution.py:657
  17.5 7.3 %collective-permute-start.5 = (f32[2,128,256]{2,1,0:T(8,128)S(1)}, f32[2,128,256]{2,1,0:T(8,128)S(1)}, u32[]{:S(2)}, u32[]{:S(2)}) collective-permute-start(f32[2,128,256]{2,1,0:T(8,128)S(1)} %get-tuple-element.47), channel_id=1, source_target_pairs={{8,16},{24,32},{40,48},{56,64},{72,80},{88,96},{104,112},{16,8},{3... | collective-permute-start | bytes 786440 | tf_op jit(solution)/shard_map/ppermute | solution.py:663
  34.9 5.8 %collective-permute-start.6 = (f32[4,256,256]{2,1,0:T(8,128)S(1)}, f32[4,256,256]{2,1,0:T(8,128)S(1)}, u32[]{:S(2)}, u32[]{:S(2)}) collective-permute-start(f32[4,256,256]{2,1,0:T(8,128)S(1)} %get-tuple-element.54), channel_id=1, source_target_pairs={{0,1},{1,0},{2,3},{3,2},{4,5},{5,4},{6,7},{7,6},{8,9},{9,8},{10,11... | collective-permute-start | bytes 3145736 | tf_op jit(solution)/shard_map/ppermute | solution.py:657
  35.0 49.3 %collective-permute-start.7 = (f32[2,768,128]{2,1,0:T(8,128)S(1)}, f32[2,768,128]{2,1,0:T(8,128)S(1)}, u32[]{:S(2)}, u32[]{:S(2)}) collective-permute-start(f32[2,768,128]{2,1,0:T(8,128)S(1)} %get-tuple-element.59), channel_id=1, source_target_pairs={{0,1},{1,0},{2,3},{3,2},{4,5},{5,4},{6,7},{7,6},{8,9},{9,8},{10,11... | collective-permute-start | bytes 2359304 | tf_op jit(solution)/shard_map/ppermute | solution.py:657
  35.5 48.8 %collective-permute-start.8 = (f32[2,768,128]{2,1,0:T(8,128)S(1)}, f32[2,768,128]{2,1,0:T(8,128)S(1)}, u32[]{:S(2)}, u32[]{:S(2)}) collective-permute-start(f32[2,768,128]{2,1,0:T(8,128)S(1)} %get-tuple-element.60), channel_id=1, source_target_pairs={{1,2},{3,4},{5,6},{2,1},{4,3},{6,5},{9,10},{11,12},{13,14},{10,9},... | collective-permute-start | bytes 2359304 | tf_op jit(solution)/shard_map/ppermute | solution.py:663
  84.3 4.3 %copy-start.6 = (f32[64,16,256]{2,1,0:T(8,128)S(1)}, f32[64,16,256]{2,1,0:T(8,128)}, u32[]{:S(2)}) copy-start(f32[64,16,256]{2,1,0:T(8,128)} %get-tuple-element.72.pieces) | copy-start | bytes 3145732
  86.8 29.0 %collective-permute-start.9 = (f32[2,128,512]{2,1,0:T(8,128)}, f32[2,128,512]{2,1,0:T(8,128)S(1)}, u32[]{:S(2)}, u32[]{:S(2)}) collective-permute-start(f32[2,128,512]{2,1,0:T(8,128)} %get-tuple-element.67), channel_id=1, source_target_pairs={{0,8},{8,0},{16,24},{24,16},{32,40},{40,32},{48,56},{56,48},{64,72... | collective-permute-start | bytes 1572872 | tf_op jit(solution)/shard_map/ppermute | solution.py:657
  87.9 27.9 %collective-permute-start.10 = (f32[2,128,512]{2,1,0:T(8,128)S(1)}, f32[2,128,512]{2,1,0:T(8,128)S(1)}, u32[]{:S(2)}, u32[]{:S(2)}) collective-permute-start(f32[2,128,512]{2,1,0:T(8,128)S(1)} %get-tuple-element.68), channel_id=1, source_target_pairs={{8,16},{24,32},{40,48},{56,64},{72,80},{88,96},{104,112},{16,8},{3... | collective-permute-start | bytes 1572872 | tf_op jit(solution)/shard_map/ppermute | solution.py:663
  115.8 5.9 %copy-start.7 = (f32[4,256,256]{2,1,0:T(8,128)S(1)}, f32[4,256,256]{2,1,0:T(8,128)}, u32[]{:S(2)}) copy-start(f32[4,256,256]{2,1,0:T(8,128)} %get-tuple-element.73.own) | copy-start | bytes 3145732
  115.8 5.9 %collective-permute-start.11 = (f32[4,256,256]{2,1,0:T(8,128)}, f32[4,256,256]{2,1,0:T(8,128)S(1)}, u32[]{:S(2)}, u32[]{:S(2)}) collective-permute-start(f32[4,256,256]{2,1,0:T(8,128)} %get-tuple-element.73.own), channel_id=1, source_target_pairs={{0,1},{1,0},{2,3},{3,2},{4,5},{5,4},{6,7},{7,6},{8,9},{9,8},{10,11... | collective-permute-start | bytes 3145736 | tf_op jit(solution)/shard_map/ppermute | solution.py:657
